TPU v7x, 256 devices: a whole 4x4x8 slice. The times are simulated.
256 devices in a mesh: dp: 8 (over z), vocab: 32 (over x, y, core).
Axes of the slice: x: 4, y: 4, z: 8, core: 2. Of those that a mesh axis runs over, the one named last changes fastest.
Arguments:
- hidden_ref: bfloat16 [512, 8192], P(('dp', 'vocab'))
- head: bfloat16 [8192, 128256], P(None, ('dp', 'vocab'))
- targets: int32 [512], P(('dp', 'vocab')), may hold values from 0 to 128255
- train_loss: float32 [512], P('dp'), may hold values from 9 to 16
- keep_index: int32 [8, 48], P('dp'), may hold values from -1 to 63, as said below
- layer_input: bfloat16 [512, 8192], P('dp', 'vocab'), may hold values from -6 to 6
- cotangent: bfloat16 [512, 8192], P('dp', 'vocab'), may hold values from -0.59765625 to 0.59765625
- layer_weight: bfloat16 [8192, 8192], P('dp', 'vocab'), may hold values from -0.0625 to 0.0625
Outputs:
- excess: float32 [512], P('dp')
- grad_weight: float32 [8192, 8192], P('dp', 'vocab')
- grad_input: bfloat16 [512, 8192], P('dp', 'vocab')
Inputs may be any that keep to these rules, and one draw needn't show every extreme that they name: `keep_index`: each group's kept rows are distinct and ascending, all -1 entries stand after them; every group keeps 48 // 2 or more, and in every draw some group keeps all 48.
All inputs are finite; a program needn't handle non-finite values.
Results may differ from a plain program's by a relative error of at most 0.017.
Values may be sent and summed in bfloat16 or wider, within the bound.
No kernel may reach another device: no remote copies, remote signals or barrier semaphores. Data moves between devices by JAX's collectives and lax.ppermute only.
A program may use at most 128 MiB of HBM per device.

v0:
```python
import jax
import jax.numpy as jnp
from jax import lax
from jax.sharding import PartitionSpec as P


def derivative(values):
    sig = jax.nn.sigmoid(values)
    return sig * (1.0 + values * (1.0 - sig))


def layer_pass(rows_x, rows_dy, layer_weight):
    full_x = lax.all_gather(rows_x, "vocab", axis=1, tiled=True)
    full_w = lax.all_gather(layer_weight, "dp", axis=0, tiled=True)
    pre = jnp.dot(full_x, full_w, preferred_element_type=jnp.float32)
    slope = (rows_dy * derivative(pre)).astype(jnp.bfloat16)
    grad_weight = lax.psum_scatter(
        lax.dot_general(
            full_x, slope, (((0,), (0,)), ((), ())), preferred_element_type=jnp.float32
        ).astype(jnp.bfloat16),
        "dp",
        scatter_dimension=0,
        tiled=True,
    ).astype(jnp.float32)
    terms = lax.dot_general(
        slope, full_w, (((1,), (1,)), ((), ())), preferred_element_type=jnp.float32
    )
    summed = lax.psum_scatter(
        terms.astype(jnp.bfloat16), "vocab", scatter_dimension=1, tiled=True
    ).astype(jnp.float32)
    return (grad_weight, rows_dy + summed)


def on_device(
    hidden_ref, head, targets, train_loss, keep_index, layer_input, cotangent, layer_weight
):
    n_voc = lax.axis_size("vocab")
    voc_dev = head.shape[1]
    group_rows = train_loss.shape[0]
    shard = lax.axis_index("dp") * n_voc + lax.axis_index("vocab")
    vocab_ids = shard * voc_dev + jnp.arange(voc_dev, dtype=jnp.int32)
    states = lax.all_gather(hidden_ref, ("dp", "vocab"), axis=0, tiled=True)
    labels = lax.all_gather(targets, ("dp", "vocab"), axis=0, tiled=True)
    logits = jnp.dot(states, head, preferred_element_type=jnp.float32)
    top = jnp.max(logits, axis=1)
    total = jnp.sum(jnp.exp(logits - top[:, None]), axis=1)
    picked = jnp.sum(jnp.where(labels[:, None] == vocab_ids[None, :], logits, 0.0), axis=1)
    top, total, picked = (top, total, picked)
    highest = lax.pmax(top, ("dp", "vocab"))
    total, picked = lax.psum((total * jnp.exp(top - highest), picked), ("dp", "vocab"))
    top = highest
    ref_loss = top + jnp.log(total) - picked
    excess = train_loss - lax.dynamic_slice_in_dim(
        ref_loss, lax.axis_index("dp") * group_rows, group_rows
    )
    kept = keep_index[0]
    valid = kept >= 0
    chosen = jnp.where(valid, kept, 0)
    credit = jnp.where(valid, jax.nn.softplus(jnp.take(excess, chosen)), 0.0)
    credit_sum, kept_count = lax.psum((jnp.sum(credit), jnp.sum(valid.astype(jnp.float32))), "dp")
    weight = credit / (credit_sum / kept_count)
    inputs = jnp.where(
        valid[:, None], jnp.take(layer_input, chosen, axis=0), jnp.zeros((), layer_input.dtype)
    )
    dy = weight[:, None] * jnp.take(cotangent, chosen, axis=0).astype(jnp.float32)
    grad_weight, grad_rows = layer_pass(inputs, dy, layer_weight)
    grad_rows = grad_rows.astype(jnp.bfloat16)
    masked = jnp.where(valid[:, None], grad_rows.astype(jnp.float32), 0.0)
    grad_input = (
        jnp.zeros(layer_input.shape, jnp.float32).at[chosen].add(masked).astype(jnp.bfloat16)
    )
    return (excess, grad_weight, grad_input)


def solution(mesh):
    in_specs = (
        P(("dp", "vocab"), None),
        P(None, ("dp", "vocab")),
        P(("dp", "vocab")),
        P("dp"),
        P("dp", None),
        P("dp", "vocab"),
        P("dp", "vocab"),
        P("dp", "vocab"),
    )
    out_specs = (P("dp"), P("dp", "vocab"), P("dp", "vocab"))
    return jax.shard_map(
        on_device, mesh=mesh, in_specs=in_specs, out_specs=out_specs, check_vma=False
    )
```

profile of v0, /device:TPU:38, one launch (start us, length us, event | category | flops | bytes accessed | tf_op | source)
XLA Modules:
  0.0 500.4 jit_solution(4365097552262539721)
XLA Ops:
  7.2 0.7 all-gather.6.cloned.1.call-update
  8.0 0.7 all-gather.4.cloned.1.call-update
  8.7 0.9 dynamic-update-slice
  9.6 78.0 %all-reduce = s32[512]{0:T(512)S(1)} all-reduce(s32[512]{0:T(512)S(1)} %dynamic-update-slice), channel_id=1, replica_groups=mesh['dp'=8,'vocab'=32] {'dp','vocab'}, use_global_device_ids=true, to_apply=%add | all-reduce | flops 512 | bytes 4096
  87.6 0.7 fusion.11
  88.3 43.1 %all-gather.6.cloned.1.call-done = bf16[256,2,8192]{2,1,0:T(2,128)(2,1)} async-done(((bf16[1,2,8192]{2,1,0:T(2,128)(2,1)}), bf16[256,2,8192]{2,1,0:T(2,128)(2,1)}) %all-gather.6.cloned.1.call-update) | async-done | bytes 8388624 | tf_op jit(solution)/shard_map/all_gather | solution.py:42
  131.4 13.1 %reshape.113 = bf16[512,8192]{1,0:T(8,128)(2,1)} reshape(bf16[256,2,8192]{2,1,0:T(2,128)(2,1)} %all-gather.6.cloned.1.call-done) | data formatting | bytes 16777216
  144.5 9.6 %fusion.17 = (f32[512]{0:T(512)S(1)}, f32[512,501]{0,1:T(8,128)S(1)}) fusion(bf16[512,8192]{1,0:T(8,128)(2,1)} %reshape.113, bf16[8192,501]{0,1:T(8,128)(2,1)} %param.11), kind=kOutput, calls=%fused_computation.44 | convolution fusion | flops 4202948608 | bytes 17625088 | tf_op jit(solution)/shard_map/dot_general | solution.py:44
  154.1 76.4 %pmax.7 = f32[512]{0:T(512)S(1)} all-reduce(f32[512]{0:T(512)S(1)} %get-tuple-element.14), channel_id=1, replica_groups=mesh['dp'=8,'vocab'=32] {'dp','vocab'}, use_global_device_ids=true, to_apply=%region_1.0 | all-reduce | flops 512 | bytes 4096 | tf_op jit(solution)/shard_map/pmax | solution.py:49
  230.7 74.1 %all-reduce.1 = (f32[512]{0:T(512)S(1)}, f32[512]{0:T(512)S(1)}) all-reduce(f32[512]{0:T(512)S(1)} %get-tuple-element.5, f32[512]{0:T(512)S(1)} %exponential_multiply_fusion), channel_id=1, replica_groups=mesh['dp'=8,'vocab'=32] {'dp','vocab'}, use_global_device_ids=true, to_apply=%region_5.6 | all-reduce | flops 1024 | bytes 8192 | tf_op jit(solution)/shard_map/psum | solution.py:50
  304.9 0.8 gather_fusion
  305.7 0.6 fusion.15
  306.3 14.9 %all-reduce.2 = (f32[]{:T(128)}, f32[]{:T(128)}) all-reduce(f32[]{:T(128)} %get-tuple-element.10, f32[]{:T(128)} %get-tuple-element.13), channel_id=1, replica_groups=mesh['dp'=8,'vocab'=32] {'dp'}, use_global_device_ids=true, to_apply=%region_7.9 | all-reduce | flops 2 | bytes 16 | tf_op jit(solution)/shard_map/psum | solution.py:60
  321.2 0.7 gather_fusion.1
  321.9 0.7 gather_fusion.2
  324.0 23.3 %all_gather.14 = bf16[48,8192]{1,0:T(8,128)(2,1)S(1)} all-gather(bf16[48,256]{1,0:T(8,128)(2,1)S(1)} %select_select_fusion), channel_id=1, replica_groups=mesh['dp'=8,'vocab'=32] {'vocab'}, dimensions={1}, use_global_device_ids=true | all-gather | bytes 811008 | tf_op jit(solution)/shard_map/all_gather | solution.py:13
  347.3 3.0 fusion.18
  350.4 4.4 convolution_convert_fusion.1
  354.9 3.2 convolution_convert_fusion
  358.1 78.0 %reduce-scatter.5.cloned.1.call-done = bf16[48,256]{1,0:T(8,128)(2,1)} async-done(((bf16[48,8192]{1,0:T(8,128)(2,1)}), bf16[48,256]{1,0:T(8,128)(2,1)}) %reduce-scatter.5.cloned.1.call-update) | async-done | bytes 24592 | tf_op jit(solution)/shard_map/reduce_scatter | solution.py:28
  436.1 1.1 scatter_custom_fusion
  437.3 0.6 convert_element_type.39
  437.9 53.9 %reduce-scatter.3.cloned.1.call-done = bf16[1024,256]{1,0:T(8,128)(2,1)} async-done(((bf16[8192,256]{1,0:T(8,128)(2,1)}), bf16[1024,256]{1,0:T(8,128)(2,1)}) %reduce-scatter.3.cloned.1.call-update) | async-done | bytes 524304 | tf_op jit(solution)/shard_map/reduce_scatter | solution.py:17
  491.8 2.1 convert_element_type.34
  (28 shorter events, 0.7 us)
Async XLA Ops:
  7.2 314.0 %copy-start = (bf16[64,256]{1,0:T(8,128)(2,1)S(1)}, bf16[64,256]{1,0:T(8,128)(2,1)}, u32[]{:S(2)}) copy-start(bf16[64,256]{1,0:T(8,128)(2,1)} %param.15) | copy-start | bytes 98308
  7.2 124.2 %all-gather.6.cloned.1.call-start = ((), (), s32[]{:S(2)}) async-start(), calls=%async_computation.5 | async-start | bytes 8421376 | tf_op jit(solution)/shard_map/all_gather | solution.py:42
  7.9 339.4 %all-gather.4.cloned.1.call-start = ((), (), s32[]{:S(2)}) async-start(), calls=%async_computation.2 | async-start | bytes 4718592 | tf_op jit(solution)/shard_map/all_gather | solution.py:14
  8.7 427.5 %reduce-scatter.5.cloned.1.call-start = ((), (), s32[]{:S(2)}) async-start(), calls=%async_computation.4 | async-start | bytes 811008 | tf_op jit(solution)/shard_map/reduce_scatter | solution.py:28
  144.5 160.3 %copy-start.4 = (f32[64]{0:T(128)S(1)}, f32[64]{0:T(128)}, u32[]{:S(2)}) copy-start(f32[64]{0:T(128)} %param.13) | copy-start | bytes 772
  144.5 161.2 %copy-start.3 = (s32[1,48]{1,0:T(1,128)S(1)}, s32[1,48]{1,0:T(1,128)}, u32[]{:S(2)}) copy-start(s32[1,48]{1,0:T(1,128)} %param.14) | copy-start | bytes 580
  144.5 177.4 %copy-start.2 = (bf16[64,256]{1,0:T(8,128)(2,1)S(1)}, bf16[64,256]{1,0:T(8,128)(2,1)}, u32[]{:S(2)}) copy-start(bf16[64,256]{1,0:T(8,128)(2,1)} %param.16) | copy-start | bytes 98308
  304.9 53.2 %copy-start.1 = (f32[64]{0:T(128)}, f32[64]{0:T(128)S(1)}, u32[]{:S(2)}) copy-start(f32[64]{0:T(128)S(1)} %dynamic-slice_subtract_fusion) | copy-start | bytes 772
  354.8 137.0 %reduce-scatter.3.cloned.1.call-start = ((), (), s32[]{:S(2)}) async-start(), calls=%async_computation.3 | async-start | bytes 4718592 | tf_op jit(solution)/shard_map/reduce_scatter | solution.py:17
Sparse Core Ops, SparseCore 0:
  11.7 119.5 all-gather.5
  133.1 51.0 all-gather.3
  354.9 81.1 reduce-scatter.4
  438.5 53.2 reduce-scatter.2
where the time goes:
time: 504 us; the launch traced here: 500 us
  blocking collectives  267 us (53%)
  waiting for transfers between devices  176 us (35%)
  matrix products  20.3 us (4%)
  local copies, waits for them, and re-layouts  16.1 us (3%)
  between operations  15.2 us (3%)
  other arithmetic  5.61 us (1%)
    unnamed x1, blocking collectives  78 us
    reduce_scatter x1, waiting for transfers between devices, layer_pass(): lax.psum_scatter(terms.astype(jnp.bfloat16), 'vocab', scatter_dimension=1...  78 us
    pmax x1, blocking collectives, on_device(): highest = lax.pmax(top, ('dp', 'vocab'))  76.4 us
    psum x1, blocking collectives, on_device(): lax.psum((total * jnp.exp(top - highest), picked), ('dp', 'vocab'))  74.1 us
    reduce_scatter x1, waiting for transfers between devices, layer_pass(): lax.psum_scatter(lax.dot_general(full_x, slope, (((0,), (0,)), ((), ())),...  53.9 us
    all_gather x1, waiting for transfers between devices, on_device(): states = lax.all_gather(hidden_ref, ('dp', 'vocab'), axis=0, tiled=True)  43.1 us
    all_gather x1, blocking collectives, layer_pass(): full_x = lax.all_gather(rows_x, 'vocab', axis=1, tiled=True)  23.3 us
    psum x1, blocking collectives, on_device(): lax.psum((jnp.sum(credit), jnp.sum(valid.astype(jnp.float32))), 'dp')  14.9 us
  transfers between devices with their start and end apart: 4, of which 3 were waited for; matrix products, arithmetic and copies ran while one was open for 6% of the time, Pallas kernels for 0%

commit v1 on v0

v1 whole, which is shorter than its diff:
```python
import functools

import jax
import jax.numpy as jnp
from jax import lax
from jax.experimental import pallas as pl
from jax.experimental.pallas import tpu as pltpu
from jax.sharding import PartitionSpec as P

AXES = ("dp", "vocab")
NZ, NX, NY, NC = 8, 4, 4, 2
STRIDE = {"z": 32, "x": 8, "y": 2, "c": 1}
SIZE = {"z": NZ, "x": NX, "y": NY, "c": NC}
BF = jnp.bfloat16
F32 = jnp.float32


def coords():
    v = lax.axis_index("vocab")
    return {"z": lax.axis_index("dp"), "x": v // 8, "y": (v // 2) % 4, "c": v % 2}


def ex(a, axis, mask):
    m = STRIDE[axis] * mask
    return lax.ppermute(a, AXES, [(i, i ^ m) for i in range(256)])


def shift(a, axis, k):
    st, n = STRIDE[axis], SIZE[axis]
    pairs = []
    for i in range(256):
        p = (i // st) % n
        pairs.append((i, i + ((p + k) % n - p) * st))
    return lax.ppermute(a, AXES, pairs)


def bit(co, axis, b):
    return ((co[axis] >> b) & 1) == 1


def pair_up(mine, other, hi, dim):
    return jnp.where(hi, jnp.concatenate([other, mine], dim), jnp.concatenate([mine, other], dim))


def gather_direct(a, co, axis, dim):
    me = co[axis]
    blocks = [(0, a)] + [(k, ex(a, axis, k)) for k in (1, 3, 2)]
    buf = jnp.zeros(a.shape[:dim] + (4,) + a.shape[dim:], a.dtype)
    for k, block in blocks:
        buf = place(buf, block, dim, me ^ k)
    return buf


def place(buf, block, dim, pos, col=0):
    start = [jnp.int32(0)] * buf.ndim
    start[dim] = pos % 4
    start[-1] = jnp.int32(col)
    return lax.dynamic_update_slice(buf, jnp.expand_dims(block, dim), tuple(start))


def ring_first(a, axis):
    return shift(a, axis, 1), shift(a, axis, -1)


def ring_second(up, down, axis, cut):
    return shift(up[..., :cut], axis, 1), shift(down[..., cut:], axis, -1)


def ring_stack(a, near, far, co, axis, dim, cut):
    me = co[axis]
    buf = jnp.zeros(a.shape[:dim] + (4,) + a.shape[dim:], a.dtype)
    buf = place(buf, a, dim, me)
    buf = place(buf, near[0], dim, me + 3)
    buf = place(buf, near[1], dim, me + 1)
    buf = place(buf, far[0], dim, me + 2)
    return place(buf, far[1], dim, me + 2, cut)


def halve(a, co, axis, b, dim, dtype):
    hi = bit(co, axis, b)
    first = lax.index_in_dim(a, 0, dim, keepdims=False)
    second = lax.index_in_dim(a, 1, dim, keepdims=False)
    keep = jnp.where(hi, second, first)
    send = jnp.where(hi, first, second).astype(dtype)
    return keep.astype(F32) + ex(send, axis, 1 << b).astype(F32)


def derivative(values):
    sig = jax.nn.sigmoid(values)
    return sig * (1.0 + values * (1.0 - sig))


def plane_pairs(back):
    pairs = [((v // 4) * 32 + 4 * g + v % 4, g * 32 + v) for g in range(8) for v in range(32)]
    return [(j, i) for i, j in pairs] if back else pairs


def logits_kernel(first_ref, p_ref, q_ref, one_ref, two_ref, out_ref):
    half = p_ref.shape[1]
    dims = (((1,), (1,)), ((), ()))

    def logits(w_ref):
        return lax.dot_general(
            w_ref[:, :half], p_ref[...], dims, preferred_element_type=F32
        ) + lax.dot_general(
            w_ref[:, half:], q_ref[:, :half], dims, preferred_element_type=F32
        )

    meta = q_ref[:, half:].astype(F32).T
    label = (meta[0:1] * 65536.0 + meta[1:2] * 256.0 + meta[2:3]).astype(jnp.int32)
    one, two = logits(one_ref), logits(two_ref)
    top = jnp.maximum(jnp.max(one, axis=0, keepdims=True), jnp.max(two, axis=0, keepdims=True))
    total = jnp.sum(jnp.exp(one - top), axis=0, keepdims=True) + jnp.sum(
        jnp.exp(two - top), axis=0, keepdims=True
    )
    ids = lax.broadcasted_iota(jnp.int32, one.shape, 0)
    picked = jnp.sum(
        jnp.where(ids == label - first_ref[0], one, 0.0)
        + jnp.where(ids == label - first_ref[1], two, 0.0),
        axis=0,
        keepdims=True,
    )
    row = lax.broadcasted_iota(jnp.int32, out_ref.shape, 0)
    out = jnp.zeros(out_ref.shape, F32)
    for j, value in enumerate((top, total, picked)):
        out = jnp.where(row == j, value, out)
    out_ref[...] = out


def local_stats(p, q, head, other_head, first):
    voc, d = head.shape
    rows = p.shape[0]
    return pl.pallas_call(
        logits_kernel,
        out_shape=jax.ShapeDtypeStruct((8, rows), F32),
        in_specs=[pl.BlockSpec(memory_space=pltpu.SMEM)]
        + [pl.BlockSpec(memory_space=pltpu.VMEM)] * 4,
        out_specs=pl.BlockSpec(memory_space=pltpu.VMEM),
        compiler_params=pltpu.CompilerParams(vmem_limit_bytes=30 * 1024 * 1024),
        cost_estimate=pl.CostEstimate(
            flops=4 * rows * d * voc,
            bytes_accessed=4 * d * voc + 2 * rows * d,
            transcendentals=2 * rows * voc,
        ),
    )(first, p, q, head, other_head)


def split3(values):
    one = lax.reduce_precision(values, 8, 7)
    two = lax.reduce_precision(values - one, 8, 7)
    return jnp.concatenate([one, two, values - one - two]).astype(BF)


def swap_both(stats, payload, axis, mask):
    n = stats.shape[0]
    terms = split3(stats)
    terms = jnp.pad(terms, ((0, -terms.shape[0] % 16), (0, 0)))
    got = ex(jnp.concatenate([payload, terms]), axis, mask)
    m = payload.shape[0]
    t = got[m : m + 3 * n].astype(F32)
    return (t[:n] + t[n : 2 * n]) + t[2 * n :], got[:m]


def combine(a, b):
    n = a.shape[0] // 3
    top = jnp.maximum(a[:n], b[:n])
    total = a[n : 2 * n] * jnp.exp(a[:n] - top) + b[n : 2 * n] * jnp.exp(b[:n] - top)
    return jnp.concatenate([top, total, a[2 * n :] + b[2 * n :]])


def split_halves(a, hi):
    n = a.shape[0] // 2
    return jnp.where(hi, a[n:], a[:n]), jnp.where(hi, a[:n], a[n:]).astype(BF)


def sync(*values):
    return lax.optimization_barrier(values)


def columns(a, first, size):
    return lax.slice_in_dim(a, first, first + size, axis=a.ndim - 1)


def on_device(
    hidden_ref, head, targets, train_loss, keep_index, layer_input, cotangent, layer_weight
):
    co = coords()
    voc_dev = head.shape[1]
    half = head.shape[0] // 2
    dv = layer_weight.shape[1]
    rows = train_loss.shape[0]
    vocab = lax.axis_index("vocab")
    shard = lax.axis_index("dp") * 32 + vocab

    head = head.T
    other_head = ex(head, "c", 1)

    def bits(axis, b):
        return bit(co, axis, b)

    lane = lax.broadcasted_iota(jnp.int32, (2, 128), 1)
    t = targets[:, None]
    meta = jnp.where(lane == 0, t // 65536, jnp.where(lane == 1, (t // 256) % 256, t % 256))
    meta = jnp.where(lane < 3, meta, 0).astype(BF)
    h = jnp.concatenate([hidden_ref, meta], axis=1)[None]
    h = pair_up(h, ex(h, "z", 4), bits("z", 2), 0)[:, None]
    xs = lax.ppermute(layer_input, AXES, plane_pairs(False))[None, None]
    h, xs = sync(h, xs)

    h = pair_up(h, ex(h, "z", 2), bits("z", 1), 1)[:, :, None]
    xs = pair_up(xs, ex(xs, "x", 2), bits("x", 1), 0)
    h, xs = sync(h, xs)

    h = pair_up(h, ex(h, "z", 1), bits("z", 0), 2).reshape(16, 2 * half + 128)
    xs = pair_up(xs, ex(xs, "y", 2), bits("y", 1), 1)
    h, xs, other_head = sync(h, xs, other_head)

    p = gather_direct(h[:, :half], co, "y", 0)
    q = gather_direct(h[:, half:], co, "x", 0)
    xs = pair_up(xs, ex(xs, "y", 1), bits("y", 0), 3)[:, None]
    p, q, xs = sync(p, q, xs)

    p_near, q_near = ring_first(p, "x"), ring_first(q, "y")
    xs = pair_up(xs, ex(xs, "x", 1), bits("x", 0), 1).reshape(8 * rows, 2 * dv)
    got = ex(xs, "c", 1)
    low, high = [
        jnp.concatenate([columns(a, 0, dv), columns(b, 0, dv), columns(a, dv, dv), columns(b, dv, dv)], 1)
        for a, b in ((xs, got), (got, xs))
    ]
    x_all = jnp.where(bits("c", 0), high, low)
    pre = jnp.dot(x_all, layer_weight, preferred_element_type=F32)
    p_near, q_near, pre = sync(p_near, q_near, pre)

    p_far, q_far = ring_second(*p_near, "x", half // 2), ring_second(*q_near, "y", half // 2)
    pre = halve(pre.reshape(2, 2, 2, rows, dv), co, "z", 0, 2, BF)
    pre = halve(pre, co, "z", 1, 1, BF).astype(BF).reshape(2 * rows, dv)
    p_far, q_far, pre = sync(p_far, q_far, pre)

    p = ring_stack(p, p_near, p_far, co, "x", 0, half // 2).reshape(256, half)
    q = ring_stack(q, q_near, q_far, co, "y", 1, half // 2).reshape(256, half + 128)
    first = jnp.stack([shard * voc_dev, (shard ^ 1) * voc_dev]).astype(jnp.int32)
    stats = local_stats(p, q, head, other_head, first)[:3]

    here = jnp.arange(8, dtype=jnp.int32) == co["z"]
    marks = jnp.any(keep_index[0][None, :] == jnp.arange(rows, dtype=jnp.int32)[:, None], axis=1)
    own = jnp.stack([train_loss, marks.astype(F32)]).reshape(2, 16, 1, 2, 2)
    own = jnp.where(bits("c", 0), own[:, :, :, 1], own[:, :, :, 0])
    own = jnp.where(here[None, None, :, None], own, 0.0).reshape(2, 256)

    got = ex(jnp.concatenate([pre, cotangent]), "z", 4)
    pre = pre.astype(F32) + got[: 2 * rows].astype(F32)
    cot = pair_up(cotangent, got[2 * rows :], bits("z", 2), 0)
    u = (cot.astype(F32) * derivative(pre)).astype(BF)
    got_s = ex(jnp.concatenate([stats, own]), "z", 4)
    stats, own = combine(stats, got_s[:3]), own + got_s[3:]

    got_s, got = swap_both(jnp.concatenate([stats, own]), u, "z", 2)
    stats, own = combine(stats, got_s[:3]), own + got_s[3:]
    u = pair_up(u.reshape(2, 1, rows, dv), got.reshape(2, 1, rows, dv), bits("z", 1), 1)

    u = u.reshape(4 * rows, dv)
    got_s, got = swap_both(jnp.concatenate([stats, own]), u, "z", 1)
    stats, own = combine(stats, got_s[:3]), own + got_s[3:]
    u = pair_up(u.reshape(4, 1, rows, dv), got.reshape(4, 1, rows, dv), bits("z", 0), 1)
    u_all = u.reshape(8 * rows, dv)

    terms = lax.dot_general(
        u_all, layer_weight, (((1,), (1,)), ((), ())), preferred_element_type=F32
    ).astype(BF)
    back = jnp.concatenate([columns(terms, j * dv, dv) for j in (0, 2, 1, 3)])
    keep, send = split_halves(back, bits("c", 0))
    got_s, got = swap_both(jnp.concatenate([stats, own]), send, "c", 1)
    hi = bits("c", 0)
    both = [jnp.where(hi, jnp.stack([b, a], 1), jnp.stack([a, b], 1)) for a, b in ((stats, got_s[:3]), (own, got_s[3:]))]
    stats, own = both[0].reshape(6, 256), both[1].reshape(4, 256)

    back = (keep.astype(F32) + got.astype(F32)).astype(BF)
    for axis, mask in (("y", 1), ("x", 1), ("y", 2)):
        hi = bits(axis, mask // 2)
        if axis == "x":
            back = back.reshape(2, 2, 2 * rows, dv).swapaxes(0, 1).reshape(8 * rows, dv)
        elif mask == 2:
            back = back.reshape(2, 2, rows, dv).swapaxes(0, 1).reshape(4 * rows, dv)
        keep, send = split_halves(back, hi)
        got_s, got = swap_both(stats, send, axis, mask)
        stats = combine(stats, got_s)
        back = keep.astype(F32) + got.astype(F32)
        if mask == 1:
            back = back.astype(BF)

    keep, send = split_halves(back, bits("x", 1))
    got_s, got = swap_both(stats, send, "x", 2)
    stats = combine(stats, got_s)
    back = lax.ppermute(keep + got.astype(F32), AXES, plane_pairs(True))
    mine_grad = cotangent.astype(F32) + back

    loss, kept = own[:2], own[2:]
    excess = loss - (stats[:2] + jnp.log(stats[2:4]) - stats[4:])
    credit = jnp.where(kept > 0.0, jax.nn.softplus(excess), 0.0)
    weight = credit / (jnp.sum(credit) / jnp.sum(kept))
    both = jnp.stack([excess, weight]).reshape(2, 2, 16, 8, 2).transpose(0, 3, 2, 1, 4).reshape(2, 8, rows)
    excess, weight = both[0], both[1]
    slope = (weight.reshape(8 * rows)[:, None] * u_all.astype(F32)).astype(BF)
    grad_weight = lax.dot_general(
        x_all, slope, (((0,), (0,)), ((), ())), preferred_element_type=F32
    )
    own_weight = lax.dynamic_index_in_dim(weight, co["z"], 0, keepdims=False)
    own_excess = lax.dynamic_index_in_dim(excess, co["z"], 0, keepdims=False)
    grad_input = (own_weight[:, None] * mine_grad).astype(BF)
    return (own_excess, grad_weight, grad_input)


def solution(mesh):
    in_specs = (
        P(("dp", "vocab"), None),
        P(None, ("dp", "vocab")),
        P(("dp", "vocab")),
        P("dp"),
        P("dp", None),
        P("dp", "vocab"),
        P("dp", "vocab"),
        P("dp", "vocab"),
    )
    out_specs = (P("dp"), P("dp", "vocab"), P("dp", "vocab"))
    return jax.shard_map(
        on_device, mesh=mesh, in_specs=in_specs, out_specs=out_specs, check_vma=False
    )
```

time: 504 us -> 167 us (0.33)
  blocking collectives: 267 us -> 0 us
  waiting for transfers between devices: 176 us -> 78 us
  starting transfers between devices: 0.16 us -> 61.9 us
  matrix products: 20.3 us -> 2.46 us
  between operations: 15.2 us -> 3.09 us
  local copies, waits for them, and re-layouts: 16.1 us -> 5.24 us
  Pallas kernels: 0 us -> 8.09 us
    reduce_scatter x2 -> x0, waiting for transfers between devices: 132 us -> none  [the longest x1 78 us: layer_pass(): lax.psum_scatter(terms.astype(jnp.bfloat16), 'vocab', scatter_dimension=1...]
    psum x2 -> x0, blocking collectives: 89 us -> none  [the longest x1 74.1 us: on_device(): lax.psum((total * jnp.exp(top - highest), picked), ('dp', 'vocab'))]
    ppermute x0 -> x36, waiting for transfers between devices: none -> 78 us  [the longest x26 68.1 us: ex(): return lax.ppermute(a, AXES, [(i, i ^ m) for i in range(256)])]
    unnamed x1 -> x0, blocking collectives: 78 us -> none
    pmax x1 -> x0, blocking collectives: 76.4 us -> none  [on_device(): highest = lax.pmax(top, ('dp', 'vocab'))]
    ppermute x0 -> x36, starting transfers between devices: none -> 61.9 us  [the longest x26 37.8 us: ex(): return lax.ppermute(a, AXES, [(i, i ^ m) for i in range(256)])]
    all_gather x2 -> x0, waiting for transfers between devices: 43.1 us -> none  [the longest x1 43.1 us: on_device(): states = lax.all_gather(hidden_ref, ('dp', 'vocab'), axis=0, tiled=True)]
    all_gather x1 -> x0, blocking collectives: 23.3 us -> none  [layer_pass(): full_x = lax.all_gather(rows_x, 'vocab', axis=1, tiled=True)]
  transfers between devices with their start and end apart: 4 -> 36, of which waited for: 3 -> 23; matrix products, arithmetic and copies ran while one was open for 6% -> 7% of each run, Pallas kernels for 0% -> 0%
where the time goes in v1:
time: 167 us; the launch traced here: 166 us
  waiting for transfers between devices  78 us (47%)
  starting transfers between devices  61.9 us (37%)
  Pallas kernels  8.09 us (5%)
  other arithmetic  6.88 us (4%)
  local copies, waits for them, and re-layouts  5.24 us (3%)
  between operations  3.09 us (2%)
  matrix products  2.46 us (1%)
    ppermute x26, waiting for transfers between devices, ex(): return lax.ppermute(a, AXES, [(i, i ^ m) for i in range(256)])  68.1 us
    ppermute x26, starting transfers between devices, ex(): return lax.ppermute(a, AXES, [(i, i ^ m) for i in range(256)])  37.8 us
    ppermute x8, starting transfers between devices, shift(): return lax.ppermute(a, AXES, pairs)  10.8 us
    ppermute x1, starting transfers between devices, on_device(): back = lax.ppermute(keep + got.astype(F32), AXES, plane_pairs(True))  8.72 us
    pallas_call x1, Pallas kernels, local_stats(): pl.pallas_call(logits_kernel, out_shape=jax.ShapeDtypeStruct((8, rows), F...  8.09 us
    ppermute x1, waiting for transfers between devices, on_device(): xs = lax.ppermute(layer_input, AXES, plane_pairs(False))[None, None]  6.98 us
    ppermute x1, starting transfers between devices, on_device(): xs = lax.ppermute(layer_input, AXES, plane_pairs(False))[None, None]  4.54 us
  transfers between devices with their start and end apart: 36, of which 23 were waited for; matrix products, arithmetic and copies ran while one was open for 7% of the time, Pallas kernels for 0%

profile of v1, /device:TPU:38, one launch (start us, length us, event | category | flops | bytes accessed | tf_op | source)
XLA Modules:
  0.0 165.7 jit_solution(12958093990375329507)
XLA Ops:
  2.4 6.4 %collective-permute-start = (bf16[1,2,8320]{2,1,0:T(2,128)(2,1)S(1)}, bf16[1,2,8320]{2,1,0:T(2,128)(2,1)S(1)}, u32[]{:S(2)}, u32[]{:S(2)}) collective-permute-start(bf16[1,2,8320]{2,1,0:T(2,128)(2,1)S(1)} %get-tuple-element.70), channel_id=1, source_target_pairs={{0,128},{1,129},{2,130},{3,131},{4,132},{5,133},{6,134},{7,135},{8... | collective-permute-start | bytes 99848 | tf_op jit(solution)/shard_map/ppermute | solution.py:25
  8.8 4.5 %collective-permute-start.1 = (bf16[64,256]{1,0:T(8,128)(2,1)}, bf16[64,256]{1,0:T(8,128)(2,1)S(1)}, u32[]{:S(2)}, u32[]{:S(2)}) collective-permute-start(bf16[64,256]{1,0:T(8,128)(2,1)} %param.13), channel_id=1, source_target_pairs={{0,0},{1,1},{2,2},{3,3},{32,4},{33,5},{34,6},{35,7},{64,8},{65,9},... | collective-permute-start | bytes 98312 | tf_op jit(solution)/shard_map/ppermute | solution.py:207
  15.4 7.0 %collective-permute-done.1 = bf16[64,256]{1,0:T(8,128)(2,1)S(1)} collective-permute-done((bf16[64,256]{1,0:T(8,128)(2,1)}, bf16[64,256]{1,0:T(8,128)(2,1)S(1)}, u32[]{:S(2)}, u32[]{:S(2)}) %collective-permute-start.1) | collective-permute-done | bytes 32800 | tf_op jit(solution)/shard_map/ppermute | solution.py:207
  24.7 3.0 %collective-permute-done.3 = bf16[1,1,64,256]{3,2,1,0:T(8,128)(2,1)S(1)} collective-permute-done((bf16[1,1,64,256]{3,2,1,0:T(8,128)(2,1)S(1)}, bf16[1,1,64,256]{3,2,1,0:T(8,128)(2,1)S(1)}, u32[]{:S(2)}, u32[]{:S(2)}) %collective-permute-start.3) | collective-permute-done | bytes 32800 | tf_op jit(solution)/shard_map/ppermute | solution.py:25
  29.2 2.5 %collective-permute-start.4 = (bf16[2,2,1,2,8320]{4,3,0,2,1:T(2,128)(2,1)S(1)}, bf16[2,2,1,2,8320]{4,3,0,2,1:T(2,128)(2,1)S(1)}, u32[]{:S(2)}, u32[]{:S(2)}) collective-permute-start(bf16[2,2,1,2,8320]{4,3,0,2,1:T(2,128)(2,1)S(1)} %broadcast_select_fusion.2), channel_id=1, source_target_pairs={{0,32},{1,33},{2,34},{3,35},{4,36},{5,37},{6,38},{7,39},{8,40},{9,... | collective-permute-start | bytes 399368 | tf_op jit(solution)/shard_map/ppermute | solution.py:25
  35.4 2.8 %collective-permute-start.10 = (bf16[16,4224]{1,0:T(8,128)(2,1)S(1)}, bf16[16,4224]{1,0:T(8,128)(2,1)S(1)}, u32[]{:S(2)}, u32[]{:S(2)}) collective-permute-start(bf16[16,4224]{1,0:T(8,128)(2,1)S(1)} %slice.368), channel_id=1, source_target_pairs={{0,8},{1,9},{2,10},{3,11},{4,12},{5,13},{6,14},{7,15},{8,0},{9,1},... | collective-permute-start | bytes 405512 | tf_op jit(solution)/shard_map/ppermute | solution.py:25
  38.2 2.8 %collective-permute-start.11 = (bf16[16,4224]{1,0:T(8,128)(2,1)S(1)}, bf16[16,4224]{1,0:T(8,128)(2,1)S(1)}, u32[]{:S(2)}, u32[]{:S(2)}) collective-permute-start(bf16[16,4224]{1,0:T(8,128)(2,1)S(1)} %slice.368), channel_id=1, source_target_pairs={{0,24},{1,25},{2,26},{3,27},{4,28},{5,29},{6,30},{7,31},{8,16},{9,... | collective-permute-start | bytes 405512 | tf_op jit(solution)/shard_map/ppermute | solution.py:25
  44.4 4.4 %collective-permute-done.7 = bf16[16,4096]{1,0:T(8,128)(2,1)S(1)} collective-permute-done((bf16[16,4096]{1,0:T(8,128)(2,1)S(1)}, bf16[16,4096]{1,0:T(8,128)(2,1)S(1)}, u32[]{:S(2)}, u32[]{:S(2)}) %collective-permute-start.7) | collective-permute-done | bytes 131104 | tf_op jit(solution)/shard_map/ppermute | solution.py:25
  51.3 5.3 %collective-permute-done.9 = bf16[16,4096]{1,0:T(8,128)(2,1)S(1)} collective-permute-done((bf16[16,4096]{1,0:T(8,128)(2,1)S(1)}, bf16[16,4096]{1,0:T(8,128)(2,1)S(1)}, u32[]{:S(2)}, u32[]{:S(2)}) %collective-permute-start.9) | collective-permute-done | bytes 131104 | tf_op jit(solution)/shard_map/ppermute | solution.py:25
  59.2 2.6 %collective-permute-start.17 = (bf16[4,16,4224]{2,1,0:T(8,128)(2,1)S(1)}, bf16[4,16,4224]{2,1,0:T(8,128)(2,1)S(1)}, u32[]{:S(2)}, u32[]{:S(2)}) collective-permute-start(bf16[4,16,4224]{2,1,0:T(8,128)(2,1)S(1)} %bitcast_dynamic-update-slice_fusion.10), channel_id=1, source_target_pairs={{0,6},{1,7},{2,0},{3,1},{4,2},{5,3},{6,4},{7,5},{8,14},{9,15},{10,... | collective-permute-start | bytes 1622024 | tf_op jit(solution)/shard_map/ppermute | solution.py:34
  61.7 2.8 %collective-permute-start.14 = (bf16[4,16,4096]{2,1,0:T(8,128)(2,1)S(1)}, bf16[4,16,4096]{2,1,0:T(8,128)(2,1)S(1)}, u32[]{:S(2)}, u32[]{:S(2)}) collective-permute-start(bf16[4,16,4096]{2,1,0:T(8,128)(2,1)S(1)} %bitcast_dynamic-update-slice_fusion.14), channel_id=1, source_target_pairs={{0,8},{1,9},{2,10},{3,11},{4,12},{5,13},{6,14},{7,15},{8,16},{9,17... | collective-permute-start | bytes 1572872 | tf_op jit(solution)/shard_map/ppermute | solution.py:34
  64.7 9.3 %collective-permute-done.18 = bf16[2,1,2,64,512]{4,3,2,1,0:T(8,128)(2,1)S(1)} collective-permute-done((bf16[2,1,2,64,512]{4,3,2,1,0:T(8,128)(2,1)S(1)}, bf16[2,1,2,64,512]{4,3,2,1,0:T(8,128)(2,1)S(1)}, u32[]{:S(2)}, u32[]{:S(2)}) %collective-permute-start.18) | collective-permute-done | bytes 262176 | tf_op jit(solution)/shard_map/ppermute | solution.py:25
  84.6 3.4 %collective-permute-done.25 = bf16[2,64,256]{2,1,0:T(8,128)(2,1)S(1)} collective-permute-done((bf16[2,64,256]{2,1,0:T(8,128)(2,1)S(1)}, bf16[2,64,256]{2,1,0:T(8,128)(2,1)S(1)}, u32[]{:S(2)}, u32[]{:S(2)}) %collective-permute-start.25) | collective-permute-done | bytes 65568 | tf_op jit(solution)/shard_map/ppermute | solution.py:25
  88.0 2.9 %collective-permute-done.21 = bf16[4,16,2048]{2,1,0:T(8,128)(2,1)S(1)} collective-permute-done((bf16[4,16,2048]{2,1,0:T(8,128)(2,1)S(1)}, bf16[4,16,2048]{2,1,0:T(8,128)(2,1)S(1)}, u32[]{:S(2)}, u32[]{:S(2)}) %collective-permute-start.21) | collective-permute-done | bytes 262176 | tf_op jit(solution)/shard_map/ppermute | solution.py:34
  91.2 8.1 %shard_map.103 = f32[8,256]{1,0:T(8,128)S(1)} custom-call(s32[2]{0:T(128)S(1)} %get-tuple-element.108.first_ref, bf16[256,4096]{1,0:T(8,128)(2,1)S(1)} %bitcast.143, bf16[256,4224]{1,0:T(8,128)(2,1)S(1)} %bitcast.142, bf16[501,8192]{1,0:T(8,128)(2,1)S(1)} %bitcast.147, bf16[501,8192]{1,0:T(8,128)(2,1)} %collective-permute-done.6.two_ref), custom_call_target="tpu_custom_call" | custom-call | flops 4202692608 | bytes 20611072 | tf_op jit(solution)/shard_map/pallas_call | solution.py:133
  99.4 6.0 %collective-permute-start.26 = (bf16[192,256]{1,0:T(8,128)(2,1)S(1)}, bf16[192,256]{1,0:T(8,128)(2,1)S(1)}, u32[]{:S(2)}, u32[]{:S(2)}) collective-permute-start(bf16[192,256]{1,0:T(8,128)(2,1)S(1)} %pad_maximum_fusion.6), channel_id=1, source_target_pairs={{0,128},{1,129},{2,130},{3,131},{4,132},{5,133},{6,134},{7,135},{8... | collective-permute-start | bytes 294920 | tf_op jit(solution)/shard_map/ppermute | solution.py:25
  109.8 5.9 %collective-permute-done.28 = bf16[144,256]{1,0:T(8,128)(2,1)S(1)} collective-permute-done((bf16[144,256]{1,0:T(8,128)(2,1)S(1)}, bf16[144,256]{1,0:T(8,128)(2,1)S(1)}, u32[]{:S(2)}, u32[]{:S(2)}) %collective-permute-start.28) | collective-permute-done | bytes 73760 | tf_op jit(solution)/shard_map/ppermute | solution.py:25
  115.9 5.0 %collective-permute-done.29 = bf16[272,256]{1,0:T(8,128)(2,1)S(1)} collective-permute-done((bf16[272,256]{1,0:T(8,128)(2,1)S(1)}, bf16[272,256]{1,0:T(8,128)(2,1)S(1)}, u32[]{:S(2)}, u32[]{:S(2)}) %collective-permute-start.29) | collective-permute-done | bytes 139296 | tf_op jit(solution)/shard_map/ppermute | solution.py:25
  124.3 8.7 %collective-permute-done.31 = bf16[544,256]{1,0:T(8,128)(2,1)S(1)} collective-permute-done((bf16[544,256]{1,0:T(8,128)(2,1)S(1)}, bf16[544,256]{1,0:T(8,128)(2,1)S(1)}, u32[]{:S(2)}, u32[]{:S(2)}) %collective-permute-start.31) | collective-permute-done | bytes 278560 | tf_op jit(solution)/shard_map/ppermute | solution.py:25
  134.9 3.6 %collective-permute-done.32 = bf16[288,256]{1,0:T(8,128)(2,1)S(1)} collective-permute-done((bf16[288,256]{1,0:T(8,128)(2,1)S(1)}, bf16[288,256]{1,0:T(8,128)(2,1)S(1)}, u32[]{:S(2)}, u32[]{:S(2)}) %collective-permute-start.32) | collective-permute-done | bytes 147488 | tf_op jit(solution)/shard_map/ppermute | solution.py:25
  140.4 4.3 %collective-permute-done.33 = bf16[160,256]{1,0:T(8,128)(2,1)S(1)} collective-permute-done((bf16[160,256]{1,0:T(8,128)(2,1)S(1)}, bf16[160,256]{1,0:T(8,128)(2,1)S(1)}, u32[]{:S(2)}, u32[]{:S(2)}) %collective-permute-start.33) | collective-permute-done | bytes 81952 | tf_op jit(solution)/shard_map/ppermute | solution.py:25
  144.9 2.8 %collective-permute-start.34 = (bf16[96,256]{1,0:T(8,128)(2,1)S(1)}, bf16[96,256]{1,0:T(8,128)(2,1)S(1)}, u32[]{:S(2)}, u32[]{:S(2)}) collective-permute-start(bf16[96,256]{1,0:T(8,128)(2,1)S(1)} %pad_maximum_fusion.9), channel_id=1, source_target_pairs={{0,16},{1,17},{2,18},{3,19},{4,20},{5,21},{6,22},{7,23},{8,24},{9,... | collective-permute-start | bytes 147464 | tf_op jit(solution)/shard_map/ppermute | solution.py:25
  147.7 2.9 %collective-permute-done.34 = bf16[96,256]{1,0:T(8,128)(2,1)S(1)} collective-permute-done((bf16[96,256]{1,0:T(8,128)(2,1)S(1)}, bf16[96,256]{1,0:T(8,128)(2,1)S(1)}, u32[]{:S(2)}, u32[]{:S(2)}) %collective-permute-start.34) | collective-permute-done | bytes 49184 | tf_op jit(solution)/shard_map/ppermute | solution.py:25
  150.6 8.7 %collective-permute-start.35 = (f32[64,256]{1,0:T(8,128)S(1)}, f32[64,256]{1,0:T(8,128)S(1)}, u32[]{:S(2)}, u32[]{:S(2)}) collective-permute-start(f32[64,256]{1,0:T(8,128)S(1)} %convert_add_fusion.2), channel_id=1, source_target_pairs={{0,0},{1,1},{2,2},{3,3},{4,32},{5,33},{6,34},{7,35},{8,64},{9,65},... | collective-permute-start | bytes 196616 | tf_op jit(solution)/shard_map/ppermute | solution.py:294
  (216 shorter events, 46.9 us)
Async XLA Ops:
  0.6 34.7 %collective-permute-start.6 = (bf16[501,8192]{1,0:T(8,128)(2,1)}, bf16[501,8192]{1,0:T(8,128)(2,1)}, u32[]{:S(2)}, u32[]{:S(2)}) collective-permute-start(bf16[501,8192]{1,0:T(8,128)(2,1)} %bitcast.144), channel_id=1, source_target_pairs={{0,1},{1,0},{2,3},{3,2},{4,5},{5,4},{6,7},{7,6},{8,9},{9,8},{10,11... | collective-permute-start | bytes 24625160 | tf_op jit(solution)/shard_map/ppermute | solution.py:25
  2.4 12.8 %collective-permute-start = (bf16[1,2,8320]{2,1,0:T(2,128)(2,1)S(1)}, bf16[1,2,8320]{2,1,0:T(2,128)(2,1)S(1)}, u32[]{:S(2)}, u32[]{:S(2)}) collective-permute-start(bf16[1,2,8320]{2,1,0:T(2,128)(2,1)S(1)} %get-tuple-element.70), channel_id=1, source_target_pairs={{0,128},{1,129},{2,130},{3,131},{4,132},{5,133},{6,134},{7,135},{8... | collective-permute-start | bytes 99848 | tf_op jit(solution)/shard_map/ppermute | solution.py:25
  8.8 13.5 %collective-permute-start.1 = (bf16[64,256]{1,0:T(8,128)(2,1)}, bf16[64,256]{1,0:T(8,128)(2,1)S(1)}, u32[]{:S(2)}, u32[]{:S(2)}) collective-permute-start(bf16[64,256]{1,0:T(8,128)(2,1)} %param.13), channel_id=1, source_target_pairs={{0,0},{1,1},{2,2},{3,3},{32,4},{33,5},{34,6},{35,7},{64,8},{65,9},... | collective-permute-start | bytes 98312 | tf_op jit(solution)/shard_map/ppermute | solution.py:207
  35.4 22.9 %collective-permute-start.10 = (bf16[16,4224]{1,0:T(8,128)(2,1)S(1)}, bf16[16,4224]{1,0:T(8,128)(2,1)S(1)}, u32[]{:S(2)}, u32[]{:S(2)}) collective-permute-start(bf16[16,4224]{1,0:T(8,128)(2,1)S(1)} %slice.368), channel_id=1, source_target_pairs={{0,8},{1,9},{2,10},{3,11},{4,12},{5,13},{6,14},{7,15},{8,0},{9,1},... | collective-permute-start | bytes 405512 | tf_op jit(solution)/shard_map/ppermute | solution.py:25
  38.2 20.2 %collective-permute-start.11 = (bf16[16,4224]{1,0:T(8,128)(2,1)S(1)}, bf16[16,4224]{1,0:T(8,128)(2,1)S(1)}, u32[]{:S(2)}, u32[]{:S(2)}) collective-permute-start(bf16[16,4224]{1,0:T(8,128)(2,1)S(1)} %slice.368), channel_id=1, source_target_pairs={{0,24},{1,25},{2,26},{3,27},{4,28},{5,29},{6,30},{7,31},{8,16},{9,... | collective-permute-start | bytes 405512 | tf_op jit(solution)/shard_map/ppermute | solution.py:25
  41.0 17.4 %collective-permute-start.12 = (bf16[16,4224]{1,0:T(8,128)(2,1)S(1)}, bf16[16,4224]{1,0:T(8,128)(2,1)S(1)}, u32[]{:S(2)}, u32[]{:S(2)}) collective-permute-start(bf16[16,4224]{1,0:T(8,128)(2,1)S(1)} %slice.368), channel_id=1, source_target_pairs={{0,16},{1,17},{2,18},{3,19},{4,20},{5,21},{6,22},{7,23},{8,24},{9,... | collective-permute-start | bytes 405512 | tf_op jit(solution)/shard_map/ppermute | solution.py:25
  42.3 6.4 %collective-permute-start.7 = (bf16[16,4096]{1,0:T(8,128)(2,1)S(1)}, bf16[16,4096]{1,0:T(8,128)(2,1)S(1)}, u32[]{:S(2)}, u32[]{:S(2)}) collective-permute-start(bf16[16,4096]{1,0:T(8,128)(2,1)S(1)} %slice.367), channel_id=1, source_target_pairs={{0,2},{1,3},{2,0},{3,1},{4,6},{5,7},{6,4},{7,5},{8,10},{9,11},{10,... | collective-permute-start | bytes 393224 | tf_op jit(solution)/shard_map/ppermute | solution.py:25
  42.4 7.2 %collective-permute-start.8 = (bf16[16,4096]{1,0:T(8,128)(2,1)S(1)}, bf16[16,4096]{1,0:T(8,128)(2,1)S(1)}, u32[]{:S(2)}, u32[]{:S(2)}) collective-permute-start(bf16[16,4096]{1,0:T(8,128)(2,1)S(1)} %slice.367), channel_id=1, source_target_pairs={{0,6},{1,7},{2,4},{3,5},{4,2},{5,3},{6,0},{7,1},{8,14},{9,15},{10,... | collective-permute-start | bytes 393224 | tf_op jit(solution)/shard_map/ppermute | solution.py:25
  48.8 7.9 %collective-permute-start.9 = (bf16[16,4096]{1,0:T(8,128)(2,1)S(1)}, bf16[16,4096]{1,0:T(8,128)(2,1)S(1)}, u32[]{:S(2)}, u32[]{:S(2)}) collective-permute-start(bf16[16,4096]{1,0:T(8,128)(2,1)S(1)} %slice.367), channel_id=1, source_target_pairs={{0,4},{1,5},{2,6},{3,7},{4,0},{5,1},{6,2},{7,3},{8,12},{9,13},{10,... | collective-permute-start | bytes 393224 | tf_op jit(solution)/shard_map/ppermute | solution.py:25
  49.7 8.5 %collective-permute-start.13 = (bf16[2,2,64,256]{3,2,1,0:T(8,128)(2,1)S(1)}, bf16[2,2,64,256]{3,2,1,0:T(8,128)(2,1)S(1)}, u32[]{:S(2)}, u32[]{:S(2)}) collective-permute-start(bf16[2,2,64,256]{3,2,1,0:T(8,128)(2,1)S(1)} %maximum_select_fusion.4), channel_id=1, source_target_pairs={{0,2},{1,3},{2,0},{3,1},{4,6},{5,7},{6,4},{7,5},{8,10},{9,11},{10,... | collective-permute-start | bytes 393224 | tf_op jit(solution)/shard_map/ppermute | solution.py:25
  58.4 18.4 %collective-permute-start.16 = (bf16[4,16,4224]{2,1,0:T(8,128)(2,1)S(1)}, bf16[4,16,4224]{2,1,0:T(8,128)(2,1)S(1)}, u32[]{:S(2)}, u32[]{:S(2)}) collective-permute-start(bf16[4,16,4224]{2,1,0:T(8,128)(2,1)S(1)} %bitcast_dynamic-update-slice_fusion.10), channel_id=1, source_target_pairs={{0,2},{1,3},{2,4},{3,5},{4,6},{5,7},{6,0},{7,1},{8,10},{9,11},{10,... | collective-permute-start | bytes 1622024 | tf_op jit(solution)/shard_map/ppermute | solution.py:34
  59.2 17.7 %collective-permute-start.17 = (bf16[4,16,4224]{2,1,0:T(8,128)(2,1)S(1)}, bf16[4,16,4224]{2,1,0:T(8,128)(2,1)S(1)}, u32[]{:S(2)}, u32[]{:S(2)}) collective-permute-start(bf16[4,16,4224]{2,1,0:T(8,128)(2,1)S(1)} %bitcast_dynamic-update-slice_fusion.10), channel_id=1, source_target_pairs={{0,6},{1,7},{2,0},{3,1},{4,2},{5,3},{6,4},{7,5},{8,14},{9,15},{10,... | collective-permute-start | bytes 1622024 | tf_op jit(solution)/shard_map/ppermute | solution.py:34
  61.7 15.1 %collective-permute-start.14 = (bf16[4,16,4096]{2,1,0:T(8,128)(2,1)S(1)}, bf16[4,16,4096]{2,1,0:T(8,128)(2,1)S(1)}, u32[]{:S(2)}, u32[]{:S(2)}) collective-permute-start(bf16[4,16,4096]{2,1,0:T(8,128)(2,1)S(1)} %bitcast_dynamic-update-slice_fusion.14), channel_id=1, source_target_pairs={{0,8},{1,9},{2,10},{3,11},{4,12},{5,13},{6,14},{7,15},{8,16},{9,17... | collective-permute-start | bytes 1572872 | tf_op jit(solution)/shard_map/ppermute | solution.py:34
  64.5 12.4 %collective-permute-start.15 = (bf16[4,16,4096]{2,1,0:T(8,128)(2,1)S(1)}, bf16[4,16,4096]{2,1,0:T(8,128)(2,1)S(1)}, u32[]{:S(2)}, u32[]{:S(2)}) collective-permute-start(bf16[4,16,4096]{2,1,0:T(8,128)(2,1)S(1)} %bitcast_dynamic-update-slice_fusion.14), channel_id=1, source_target_pairs={{0,24},{1,25},{2,26},{3,27},{4,28},{5,29},{6,30},{7,31},{8,0},{9,1... | collective-permute-start | bytes 1572872 | tf_op jit(solution)/shard_map/ppermute | solution.py:34
  64.5 9.5 %collective-permute-start.18 = (bf16[2,1,2,64,512]{4,3,2,1,0:T(8,128)(2,1)S(1)}, bf16[2,1,2,64,512]{4,3,2,1,0:T(8,128)(2,1)S(1)}, u32[]{:S(2)}, u32[]{:S(2)}) collective-permute-start(bf16[2,1,2,64,512]{4,3,2,1,0:T(8,128)(2,1)S(1)} %maximum_select_fusion.2), channel_id=1, source_target_pairs={{0,8},{1,9},{2,10},{3,11},{4,12},{5,13},{6,14},{7,15},{8,0},{9,1},... | collective-permute-start | bytes 786440 | tf_op jit(solution)/shard_map/ppermute | solution.py:25
  77.5 13.5 %collective-permute-start.23 = (bf16[4,16,2176]{2,1,0:T(8,128)(2,1)S(1)}, bf16[4,16,2176]{2,1,0:T(8,128)(2,1)S(1)}, u32[]{:S(2)}, u32[]{:S(2)}) collective-permute-start(bf16[4,16,2176]{2,1,0:T(8,128)(2,1)S(1)} %slice.376), channel_id=1, source_target_pairs={{0,6},{1,7},{2,0},{3,1},{4,2},{5,3},{6,4},{7,5},{8,14},{9,15},{10,... | collective-permute-start | bytes 835592 | tf_op jit(solution)/shard_map/ppermute | solution.py:34
  79.6 8.4 %collective-permute-start.20 = (bf16[4,16,2048]{2,1,0:T(8,128)(2,1)S(1)}, bf16[4,16,2048]{2,1,0:T(8,128)(2,1)S(1)}, u32[]{:S(2)}, u32[]{:S(2)}) collective-permute-start(bf16[4,16,2048]{2,1,0:T(8,128)(2,1)S(1)} %slice.373), channel_id=1, source_target_pairs={{0,8},{1,9},{2,10},{3,11},{4,12},{5,13},{6,14},{7,15},{8,16},{9,17... | collective-permute-start | bytes 786440 | tf_op jit(solution)/shard_map/ppermute | solution.py:34
  82.1 8.8 %collective-permute-start.21 = (bf16[4,16,2048]{2,1,0:T(8,128)(2,1)S(1)}, bf16[4,16,2048]{2,1,0:T(8,128)(2,1)S(1)}, u32[]{:S(2)}, u32[]{:S(2)}) collective-permute-start(bf16[4,16,2048]{2,1,0:T(8,128)(2,1)S(1)} %slice.374), channel_id=1, source_target_pairs={{0,24},{1,25},{2,26},{3,27},{4,28},{5,29},{6,30},{7,31},{8,0},{9,1... | collective-permute-start | bytes 786440 | tf_op jit(solution)/shard_map/ppermute | solution.py:34
  82.2 8.8 %collective-permute-start.22 = (bf16[4,16,2048]{2,1,0:T(8,128)(2,1)S(1)}, bf16[4,16,2048]{2,1,0:T(8,128)(2,1)S(1)}, u32[]{:S(2)}, u32[]{:S(2)}) collective-permute-start(bf16[4,16,2048]{2,1,0:T(8,128)(2,1)S(1)} %slice.375), channel_id=1, source_target_pairs={{0,2},{1,3},{2,4},{3,5},{4,6},{5,7},{6,0},{7,1},{8,10},{9,11},{10,... | collective-permute-start | bytes 786440 | tf_op jit(solution)/shard_map/ppermute | solution.py:34
  99.3 7.6 %collective-permute-start.27 = (f32[5,256]{1,0:T(8,128)S(1)}, f32[5,256]{1,0:T(8,128)S(1)}, u32[]{:S(2)}, u32[]{:S(2)}) collective-permute-start(f32[5,256]{1,0:T(8,128)S(1)} %pad_maximum_fusion.11), channel_id=1, source_target_pairs={{0,128},{1,129},{2,130},{3,131},{4,132},{5,133},{6,134},{7,135},{8... | collective-permute-start | bytes 15368 | tf_op jit(solution)/shard_map/ppermute | solution.py:25
  99.4 9.9 %collective-permute-start.26 = (bf16[192,256]{1,0:T(8,128)(2,1)S(1)}, bf16[192,256]{1,0:T(8,128)(2,1)S(1)}, u32[]{:S(2)}, u32[]{:S(2)}) collective-permute-start(bf16[192,256]{1,0:T(8,128)(2,1)S(1)} %pad_maximum_fusion.6), channel_id=1, source_target_pairs={{0,128},{1,129},{2,130},{3,131},{4,132},{5,133},{6,134},{7,135},{8... | collective-permute-start | bytes 294920 | tf_op jit(solution)/shard_map/ppermute | solution.py:25
  109.4 6.3 %collective-permute-start.28 = (bf16[144,256]{1,0:T(8,128)(2,1)S(1)}, bf16[144,256]{1,0:T(8,128)(2,1)S(1)}, u32[]{:S(2)}, u32[]{:S(2)}) collective-permute-start(bf16[144,256]{1,0:T(8,128)(2,1)S(1)} %pad_maximum_fusion.8), channel_id=1, source_target_pairs={{0,64},{1,65},{2,66},{3,67},{4,68},{5,69},{6,70},{7,71},{8,72},{9,... | collective-permute-start | bytes 221192 | tf_op jit(solution)/shard_map/ppermute | solution.py:25
  124.2 8.8 %collective-permute-start.31 = (bf16[544,256]{1,0:T(8,128)(2,1)S(1)}, bf16[544,256]{1,0:T(8,128)(2,1)S(1)}, u32[]{:S(2)}, u32[]{:S(2)}) collective-permute-start(bf16[544,256]{1,0:T(8,128)(2,1)S(1)} %pad_maximum_fusion.3), channel_id=1, source_target_pairs={{0,2},{1,3},{2,0},{3,1},{4,6},{5,7},{6,4},{7,5},{8,10},{9,11},{10,... | collective-permute-start | bytes 835592 | tf_op jit(solution)/shard_map/ppermute | solution.py:25
  150.6 14.4 %collective-permute-start.35 = (f32[64,256]{1,0:T(8,128)S(1)}, f32[64,256]{1,0:T(8,128)S(1)}, u32[]{:S(2)}, u32[]{:S(2)}) collective-permute-start(f32[64,256]{1,0:T(8,128)S(1)} %convert_add_fusion.2), channel_id=1, source_target_pairs={{0,0},{1,1},{2,2},{3,3},{4,32},{5,33},{6,34},{7,35},{8,64},{9,65},... | collective-permute-start | bytes 196616 | tf_op jit(solution)/shard_map/ppermute | solution.py:294
  (16 other events, 167.1 us)

commit v2 on v1

--- a/solution.py
+++ b/solution.py
@@ -95,48 +95,72 @@
     return [(j, i) for i, j in pairs] if back else pairs
 
 
-def logits_kernel(first_ref, p_ref, q_ref, one_ref, two_ref, out_ref):
+def logits_kernel(first_ref, p_ref, q_ref, one_ref, two_ref, out_ref, buf, sems):
     half = p_ref.shape[1]
+    kb = buf.shape[2]
+    steps = buf.shape[0]
     dims = (((1,), (1,)), ((), ()))
-
-    def logits(w_ref):
-        return lax.dot_general(
-            w_ref[:, :half], p_ref[...], dims, preferred_element_type=F32
-        ) + lax.dot_general(
-            w_ref[:, half:], q_ref[:, :half], dims, preferred_element_type=F32
+    copies = [
+        pltpu.make_async_copy(two_ref.at[:, pl.ds(j * kb, kb)], buf.at[j], sems.at[j])
+        for j in range(steps)
+    ]
+    for copy in copies:
+        copy.start()
+
+    one = lax.dot_general(
+        p_ref[...], one_ref[:, :half], dims, preferred_element_type=F32
+    ) + lax.dot_general(q_ref[:, :half], one_ref[:, half:], dims, preferred_element_type=F32)
+    for copy in copies:
+        copy.wait()
+    n = steps // 2
+    two = jnp.zeros(one.shape, F32)
+    for j in range(steps):
+        a_ref = p_ref if j < n else q_ref
+        two += lax.dot_general(
+            a_ref[:, (j % n) * kb : (j % n + 1) * kb], buf[j], dims, preferred_element_type=F32
         )
 
-    meta = q_ref[:, half:].astype(F32).T
-    label = (meta[0:1] * 65536.0 + meta[1:2] * 256.0 + meta[2:3]).astype(jnp.int32)
-    one, two = logits(one_ref), logits(two_ref)
-    top = jnp.maximum(jnp.max(one, axis=0, keepdims=True), jnp.max(two, axis=0, keepdims=True))
-    total = jnp.sum(jnp.exp(one - top), axis=0, keepdims=True) + jnp.sum(
-        jnp.exp(two - top), axis=0, keepdims=True
-    )
-    ids = lax.broadcasted_iota(jnp.int32, one.shape, 0)
+    meta = q_ref[:, half:].astype(F32)
+    label = (meta[:, 0:1] * 65536.0 + meta[:, 1:2] * 256.0 + meta[:, 2:3]).astype(jnp.int32)
+    top = jnp.maximum(jnp.max(one, axis=1, keepdims=True), jnp.max(two, axis=1, keepdims=True))
+    total = jnp.sum(jnp.exp(one - top), axis=1, keepdims=True) + jnp.sum(
+        jnp.exp(two - top), axis=1, keepdims=True
+    )
+    ids = lax.broadcasted_iota(jnp.int32, one.shape, 1)
     picked = jnp.sum(
         jnp.where(ids == label - first_ref[0], one, 0.0)
         + jnp.where(ids == label - first_ref[1], two, 0.0),
-        axis=0,
+        axis=1,
         keepdims=True,
     )
-    row = lax.broadcasted_iota(jnp.int32, out_ref.shape, 0)
-    out = jnp.zeros(out_ref.shape, F32)
+    lane = lax.broadcasted_iota(jnp.int32, (one.shape[0], 128), 1)
+    cols = jnp.zeros(lane.shape, F32)
     for j, value in enumerate((top, total, picked)):
-        out = jnp.where(row == j, value, out)
-    out_ref[...] = out
+        cols = jnp.where(lane == j, value, cols)
+    out_ref[...] = cols.T[:8]
 
 
 def local_stats(p, q, head, other_head, first):
     voc, d = head.shape
     rows = p.shape[0]
+    steps = 2
+    vmem = pl.BlockSpec(memory_space=pltpu.VMEM)
     return pl.pallas_call(
         logits_kernel,
         out_shape=jax.ShapeDtypeStruct((8, rows), F32),
-        in_specs=[pl.BlockSpec(memory_space=pltpu.SMEM)]
-        + [pl.BlockSpec(memory_space=pltpu.VMEM)] * 4,
-        out_specs=pl.BlockSpec(memory_space=pltpu.VMEM),
-        compiler_params=pltpu.CompilerParams(vmem_limit_bytes=30 * 1024 * 1024),
+        in_specs=[
+            pl.BlockSpec(memory_space=pltpu.SMEM),
+            vmem,
+            vmem,
+            vmem,
+            pl.BlockSpec(memory_space=pl.ANY),
+        ],
+        out_specs=vmem,
+        scratch_shapes=[
+            pltpu.VMEM((steps, voc, d // steps), BF),
+            pltpu.SemaphoreType.DMA((steps,)),
+        ],
+        compiler_params=pltpu.CompilerParams(vmem_limit_bytes=20 * 1024 * 1024),
         cost_estimate=pl.CostEstimate(
             flops=4 * rows * d * voc,
             bytes_accessed=4 * d * voc + 2 * rows * d,
@@ -151,14 +175,27 @@
     return jnp.concatenate([one, two, values - one - two]).astype(BF)
 
 
-def swap_both(stats, payload, axis, mask):
-    n = stats.shape[0]
+def with_terms(stats, payload):
     terms = split3(stats)
     terms = jnp.pad(terms, ((0, -terms.shape[0] % 16), (0, 0)))
-    got = ex(jnp.concatenate([payload, terms]), axis, mask)
-    m = payload.shape[0]
-    t = got[m : m + 3 * n].astype(F32)
-    return (t[:n] + t[n : 2 * n]) + t[2 * n :], got[:m]
+    return jnp.concatenate([payload, terms])
+
+
+def without_terms(message, n):
+    m = message.shape[0] - 3 * n - (-3 * n) % 16
+    t = message[m : m + 3 * n].astype(F32)
+    return (t[:n] + t[n : 2 * n]) + t[2 * n :], message[:m]
+
+
+def four_way(stats, parts, co, axis):
+    me = co[axis]
+    n = stats.shape[0]
+    total, own = lax.dynamic_index_in_dim(parts, me, 0, keepdims=False).astype(F32), stats
+    for mask in (1, 3, 2):
+        part = lax.dynamic_index_in_dim(parts, me ^ mask, 0, keepdims=False)
+        got_s, got = without_terms(ex(with_terms(own, part), axis, mask), n)
+        total, stats = total + got.astype(F32), combine(stats, got_s)
+    return stats, total
 
 
 def combine(a, b):
@@ -204,42 +241,45 @@
     meta = jnp.where(lane < 3, meta, 0).astype(BF)
     h = jnp.concatenate([hidden_ref, meta], axis=1)[None]
     h = pair_up(h, ex(h, "z", 4), bits("z", 2), 0)[:, None]
-    xs = lax.ppermute(layer_input, AXES, plane_pairs(False))[None, None]
+    xs = lax.ppermute(layer_input, AXES, plane_pairs(False))
     h, xs = sync(h, xs)
 
     h = pair_up(h, ex(h, "z", 2), bits("z", 1), 1)[:, :, None]
-    xs = pair_up(xs, ex(xs, "x", 2), bits("x", 1), 0)
+    xs = gather_direct(xs, co, "x", 0)
     h, xs = sync(h, xs)
 
     h = pair_up(h, ex(h, "z", 1), bits("z", 0), 2).reshape(16, 2 * half + 128)
-    xs = pair_up(xs, ex(xs, "y", 2), bits("y", 1), 1)
-    h, xs, other_head = sync(h, xs, other_head)
+    xs = gather_direct(xs, co, "y", 0).reshape(2, 2, 4, rows, dv)
+    xs = jnp.concatenate([xs[:, j].swapaxes(0, 1).reshape(8 * rows, dv) for j in (0, 1)], 1)
+    got = ex(xs, "c", 1)
+    h, xs, got, other_head = sync(h, xs, got, other_head)
 
     p = gather_direct(h[:, :half], co, "y", 0)
     q = gather_direct(h[:, half:], co, "x", 0)
-    xs = pair_up(xs, ex(xs, "y", 1), bits("y", 0), 3)[:, None]
-    p, q, xs = sync(p, q, xs)
-
-    p_near, q_near = ring_first(p, "x"), ring_first(q, "y")
-    xs = pair_up(xs, ex(xs, "x", 1), bits("x", 0), 1).reshape(8 * rows, 2 * dv)
-    got = ex(xs, "c", 1)
     low, high = [
         jnp.concatenate([columns(a, 0, dv), columns(b, 0, dv), columns(a, dv, dv), columns(b, dv, dv)], 1)
         for a, b in ((xs, got), (got, xs))
     ]
     x_all = jnp.where(bits("c", 0), high, low)
     pre = jnp.dot(x_all, layer_weight, preferred_element_type=F32)
-    p_near, q_near, pre = sync(p_near, q_near, pre)
-
-    p_far, q_far = ring_second(*p_near, "x", half // 2), ring_second(*q_near, "y", half // 2)
+    p, q, pre = sync(p, q, pre)
+
+    p_near, q_near = ring_first(p, "x"), ring_first(q, "y")
     pre = halve(pre.reshape(2, 2, 2, rows, dv), co, "z", 0, 2, BF)
     pre = halve(pre, co, "z", 1, 1, BF).astype(BF).reshape(2 * rows, dv)
-    p_far, q_far, pre = sync(p_far, q_far, pre)
+    p_near, q_near, pre = sync(p_near, q_near, pre)
+
+    p_far, q_far = ring_second(*p_near, "x", half // 2), ring_second(*q_near, "y", half // 2)
+    got = ex(jnp.concatenate([pre, cotangent]), "z", 4)
+    pre = pre.astype(F32) + got[: 2 * rows].astype(F32)
+    cot = pair_up(cotangent, got[2 * rows :], bits("z", 2), 0)
+    u = (cot.astype(F32) * derivative(pre)).astype(BF)
+    p_far, q_far, u = sync(p_far, q_far, u)
 
     p = ring_stack(p, p_near, p_far, co, "x", 0, half // 2).reshape(256, half)
     q = ring_stack(q, q_near, q_far, co, "y", 1, half // 2).reshape(256, half + 128)
     first = jnp.stack([shard * voc_dev, (shard ^ 1) * voc_dev]).astype(jnp.int32)
-    stats = local_stats(p, q, head, other_head, first)[:3]
+    stats, u = sync(local_stats(p, q, head, other_head, first)[:3], u)
 
     here = jnp.arange(8, dtype=jnp.int32) == co["z"]
     marks = jnp.any(keep_index[0][None, :] == jnp.arange(rows, dtype=jnp.int32)[:, None], axis=1)
@@ -247,51 +287,37 @@
     own = jnp.where(bits("c", 0), own[:, :, :, 1], own[:, :, :, 0])
     own = jnp.where(here[None, None, :, None], own, 0.0).reshape(2, 256)
 
-    got = ex(jnp.concatenate([pre, cotangent]), "z", 4)
-    pre = pre.astype(F32) + got[: 2 * rows].astype(F32)
-    cot = pair_up(cotangent, got[2 * rows :], bits("z", 2), 0)
-    u = (cot.astype(F32) * derivative(pre)).astype(BF)
     got_s = ex(jnp.concatenate([stats, own]), "z", 4)
+    u = u.reshape(2, 1, rows, dv)
+    full = jnp.zeros((2, 4, rows, dv), BF)
+    low_z = co["z"] % 4
+    for mask in (0, 1, 3, 2):
+        block = ex(u, "z", mask) if mask else u
+        full = lax.dynamic_update_slice_in_dim(full, block, low_z ^ mask, 1)
     stats, own = combine(stats, got_s[:3]), own + got_s[3:]
-
-    got_s, got = swap_both(jnp.concatenate([stats, own]), u, "z", 2)
-    stats, own = combine(stats, got_s[:3]), own + got_s[3:]
-    u = pair_up(u.reshape(2, 1, rows, dv), got.reshape(2, 1, rows, dv), bits("z", 1), 1)
-
-    u = u.reshape(4 * rows, dv)
-    got_s, got = swap_both(jnp.concatenate([stats, own]), u, "z", 1)
-    stats, own = combine(stats, got_s[:3]), own + got_s[3:]
-    u = pair_up(u.reshape(4, 1, rows, dv), got.reshape(4, 1, rows, dv), bits("z", 0), 1)
-    u_all = u.reshape(8 * rows, dv)
+    u_all = full.reshape(8 * rows, dv)
+    stats, own, u_all = sync(stats, own, u_all)
 
     terms = lax.dot_general(
         u_all, layer_weight, (((1,), (1,)), ((), ())), preferred_element_type=F32
     ).astype(BF)
     back = jnp.concatenate([columns(terms, j * dv, dv) for j in (0, 2, 1, 3)])
-    keep, send = split_halves(back, bits("c", 0))
-    got_s, got = swap_both(jnp.concatenate([stats, own]), send, "c", 1)
     hi = bits("c", 0)
-    both = [jnp.where(hi, jnp.stack([b, a], 1), jnp.stack([a, b], 1)) for a, b in ((stats, got_s[:3]), (own, got_s[3:]))]
-    stats, own = both[0].reshape(6, 256), both[1].reshape(4, 256)
-
+    keep, send = split_halves(back, hi)
+    got_s, got = without_terms(ex(with_terms(jnp.concatenate([stats, own]), send), "c", 1), 5)
+    stats, own = [
+        jnp.where(hi, jnp.stack([b, a], 1), jnp.stack([a, b], 1)).reshape(-1, 256)
+        for a, b in ((stats, got_s[:3]), (own, got_s[3:]))
+    ]
     back = (keep.astype(F32) + got.astype(F32)).astype(BF)
-    for axis, mask in (("y", 1), ("x", 1), ("y", 2)):
-        hi = bits(axis, mask // 2)
-        if axis == "x":
-            back = back.reshape(2, 2, 2 * rows, dv).swapaxes(0, 1).reshape(8 * rows, dv)
-        elif mask == 2:
-            back = back.reshape(2, 2, rows, dv).swapaxes(0, 1).reshape(4 * rows, dv)
-        keep, send = split_halves(back, hi)
-        got_s, got = swap_both(stats, send, axis, mask)
-        stats = combine(stats, got_s)
-        back = keep.astype(F32) + got.astype(F32)
-        if mask == 1:
-            back = back.astype(BF)
-
-    keep, send = split_halves(back, bits("x", 1))
-    got_s, got = swap_both(stats, send, "x", 2)
-    stats = combine(stats, got_s)
-    back = lax.ppermute(keep + got.astype(F32), AXES, plane_pairs(True))
+    back = back.reshape(2, 4, 2, rows, dv).transpose(2, 0, 1, 3, 4).reshape(4, 4 * rows, dv)
+    stats, back = four_way(stats, back, co, "y")
+    stats, back = four_way(stats, back.astype(BF).reshape(4, rows, dv), co, "x")
+    back = lax.ppermute(back, AXES, plane_pairs(True))
+    mine = jnp.concatenate([stats, own])
+    for mask in (1, 3, 2):
+        got_s = ex(mine, "z", mask)
+        stats, own = combine(stats, got_s[:6]), own + got_s[6:]
     mine_grad = cotangent.astype(F32) + back
 
     loss, kept = own[:2], own[2:]

time: 167 us -> 151 us (0.904)
  waiting for transfers between devices: 78 us -> 51.6 us
  starting transfers between devices: 61.9 us -> 74.2 us
    ppermute x26 -> x34, waiting for transfers between devices: 68.1 us -> 41 us  [ex(): return lax.ppermute(a, AXES, [(i, i ^ m) for i in range(256)])]
    ppermute x26 -> x34, starting transfers between devices: 37.8 us -> 52.5 us  [ex(): return lax.ppermute(a, AXES, [(i, i ^ m) for i in range(256)])]
    ppermute x2, starting transfers between devices: 13.3 us -> 11.2 us  [the longest x1 6.64 us: on_device(): back = lax.ppermute(back, AXES, plane_pairs(True))]
  transfers between devices with their start and end apart: 36 -> 44, of which waited for: 23 -> 22; matrix products, arithmetic and copies ran while one was open for 7% -> 8% of each run, Pallas kernels for 0% -> 0%
where the time goes in v2:
time: 151 us
  starting transfers between devices  74.2 us (49%)
  waiting for transfers between devices  51.6 us (34%)
  Pallas kernels  6.81 us (5%)
  other arithmetic  6.59 us (4%)
  local copies, waits for them, and re-layouts  5.57 us (4%)
  between operations  3.36 us (2%)
  matrix products  2.46 us (2%)
    ppermute x34, starting transfers between devices, ex(): return lax.ppermute(a, AXES, [(i, i ^ m) for i in range(256)])  52.5 us
    ppermute x34, waiting for transfers between devices, ex(): return lax.ppermute(a, AXES, [(i, i ^ m) for i in range(256)])  41 us
    ppermute x8, starting transfers between devices, shift(): return lax.ppermute(a, AXES, pairs)  10.5 us
    pallas_call x1, Pallas kernels, local_stats(): pl.pallas_call(logits_kernel, out_shape=jax.ShapeDtypeStruct((8, rows), F...  6.81 us
    ppermute x1, starting transfers between devices, on_device(): back = lax.ppermute(back, AXES, plane_pairs(True))  6.64 us
    ppermute x1, waiting for transfers between devices, on_device(): xs = lax.ppermute(layer_input, AXES, plane_pairs(False))  6.1 us
    ppermute x1, starting transfers between devices, on_device(): xs = lax.ppermute(layer_input, AXES, plane_pairs(False))  4.54 us
    ppermute x8, waiting for transfers between devices, shift(): return lax.ppermute(a, AXES, pairs)  3.2 us
  transfers between devices with their start and end apart: 44, of which 22 were waited for; matrix products, arithmetic and copies ran while one was open for 8% of the time, Pallas kernels for 0%

profile of v2, /device:TPU:38, one launch (start us, length us, event | category | flops | bytes accessed | tf_op | source)
XLA Modules:
  0.0 150.6 jit_solution(17063594783287539179)
XLA Ops:
  2.4 6.4 %collective-permute-start = (bf16[1,2,8320]{2,1,0:T(2,128)(2,1)S(1)}, bf16[1,2,8320]{2,1,0:T(2,128)(2,1)S(1)}, u32[]{:S(2)}, u32[]{:S(2)}) collective-permute-start(bf16[1,2,8320]{2,1,0:T(2,128)(2,1)S(1)} %get-tuple-element.80), channel_id=1, source_target_pairs={{0,128},{1,129},{2,130},{3,131},{4,132},{5,133},{6,134},{7,135},{8... | collective-permute-start | bytes 99848 | tf_op jit(solution)/shard_map/ppermute | solution.py:25
  8.8 4.5 %collective-permute-start.1 = (bf16[64,256]{1,0:T(8,128)(2,1)}, bf16[64,256]{1,0:T(8,128)(2,1)S(1)}, u32[]{:S(2)}, u32[]{:S(2)}) collective-permute-start(bf16[64,256]{1,0:T(8,128)(2,1)} %param.13), channel_id=1, source_target_pairs={{0,0},{1,1},{2,2},{3,3},{32,4},{33,5},{34,6},{35,7},{64,8},{65,9},... | collective-permute-start | bytes 98312 | tf_op jit(solution)/shard_map/ppermute | solution.py:244
  16.2 6.1 %collective-permute-done.1 = bf16[64,256]{1,0:T(8,128)(2,1)S(1)} collective-permute-done((bf16[64,256]{1,0:T(8,128)(2,1)}, bf16[64,256]{1,0:T(8,128)(2,1)S(1)}, u32[]{:S(2)}, u32[]{:S(2)}) %collective-permute-start.1) | collective-permute-done | bytes 32800 | tf_op jit(solution)/shard_map/ppermute | solution.py:244
  23.5 3.0 %collective-permute-start.5 = (bf16[64,256]{1,0:T(8,128)(2,1)S(1)}, bf16[64,256]{1,0:T(8,128)(2,1)S(1)}, u32[]{:S(2)}, u32[]{:S(2)}) collective-permute-start(bf16[64,256]{1,0:T(8,128)(2,1)S(1)} %collective-permute-done.1), channel_id=1, source_target_pairs={{0,16},{1,17},{2,18},{3,19},{4,20},{5,21},{6,22},{7,23},{8,24},{9,... | collective-permute-start | bytes 98312 | tf_op jit(solution)/shard_map/ppermute | solution.py:25
  28.9 2.7 %collective-permute-done.2 = bf16[2,1,2,8320]{3,2,0,1:T(2,128)(2,1)S(1)} collective-permute-done((bf16[2,1,2,8320]{3,2,0,1:T(2,128)(2,1)S(1)}, bf16[2,1,2,8320]{3,2,0,1:T(2,128)(2,1)S(1)}, u32[]{:S(2)}, u32[]{:S(2)}) %collective-permute-start.2) | collective-permute-done | bytes 66592 | tf_op jit(solution)/shard_map/ppermute | solution.py:25
  33.5 2.5 %collective-permute-start.9 = (bf16[4,64,256]{2,1,0:T(8,128)(2,1)S(1)}, bf16[4,64,256]{2,1,0:T(8,128)(2,1)S(1)}, u32[]{:S(2)}, u32[]{:S(2)}) collective-permute-start(bf16[4,64,256]{2,1,0:T(8,128)(2,1)S(1)} %bitcast_dynamic-update-slice_fusion.22), channel_id=1, source_target_pairs={{0,4},{1,5},{2,6},{3,7},{4,0},{5,1},{6,2},{7,3},{8,12},{9,13},{10,... | collective-permute-start | bytes 393224 | tf_op jit(solution)/shard_map/ppermute | solution.py:25
  37.7 3.3 %collective-permute-done.8 = bf16[4,64,256]{2,1,0:T(8,128)(2,1)S(1)} collective-permute-done((bf16[4,64,256]{2,1,0:T(8,128)(2,1)S(1)}, bf16[4,64,256]{2,1,0:T(8,128)(2,1)S(1)}, u32[]{:S(2)}, u32[]{:S(2)}) %collective-permute-start.8) | collective-permute-done | bytes 131104 | tf_op jit(solution)/shard_map/ppermute | solution.py:25
  44.9 2.6 %collective-permute-start.17 = (bf16[16,4224]{1,0:T(8,128)(2,1)S(1)}, bf16[16,4224]{1,0:T(8,128)(2,1)S(1)}, u32[]{:S(2)}, u32[]{:S(2)}) collective-permute-start(bf16[16,4224]{1,0:T(8,128)(2,1)S(1)} %slice.370), channel_id=1, source_target_pairs={{0,16},{1,17},{2,18},{3,19},{4,20},{5,21},{6,22},{7,23},{8,24},{9,... | collective-permute-start | bytes 405512 | tf_op jit(solution)/shard_map/ppermute | solution.py:25
  54.1 4.9 %collective-permute-done.14 = bf16[16,4096]{1,0:T(8,128)(2,1)S(1)} collective-permute-done((bf16[16,4096]{1,0:T(8,128)(2,1)S(1)}, bf16[16,4096]{1,0:T(8,128)(2,1)S(1)}, u32[]{:S(2)}, u32[]{:S(2)}) %collective-permute-start.14) | collective-permute-done | bytes 131104 | tf_op jit(solution)/shard_map/ppermute | solution.py:25
  59.2 3.2 %collective-permute-start.21 = (bf16[4,16,4224]{2,1,0:T(8,128)(2,1)S(1)}, bf16[4,16,4224]{2,1,0:T(8,128)(2,1)S(1)}, u32[]{:S(2)}, u32[]{:S(2)}) collective-permute-start(bf16[4,16,4224]{2,1,0:T(8,128)(2,1)S(1)} %bitcast_dynamic-update-slice_fusion.10), channel_id=1, source_target_pairs={{0,6},{1,7},{2,0},{3,1},{4,2},{5,3},{6,4},{7,5},{8,14},{9,15},{10,... | collective-permute-start | bytes 1622024 | tf_op jit(solution)/shard_map/ppermute | solution.py:34
  66.0 3.6 %collective-permute-done.22 = bf16[2,2,64,256]{3,2,1,0:T(8,128)(2,1)S(1)} collective-permute-done((bf16[2,2,64,256]{3,2,1,0:T(8,128)(2,1)S(1)}, bf16[2,2,64,256]{3,2,1,0:T(8,128)(2,1)S(1)}, u32[]{:S(2)}, u32[]{:S(2)}) %collective-permute-start.22) | collective-permute-done | bytes 131104 | tf_op jit(solution)/shard_map/ppermute | solution.py:25
  69.7 2.9 %collective-permute-start.23 = (bf16[2,64,256]{2,1,0:T(8,128)(2,1)S(1)}, bf16[2,64,256]{2,1,0:T(8,128)(2,1)S(1)}, u32[]{:S(2)}, u32[]{:S(2)}) collective-permute-start(bf16[2,64,256]{2,1,0:T(8,128)(2,1)S(1)} %fusion.11), channel_id=1, source_target_pairs={{0,64},{1,65},{2,66},{3,67},{4,68},{5,69},{6,70},{7,71},{8,72},{9,... | collective-permute-start | bytes 196616 | tf_op jit(solution)/shard_map/ppermute | solution.py:25
  72.9 2.8 %collective-permute-done.23 = bf16[2,64,256]{2,1,0:T(8,128)(2,1)S(1)} collective-permute-done((bf16[2,64,256]{2,1,0:T(8,128)(2,1)S(1)}, bf16[2,64,256]{2,1,0:T(8,128)(2,1)S(1)}, u32[]{:S(2)}, u32[]{:S(2)}) %collective-permute-start.23) | collective-permute-done | bytes 65568 | tf_op jit(solution)/shard_map/ppermute | solution.py:25
  77.4 2.3 %collective-permute-start.24 = (bf16[4,16,2048]{2,1,0:T(8,128)(2,1)S(1)}, bf16[4,16,2048]{2,1,0:T(8,128)(2,1)S(1)}, u32[]{:S(2)}, u32[]{:S(2)}) collective-permute-start(bf16[4,16,2048]{2,1,0:T(8,128)(2,1)S(1)} %slice.379), channel_id=1, source_target_pairs={{0,8},{1,9},{2,10},{3,11},{4,12},{5,13},{6,14},{7,15},{8,16},{9,17... | collective-permute-start | bytes 786440 | tf_op jit(solution)/shard_map/ppermute | solution.py:34
  81.4 3.0 %collective-permute-done.28 = bf16[192,256]{1,0:T(8,128)(2,1)S(1)} collective-permute-done((bf16[192,256]{1,0:T(8,128)(2,1)S(1)}, bf16[192,256]{1,0:T(8,128)(2,1)S(1)}, u32[]{:S(2)}, u32[]{:S(2)}) %collective-permute-start.28) | collective-permute-done | bytes 98336 | tf_op jit(solution)/shard_map/ppermute | solution.py:25
  84.5 2.8 %collective-permute-done.25 = bf16[4,16,2048]{2,1,0:T(8,128)(2,1)S(1)} collective-permute-done((bf16[4,16,2048]{2,1,0:T(8,128)(2,1)S(1)}, bf16[4,16,2048]{2,1,0:T(8,128)(2,1)S(1)}, u32[]{:S(2)}, u32[]{:S(2)}) %collective-permute-start.25) | collective-permute-done | bytes 262176 | tf_op jit(solution)/shard_map/ppermute | solution.py:34
  87.8 6.8 %shard_map.103 = f32[8,256]{1,0:T(8,128)S(1)} custom-call(s32[2]{0:T(128)S(1)} %get-tuple-element.106.first_ref, bf16[256,4096]{1,0:T(8,128)(2,1)S(1)} %bitcast.195, bf16[256,4224]{1,0:T(8,128)(2,1)S(1)} %bitcast.194, bf16[501,8192]{1,0:T(8,128)(2,1)S(1)} %bitcast.199, bf16[501,8192]{1,0:T(8,128)(2,1)} %collective-permute-done.11.two_ref), custom_call_target="tpu_custom_call" | custom-call | flops 4202692608 | bytes 20611072 | tf_op jit(solution)/shard_map/pallas_call | solution.py:148
  99.2 5.7 %collective-permute-start.29 = (f32[5,256]{1,0:T(8,128)S(1)}, f32[5,256]{1,0:T(8,128)S(1)}, u32[]{:S(2)}, u32[]{:S(2)}) collective-permute-start(f32[5,256]{1,0:T(8,128)S(1)} %pad_maximum_fusion.13), channel_id=1, source_target_pairs={{0,128},{1,129},{2,130},{3,131},{4,132},{5,133},{6,134},{7,135},{8... | collective-permute-start | bytes 15368 | tf_op jit(solution)/shard_map/ppermute | solution.py:25
  112.1 3.5 %collective-permute-start.36 = (bf16[288,256]{1,0:T(8,128)(2,1)S(1)}, bf16[288,256]{1,0:T(8,128)(2,1)S(1)}, u32[]{:S(2)}, u32[]{:S(2)}) collective-permute-start(bf16[288,256]{1,0:T(8,128)(2,1)S(1)} %get-tuple-element.91), channel_id=1, source_target_pairs={{0,4},{1,5},{2,6},{3,7},{4,0},{5,1},{6,2},{7,3},{8,12},{9,13},{10,... | collective-permute-start | bytes 442376 | tf_op jit(solution)/shard_map/ppermute | solution.py:25
  115.5 2.6 %collective-permute-done.34 = bf16[288,256]{1,0:T(8,128)(2,1)S(1)} collective-permute-done((bf16[288,256]{1,0:T(8,128)(2,1)S(1)}, bf16[288,256]{1,0:T(8,128)(2,1)S(1)}, u32[]{:S(2)}, u32[]{:S(2)}) %collective-permute-start.34) | collective-permute-done | bytes 147488 | tf_op jit(solution)/shard_map/ppermute | solution.py:25
  123.4 3.0 %collective-permute-start.37 = (bf16[96,256]{1,0:T(8,128)(2,1)S(1)}, bf16[96,256]{1,0:T(8,128)(2,1)S(1)}, u32[]{:S(2)}, u32[]{:S(2)}) collective-permute-start(bf16[96,256]{1,0:T(8,128)(2,1)S(1)} %get-tuple-element.86), channel_id=1, source_target_pairs={{0,8},{1,9},{2,10},{3,11},{4,12},{5,13},{6,14},{7,15},{8,0},{9,1},... | collective-permute-start | bytes 147464 | tf_op jit(solution)/shard_map/ppermute | solution.py:25
  128.1 3.6 %collective-permute-done.38 = bf16[96,256]{1,0:T(8,128)(2,1)S(1)} collective-permute-done((bf16[96,256]{1,0:T(8,128)(2,1)S(1)}, bf16[96,256]{1,0:T(8,128)(2,1)S(1)}, u32[]{:S(2)}, u32[]{:S(2)}) %collective-permute-start.38) | collective-permute-done | bytes 49184 | tf_op jit(solution)/shard_map/ppermute | solution.py:25
  133.7 2.6 %collective-permute-start.42 = (f32[10,256]{1,0:T(8,128)S(1)}, f32[10,256]{1,0:T(8,128)S(1)}, u32[]{:S(2)}, u32[]{:S(2)}) collective-permute-start(f32[10,256]{1,0:T(8,128)S(1)} %pad_maximum_fusion.12), channel_id=1, source_target_pairs={{0,64},{1,65},{2,66},{3,67},{4,68},{5,69},{6,70},{7,71},{8,72},{9,... | collective-permute-start | bytes 30728 | tf_op jit(solution)/shard_map/ppermute | solution.py:25
  136.3 6.6 %collective-permute-start.43 = (f32[64,256]{1,0:T(8,128)S(1)}, f32[64,256]{1,0:T(8,128)S(1)}, u32[]{:S(2)}, u32[]{:S(2)}) collective-permute-start(f32[64,256]{1,0:T(8,128)S(1)} %fusion.13), channel_id=1, source_target_pairs={{0,0},{1,1},{2,2},{3,3},{4,32},{5,33},{6,34},{7,35},{8,64},{9,65},... | collective-permute-start | bytes 196616 | tf_op jit(solution)/shard_map/ppermute | solution.py:316
  (222 shorter events, 56.3 us)
Async XLA Ops:
  0.6 42.6 %collective-permute-start.11 = (bf16[501,8192]{1,0:T(8,128)(2,1)}, bf16[501,8192]{1,0:T(8,128)(2,1)}, u32[]{:S(2)}, u32[]{:S(2)}) collective-permute-start(bf16[501,8192]{1,0:T(8,128)(2,1)} %bitcast.196), channel_id=1, source_target_pairs={{0,1},{1,0},{2,3},{3,2},{4,5},{5,4},{6,7},{7,6},{8,9},{9,8},{10,11... | collective-permute-start | bytes 24625160 | tf_op jit(solution)/shard_map/ppermute | solution.py:25
  2.4 13.7 %collective-permute-start = (bf16[1,2,8320]{2,1,0:T(2,128)(2,1)S(1)}, bf16[1,2,8320]{2,1,0:T(2,128)(2,1)S(1)}, u32[]{:S(2)}, u32[]{:S(2)}) collective-permute-start(bf16[1,2,8320]{2,1,0:T(2,128)(2,1)S(1)} %get-tuple-element.80), channel_id=1, source_target_pairs={{0,128},{1,129},{2,130},{3,131},{4,132},{5,133},{6,134},{7,135},{8... | collective-permute-start | bytes 99848 | tf_op jit(solution)/shard_map/ppermute | solution.py:25
  8.8 13.5 %collective-permute-start.1 = (bf16[64,256]{1,0:T(8,128)(2,1)}, bf16[64,256]{1,0:T(8,128)(2,1)S(1)}, u32[]{:S(2)}, u32[]{:S(2)}) collective-permute-start(bf16[64,256]{1,0:T(8,128)(2,1)} %param.13), channel_id=1, source_target_pairs={{0,0},{1,1},{2,2},{3,3},{32,4},{33,5},{34,6},{35,7},{64,8},{65,9},... | collective-permute-start | bytes 98312 | tf_op jit(solution)/shard_map/ppermute | solution.py:244
  43.3 15.7 %collective-permute-start.15 = (bf16[16,4224]{1,0:T(8,128)(2,1)S(1)}, bf16[16,4224]{1,0:T(8,128)(2,1)S(1)}, u32[]{:S(2)}, u32[]{:S(2)}) collective-permute-start(bf16[16,4224]{1,0:T(8,128)(2,1)S(1)} %slice.370), channel_id=1, source_target_pairs={{0,8},{1,9},{2,10},{3,11},{4,12},{5,13},{6,14},{7,15},{8,0},{9,1},... | collective-permute-start | bytes 405512 | tf_op jit(solution)/shard_map/ppermute | solution.py:25
  44.9 14.2 %collective-permute-start.16 = (bf16[16,4224]{1,0:T(8,128)(2,1)S(1)}, bf16[16,4224]{1,0:T(8,128)(2,1)S(1)}, u32[]{:S(2)}, u32[]{:S(2)}) collective-permute-start(bf16[16,4224]{1,0:T(8,128)(2,1)S(1)} %slice.370), channel_id=1, source_target_pairs={{0,24},{1,25},{2,26},{3,27},{4,28},{5,29},{6,30},{7,31},{8,16},{9,... | collective-permute-start | bytes 405512 | tf_op jit(solution)/shard_map/ppermute | solution.py:25
  44.9 14.2 %collective-permute-start.17 = (bf16[16,4224]{1,0:T(8,128)(2,1)S(1)}, bf16[16,4224]{1,0:T(8,128)(2,1)S(1)}, u32[]{:S(2)}, u32[]{:S(2)}) collective-permute-start(bf16[16,4224]{1,0:T(8,128)(2,1)S(1)} %slice.370), channel_id=1, source_target_pairs={{0,16},{1,17},{2,18},{3,19},{4,20},{5,21},{6,22},{7,23},{8,24},{9,... | collective-permute-start | bytes 405512 | tf_op jit(solution)/shard_map/ppermute | solution.py:25
  59.1 16.6 %collective-permute-start.20 = (bf16[4,16,4224]{2,1,0:T(8,128)(2,1)S(1)}, bf16[4,16,4224]{2,1,0:T(8,128)(2,1)S(1)}, u32[]{:S(2)}, u32[]{:S(2)}) collective-permute-start(bf16[4,16,4224]{2,1,0:T(8,128)(2,1)S(1)} %bitcast_dynamic-update-slice_fusion.10), channel_id=1, source_target_pairs={{0,2},{1,3},{2,4},{3,5},{4,6},{5,7},{6,0},{7,1},{8,10},{9,11},{10,... | collective-permute-start | bytes 1622024 | tf_op jit(solution)/shard_map/ppermute | solution.py:34
  59.2 16.5 %collective-permute-start.21 = (bf16[4,16,4224]{2,1,0:T(8,128)(2,1)S(1)}, bf16[4,16,4224]{2,1,0:T(8,128)(2,1)S(1)}, u32[]{:S(2)}, u32[]{:S(2)}) collective-permute-start(bf16[4,16,4224]{2,1,0:T(8,128)(2,1)S(1)} %bitcast_dynamic-update-slice_fusion.10), channel_id=1, source_target_pairs={{0,6},{1,7},{2,0},{3,1},{4,2},{5,3},{6,4},{7,5},{8,14},{9,15},{10,... | collective-permute-start | bytes 1622024 | tf_op jit(solution)/shard_map/ppermute | solution.py:34
  62.4 13.3 %collective-permute-start.18 = (bf16[4,16,4096]{2,1,0:T(8,128)(2,1)S(1)}, bf16[4,16,4096]{2,1,0:T(8,128)(2,1)S(1)}, u32[]{:S(2)}, u32[]{:S(2)}) collective-permute-start(bf16[4,16,4096]{2,1,0:T(8,128)(2,1)S(1)} %bitcast_dynamic-update-slice_fusion.14), channel_id=1, source_target_pairs={{0,8},{1,9},{2,10},{3,11},{4,12},{5,13},{6,14},{7,15},{8,16},{9,17... | collective-permute-start | bytes 1572872 | tf_op jit(solution)/shard_map/ppermute | solution.py:34
  63.4 12.4 %collective-permute-start.19 = (bf16[4,16,4096]{2,1,0:T(8,128)(2,1)S(1)}, bf16[4,16,4096]{2,1,0:T(8,128)(2,1)S(1)}, u32[]{:S(2)}, u32[]{:S(2)}) collective-permute-start(bf16[4,16,4096]{2,1,0:T(8,128)(2,1)S(1)} %bitcast_dynamic-update-slice_fusion.14), channel_id=1, source_target_pairs={{0,24},{1,25},{2,26},{3,27},{4,28},{5,29},{6,30},{7,31},{8,0},{9,1... | collective-permute-start | bytes 1572872 | tf_op jit(solution)/shard_map/ppermute | solution.py:34
  75.8 8.6 %collective-permute-start.28 = (bf16[192,256]{1,0:T(8,128)(2,1)S(1)}, bf16[192,256]{1,0:T(8,128)(2,1)S(1)}, u32[]{:S(2)}, u32[]{:S(2)}) collective-permute-start(bf16[192,256]{1,0:T(8,128)(2,1)S(1)} %pad_maximum_fusion.7), channel_id=1, source_target_pairs={{0,128},{1,129},{2,130},{3,131},{4,132},{5,133},{6,134},{7,135},{8... | collective-permute-start | bytes 294920 | tf_op jit(solution)/shard_map/ppermute | solution.py:25
  75.9 11.8 %collective-permute-start.27 = (bf16[4,16,2176]{2,1,0:T(8,128)(2,1)S(1)}, bf16[4,16,2176]{2,1,0:T(8,128)(2,1)S(1)}, u32[]{:S(2)}, u32[]{:S(2)}) collective-permute-start(bf16[4,16,2176]{2,1,0:T(8,128)(2,1)S(1)} %slice.382), channel_id=1, source_target_pairs={{0,6},{1,7},{2,0},{3,1},{4,2},{5,3},{6,4},{7,5},{8,14},{9,15},{10,... | collective-permute-start | bytes 835592 | tf_op jit(solution)/shard_map/ppermute | solution.py:34
  79.8 7.9 %collective-permute-start.26 = (bf16[4,16,2048]{2,1,0:T(8,128)(2,1)S(1)}, bf16[4,16,2048]{2,1,0:T(8,128)(2,1)S(1)}, u32[]{:S(2)}, u32[]{:S(2)}) collective-permute-start(bf16[4,16,2048]{2,1,0:T(8,128)(2,1)S(1)} %slice.381), channel_id=1, source_target_pairs={{0,2},{1,3},{2,4},{3,5},{4,6},{5,7},{6,0},{7,1},{8,10},{9,11},{10,... | collective-permute-start | bytes 786440 | tf_op jit(solution)/shard_map/ppermute | solution.py:34
  94.7 12.4 %collective-permute-start.30 = (bf16[2,1,64,256]{3,2,1,0:T(8,128)(2,1)S(1)}, bf16[2,1,64,256]{3,2,1,0:T(8,128)(2,1)S(1)}, u32[]{:S(2)}, u32[]{:S(2)}) collective-permute-start(bf16[2,1,64,256]{3,2,1,0:T(8,128)(2,1)S(1)} %bitcast.216), channel_id=1, source_target_pairs={{0,32},{1,33},{2,34},{3,35},{4,36},{5,37},{6,38},{7,39},{8,40},{9,... | collective-permute-start | bytes 196616 | tf_op jit(solution)/shard_map/ppermute | solution.py:25
  96.4 10.7 %collective-permute-start.31 = (bf16[2,1,64,256]{3,2,1,0:T(8,128)(2,1)S(1)}, bf16[2,1,64,256]{3,2,1,0:T(8,128)(2,1)S(1)}, u32[]{:S(2)}, u32[]{:S(2)}) collective-permute-start(bf16[2,1,64,256]{3,2,1,0:T(8,128)(2,1)S(1)} %bitcast.217), channel_id=1, source_target_pairs={{0,96},{1,97},{2,98},{3,99},{4,100},{5,101},{6,102},{7,103},{8,104... | collective-permute-start | bytes 196616 | tf_op jit(solution)/shard_map/ppermute | solution.py:25
  97.5 9.6 %collective-permute-start.32 = (bf16[2,1,64,256]{3,2,1,0:T(8,128)(2,1)S(1)}, bf16[2,1,64,256]{3,2,1,0:T(8,128)(2,1)S(1)}, u32[]{:S(2)}, u32[]{:S(2)}) collective-permute-start(bf16[2,1,64,256]{3,2,1,0:T(8,128)(2,1)S(1)} %bitcast.218), channel_id=1, source_target_pairs={{0,64},{1,65},{2,66},{3,67},{4,68},{5,69},{6,70},{7,71},{8,72},{9,... | collective-permute-start | bytes 196616 | tf_op jit(solution)/shard_map/ppermute | solution.py:25
  99.2 7.9 %collective-permute-start.29 = (f32[5,256]{1,0:T(8,128)S(1)}, f32[5,256]{1,0:T(8,128)S(1)}, u32[]{:S(2)}, u32[]{:S(2)}) collective-permute-start(f32[5,256]{1,0:T(8,128)S(1)} %pad_maximum_fusion.13), channel_id=1, source_target_pairs={{0,128},{1,129},{2,130},{3,131},{4,132},{5,133},{6,134},{7,135},{8... | collective-permute-start | bytes 15368 | tf_op jit(solution)/shard_map/ppermute | solution.py:25
  112.1 10.0 %collective-permute-start.35 = (bf16[288,256]{1,0:T(8,128)(2,1)S(1)}, bf16[288,256]{1,0:T(8,128)(2,1)S(1)}, u32[]{:S(2)}, u32[]{:S(2)}) collective-permute-start(bf16[288,256]{1,0:T(8,128)(2,1)S(1)} %get-tuple-element.90), channel_id=1, source_target_pairs={{0,6},{1,7},{2,4},{3,5},{4,2},{5,3},{6,0},{7,1},{8,14},{9,15},{10,... | collective-permute-start | bytes 442376 | tf_op jit(solution)/shard_map/ppermute | solution.py:25
  112.1 8.0 %collective-permute-start.36 = (bf16[288,256]{1,0:T(8,128)(2,1)S(1)}, bf16[288,256]{1,0:T(8,128)(2,1)S(1)}, u32[]{:S(2)}, u32[]{:S(2)}) collective-permute-start(bf16[288,256]{1,0:T(8,128)(2,1)S(1)} %get-tuple-element.91), channel_id=1, source_target_pairs={{0,4},{1,5},{2,6},{3,7},{4,0},{5,1},{6,2},{7,3},{8,12},{9,13},{10,... | collective-permute-start | bytes 442376 | tf_op jit(solution)/shard_map/ppermute | solution.py:25
  123.4 8.3 %collective-permute-start.37 = (bf16[96,256]{1,0:T(8,128)(2,1)S(1)}, bf16[96,256]{1,0:T(8,128)(2,1)S(1)}, u32[]{:S(2)}, u32[]{:S(2)}) collective-permute-start(bf16[96,256]{1,0:T(8,128)(2,1)S(1)} %get-tuple-element.86), channel_id=1, source_target_pairs={{0,8},{1,9},{2,10},{3,11},{4,12},{5,13},{6,14},{7,15},{8,0},{9,1},... | collective-permute-start | bytes 147464 | tf_op jit(solution)/shard_map/ppermute | solution.py:25
  131.8 11.1 %collective-permute-start.40 = (f32[10,256]{1,0:T(8,128)S(1)}, f32[10,256]{1,0:T(8,128)S(1)}, u32[]{:S(2)}, u32[]{:S(2)}) collective-permute-start(f32[10,256]{1,0:T(8,128)S(1)} %pad_maximum_fusion.12), channel_id=1, source_target_pairs={{0,32},{1,33},{2,34},{3,35},{4,36},{5,37},{6,38},{7,39},{8,40},{9,... | collective-permute-start | bytes 30728 | tf_op jit(solution)/shard_map/ppermute | solution.py:25
  132.7 10.3 %collective-permute-start.41 = (f32[10,256]{1,0:T(8,128)S(1)}, f32[10,256]{1,0:T(8,128)S(1)}, u32[]{:S(2)}, u32[]{:S(2)}) collective-permute-start(f32[10,256]{1,0:T(8,128)S(1)} %pad_maximum_fusion.12), channel_id=1, source_target_pairs={{0,96},{1,97},{2,98},{3,99},{4,100},{5,101},{6,102},{7,103},{8,104... | collective-permute-start | bytes 30728 | tf_op jit(solution)/shard_map/ppermute | solution.py:25
  133.7 9.2 %collective-permute-start.42 = (f32[10,256]{1,0:T(8,128)S(1)}, f32[10,256]{1,0:T(8,128)S(1)}, u32[]{:S(2)}, u32[]{:S(2)}) collective-permute-start(f32[10,256]{1,0:T(8,128)S(1)} %pad_maximum_fusion.12), channel_id=1, source_target_pairs={{0,64},{1,65},{2,66},{3,67},{4,68},{5,69},{6,70},{7,71},{8,72},{9,... | collective-permute-start | bytes 30728 | tf_op jit(solution)/shard_map/ppermute | solution.py:25
  136.3 13.7 %collective-permute-start.43 = (f32[64,256]{1,0:T(8,128)S(1)}, f32[64,256]{1,0:T(8,128)S(1)}, u32[]{:S(2)}, u32[]{:S(2)}) collective-permute-start(f32[64,256]{1,0:T(8,128)S(1)} %fusion.13), channel_id=1, source_target_pairs={{0,0},{1,1},{2,2},{3,3},{4,32},{5,33},{6,34},{7,35},{8,64},{9,65},... | collective-permute-start | bytes 196616 | tf_op jit(solution)/shard_map/ppermute | solution.py:316
  (24 other events, 203.8 us)

commit v3 on v2

--- a/solution.py
+++ b/solution.py
@@ -110,11 +110,10 @@
     one = lax.dot_general(
         p_ref[...], one_ref[:, :half], dims, preferred_element_type=F32
     ) + lax.dot_general(q_ref[:, :half], one_ref[:, half:], dims, preferred_element_type=F32)
-    for copy in copies:
-        copy.wait()
     n = steps // 2
     two = jnp.zeros(one.shape, F32)
-    for j in range(steps):
+    for j, copy in enumerate(copies):
+        copy.wait()
         a_ref = p_ref if j < n else q_ref
         two += lax.dot_general(
             a_ref[:, (j % n) * kb : (j % n + 1) * kb], buf[j], dims, preferred_element_type=F32
@@ -143,7 +142,7 @@
 def local_stats(p, q, head, other_head, first):
     voc, d = head.shape
     rows = p.shape[0]
-    steps = 2
+    steps = 4
     vmem = pl.BlockSpec(memory_space=pltpu.VMEM)
     return pl.pallas_call(
         logits_kernel,
@@ -214,6 +213,50 @@
     return lax.optimization_barrier(values)
 
 
+def tail_kernel(z_ref, mine_ref, got_ref, u_ref, x_ref, grad_ref, own_ref):
+    mine, got = mine_ref[...], got_ref[...]
+    top = jnp.maximum(mine[:2], got[:2])
+    total = mine[2:4] * jnp.exp(mine[:2] - top) + got[2:4] * jnp.exp(got[:2] - top)
+    rest = mine[4:] + got[4:]
+    loss, kept = rest[2:4], rest[4:6]
+    excess = loss - (top + jnp.log(total) - rest[0:2])
+    credit = jnp.where(kept > 0.0, jax.nn.softplus(excess), 0.0)
+    weight = credit / (jnp.sum(credit) / jnp.sum(kept))
+
+    def column(values, n, first):
+        r = lax.broadcasted_iota(jnp.int32, (n, 256), 0) + first
+        j = lax.broadcasted_iota(jnp.int32, (n, 256), 1)
+        at = ((r // 4) % 16) * 16 + (r // 64) * 2 + r % 2
+        picked = jnp.where((r // 2) % 2 == 1, values[1:2], values[0:1])
+        return jnp.sum(jnp.where(at == j, picked, 0.0), axis=1, keepdims=True)
+
+    slope = (column(weight, 512, 0) * u_ref[...].astype(F32)).astype(BF)
+    grad_ref[...] = lax.dot_general(
+        x_ref[...], slope, (((0,), (0,)), ((), ())), preferred_element_type=F32
+    )
+    first = z_ref[0] * 64
+    lane = lax.broadcasted_iota(jnp.int32, (64, 128), 1)
+    own_ref[...] = jnp.where(lane == 0, column(weight, 64, first), column(excess, 64, first))
+
+
+def tail(z, mine, got, u_all, x_all):
+    vmem = pl.BlockSpec(memory_space=pltpu.VMEM)
+    out = (
+        jax.ShapeDtypeStruct((x_all.shape[1], u_all.shape[1]), F32),
+        jax.ShapeDtypeStruct((64, 128), F32),
+    )
+    return pl.pallas_call(
+        tail_kernel,
+        out_shape=out,
+        in_specs=[pl.BlockSpec(memory_space=pltpu.SMEM)] + [vmem] * 4,
+        out_specs=(vmem, vmem),
+        compiler_params=pltpu.CompilerParams(vmem_limit_bytes=16 * 1024 * 1024),
+        cost_estimate=pl.CostEstimate(
+            flops=2 * x_all.size * u_all.shape[1], bytes_accessed=4 * x_all.size, transcendentals=4096
+        ),
+    )(z, mine, got, u_all, x_all)
+
+
 def columns(a, first, size):
     return lax.slice_in_dim(a, first, first + size, axis=a.ndim - 1)
 
@@ -242,7 +285,6 @@
     h = jnp.concatenate([hidden_ref, meta], axis=1)[None]
     h = pair_up(h, ex(h, "z", 4), bits("z", 2), 0)[:, None]
     xs = lax.ppermute(layer_input, AXES, plane_pairs(False))
-    h, xs = sync(h, xs)
 
     h = pair_up(h, ex(h, "z", 2), bits("z", 1), 1)[:, :, None]
     xs = gather_direct(xs, co, "x", 0)
@@ -251,11 +293,14 @@
     h = pair_up(h, ex(h, "z", 1), bits("z", 0), 2).reshape(16, 2 * half + 128)
     xs = gather_direct(xs, co, "y", 0).reshape(2, 2, 4, rows, dv)
     xs = jnp.concatenate([xs[:, j].swapaxes(0, 1).reshape(8 * rows, dv) for j in (0, 1)], 1)
+    h, xs, other_head = sync(h, xs, other_head)
+
+    p, q = h[:, :half], h[:, half:]
+    p = gather_direct(p, co, "y", 0)
     got = ex(xs, "c", 1)
-    h, xs, got, other_head = sync(h, xs, got, other_head)
-
-    p = gather_direct(h[:, :half], co, "y", 0)
-    q = gather_direct(h[:, half:], co, "x", 0)
+    p, q, xs, got = sync(p, q, xs, got)
+
+    q = gather_direct(q, co, "x", 0)
     low, high = [
         jnp.concatenate([columns(a, 0, dv), columns(b, 0, dv), columns(a, dv, dv), columns(b, dv, dv)], 1)
         for a, b in ((xs, got), (got, xs))
@@ -287,15 +332,15 @@
     own = jnp.where(bits("c", 0), own[:, :, :, 1], own[:, :, :, 0])
     own = jnp.where(here[None, None, :, None], own, 0.0).reshape(2, 256)
 
-    got_s = ex(jnp.concatenate([stats, own]), "z", 4)
-    u = u.reshape(2, 1, rows, dv)
-    full = jnp.zeros((2, 4, rows, dv), BF)
-    low_z = co["z"] % 4
-    for mask in (0, 1, 3, 2):
-        block = ex(u, "z", mask) if mask else u
-        full = lax.dynamic_update_slice_in_dim(full, block, low_z ^ mask, 1)
-    stats, own = combine(stats, got_s[:3]), own + got_s[3:]
-    u_all = full.reshape(8 * rows, dv)
+    u_all = jnp.zeros((2, 4, rows, dv), BF)
+    u_all = lax.dynamic_update_slice_in_dim(u_all, u.reshape(2, 1, rows, dv), co["z"] % 4, 1)
+    mine = jnp.concatenate([stats, own])
+    for mask in (1, 3, 2):
+        got_s, got = without_terms(ex(with_terms(mine, u), "z", mask), 5)
+        stats, own = combine(stats, got_s[:3]), own + got_s[3:]
+        got = got.reshape(2, 1, rows, dv)
+        u_all = lax.dynamic_update_slice_in_dim(u_all, got, (co["z"] % 4) ^ mask, 1)
+    u_all = u_all.reshape(8 * rows, dv)
     stats, own, u_all = sync(stats, own, u_all)
 
     terms = lax.dot_general(
@@ -313,27 +358,13 @@
     back = back.reshape(2, 4, 2, rows, dv).transpose(2, 0, 1, 3, 4).reshape(4, 4 * rows, dv)
     stats, back = four_way(stats, back, co, "y")
     stats, back = four_way(stats, back.astype(BF).reshape(4, rows, dv), co, "x")
-    back = lax.ppermute(back, AXES, plane_pairs(True))
+    back = lax.ppermute(back.astype(BF), AXES, plane_pairs(True))
     mine = jnp.concatenate([stats, own])
-    for mask in (1, 3, 2):
-        got_s = ex(mine, "z", mask)
-        stats, own = combine(stats, got_s[:6]), own + got_s[6:]
-    mine_grad = cotangent.astype(F32) + back
-
-    loss, kept = own[:2], own[2:]
-    excess = loss - (stats[:2] + jnp.log(stats[2:4]) - stats[4:])
-    credit = jnp.where(kept > 0.0, jax.nn.softplus(excess), 0.0)
-    weight = credit / (jnp.sum(credit) / jnp.sum(kept))
-    both = jnp.stack([excess, weight]).reshape(2, 2, 16, 8, 2).transpose(0, 3, 2, 1, 4).reshape(2, 8, rows)
-    excess, weight = both[0], both[1]
-    slope = (weight.reshape(8 * rows)[:, None] * u_all.astype(F32)).astype(BF)
-    grad_weight = lax.dot_general(
-        x_all, slope, (((0,), (0,)), ((), ())), preferred_element_type=F32
-    )
-    own_weight = lax.dynamic_index_in_dim(weight, co["z"], 0, keepdims=False)
-    own_excess = lax.dynamic_index_in_dim(excess, co["z"], 0, keepdims=False)
-    grad_input = (own_weight[:, None] * mine_grad).astype(BF)
-    return (own_excess, grad_weight, grad_input)
+    got_s = ex(mine, "z", 4)
+    mine_grad = cotangent.astype(F32) + back.astype(F32)
+    grad_weight, own = tail(co["z"].astype(jnp.int32)[None], mine, got_s, u_all, x_all)
+    grad_input = (own[:, :1] * mine_grad).astype(BF)
+    return (own[:, 1], grad_weight, grad_input)
 
 
 def solution(mesh):

time: 151 us -> 146 us (0.967)
  matrix products: 2.46 us -> 0.91 us
    ppermute x1, waiting for transfers between devices: 6.1 us -> 0.01 us  [on_device(): xs = lax.ppermute(layer_input, AXES, plane_pairs(False))]
    ppermute x1, starting transfers between devices: 4.54 us -> 10.4 us  [on_device(): xs = lax.ppermute(layer_input, AXES, plane_pairs(False))]
    ppermute x34 -> x31, starting transfers between devices: 52.5 us -> 47.3 us  [ex(): return lax.ppermute(a, AXES, [(i, i ^ m) for i in range(256)])]
    ppermute x1, waiting for transfers between devices: 1.32 us -> 6.22 us  [on_device(): back = lax.ppermute(back.astype(BF), AXES, plane_pairs(True))]
    ppermute x1, starting transfers between devices: 6.64 us -> 4.48 us  [on_device(): back = lax.ppermute(back.astype(BF), AXES, plane_pairs(True))]
    ppermute x8, waiting for transfers between devices: 3.2 us -> 5.26 us  [shift(): return lax.ppermute(a, AXES, pairs)]
    ppermute x34 -> x31, waiting for transfers between devices: 41 us -> 39.1 us  [ex(): return lax.ppermute(a, AXES, [(i, i ^ m) for i in range(256)])]
    pallas_call x0 -> x1, Pallas kernels: none -> 1.81 us  [tail(): pl.pallas_call(tail_kernel, out_shape=out, in_specs=[pl.BlockSpec(memory_...]
  transfers between devices with their start and end apart: 44 -> 41, of which waited for: 22 -> 26; matrix products, arithmetic and copies ran while one was open for 8% -> 6% of each run, Pallas kernels for 0% -> 1%
where the time goes in v3:
time: 146 us; the launch traced here: 145 us
  starting transfers between devices  73.7 us (50%)
  waiting for transfers between devices  50.5 us (35%)
  Pallas kernels  7.9 us (5%)
  other arithmetic  6.06 us (4%)
  local copies, waits for them, and re-layouts  4.25 us (3%)
  between operations  1.98 us (1%)
    ppermute x31, starting transfers between devices, ex(): return lax.ppermute(a, AXES, [(i, i ^ m) for i in range(256)])  47.3 us
    ppermute x31, waiting for transfers between devices, ex(): return lax.ppermute(a, AXES, [(i, i ^ m) for i in range(256)])  39.1 us
    ppermute x8, starting transfers between devices, shift(): return lax.ppermute(a, AXES, pairs)  11.5 us
    ppermute x1, starting transfers between devices, on_device(): xs = lax.ppermute(layer_input, AXES, plane_pairs(False))  10.4 us
    ppermute x1, waiting for transfers between devices, on_device(): back = lax.ppermute(back.astype(BF), AXES, plane_pairs(True))  6.22 us
    pallas_call x1, Pallas kernels, local_stats(): pl.pallas_call(logits_kernel, out_shape=jax.ShapeDtypeStruct((8, rows), F...  6.08 us
    ppermute x8, waiting for transfers between devices, shift(): return lax.ppermute(a, AXES, pairs)  5.26 us
    ppermute x1, starting transfers between devices, on_device(): back = lax.ppermute(back.astype(BF), AXES, plane_pairs(True))  4.48 us
  transfers between devices with their start and end apart: 41, of which 26 were waited for; matrix products, arithmetic and copies ran while one was open for 6% of the time, Pallas kernels for 1%

profile of v3, /device:TPU:38, one launch (start us, length us, event | category | flops | bytes accessed | tf_op | source)
XLA Modules:
  0.0 145.3 jit_solution(15923282366492935514)
XLA Ops:
  0.6 10.4 %collective-permute-start.2 = (bf16[64,256]{1,0:T(8,128)(2,1)}, bf16[64,256]{1,0:T(8,128)(2,1)S(1)}, u32[]{:S(2)}, u32[]{:S(2)}) collective-permute-start(bf16[64,256]{1,0:T(8,128)(2,1)} %param.13), channel_id=1, source_target_pairs={{0,0},{1,1},{2,2},{3,3},{32,4},{33,5},{34,6},{35,7},{64,8},{65,9},... | collective-permute-start | bytes 98312 | tf_op jit(solution)/shard_map/ppermute | solution.py:287
  19.3 2.4 %collective-permute-start.5 = (bf16[64,256]{1,0:T(8,128)(2,1)S(1)}, bf16[64,256]{1,0:T(8,128)(2,1)S(1)}, u32[]{:S(2)}, u32[]{:S(2)}) collective-permute-start(bf16[64,256]{1,0:T(8,128)(2,1)S(1)} %collective-permute-done.2), channel_id=1, source_target_pairs={{0,16},{1,17},{2,18},{3,19},{4,20},{5,21},{6,22},{7,23},{8,24},{9,... | collective-permute-start | bytes 98312 | tf_op jit(solution)/shard_map/ppermute | solution.py:25
  24.7 2.5 %collective-permute-done.1 = bf16[2,1,2,8320]{3,2,0,1:T(2,128)(2,1)S(1)} collective-permute-done((bf16[2,1,2,8320]{3,2,0,1:T(2,128)(2,1)S(1)}, bf16[2,1,2,8320]{3,2,0,1:T(2,128)(2,1)S(1)}, u32[]{:S(2)}, u32[]{:S(2)}) %collective-permute-start.1) | collective-permute-done | bytes 66592 | tf_op jit(solution)/shard_map/ppermute | solution.py:25
  29.2 2.4 %collective-permute-start.9 = (bf16[4,64,256]{2,1,0:T(8,128)(2,1)S(1)}, bf16[4,64,256]{2,1,0:T(8,128)(2,1)S(1)}, u32[]{:S(2)}, u32[]{:S(2)}) collective-permute-start(bf16[4,64,256]{2,1,0:T(8,128)(2,1)S(1)} %bitcast_dynamic-update-slice_fusion.22), channel_id=1, source_target_pairs={{0,4},{1,5},{2,6},{3,7},{4,0},{5,1},{6,2},{7,3},{8,12},{9,13},{10,... | collective-permute-start | bytes 393224 | tf_op jit(solution)/shard_map/ppermute | solution.py:25
  33.4 2.6 %collective-permute-done.8 = bf16[4,64,256]{2,1,0:T(8,128)(2,1)S(1)} collective-permute-done((bf16[4,64,256]{2,1,0:T(8,128)(2,1)S(1)}, bf16[4,64,256]{2,1,0:T(8,128)(2,1)S(1)}, u32[]{:S(2)}, u32[]{:S(2)}) %collective-permute-start.8) | collective-permute-done | bytes 131104 | tf_op jit(solution)/shard_map/ppermute | solution.py:25
  47.9 2.4 %collective-permute-start.17 = (bf16[16,4224]{1,0:T(8,128)(2,1)S(1)}, bf16[16,4224]{1,0:T(8,128)(2,1)S(1)}, u32[]{:S(2)}, u32[]{:S(2)}) collective-permute-start(bf16[16,4224]{1,0:T(8,128)(2,1)S(1)} %slice.390), channel_id=1, source_target_pairs={{0,16},{1,17},{2,18},{3,19},{4,20},{5,21},{6,22},{7,23},{8,24},{9,... | collective-permute-start | bytes 405512 | tf_op jit(solution)/shard_map/ppermute | solution.py:25
  55.4 2.4 %collective-permute-start.21 = (bf16[4,16,4224]{2,1,0:T(8,128)(2,1)S(1)}, bf16[4,16,4224]{2,1,0:T(8,128)(2,1)S(1)}, u32[]{:S(2)}, u32[]{:S(2)}) collective-permute-start(bf16[4,16,4224]{2,1,0:T(8,128)(2,1)S(1)} %bitcast_dynamic-update-slice_fusion.10), channel_id=1, source_target_pairs={{0,6},{1,7},{2,0},{3,1},{4,2},{5,3},{6,4},{7,5},{8,14},{9,15},{10,... | collective-permute-start | bytes 1622024 | tf_op jit(solution)/shard_map/ppermute | solution.py:34
  61.6 3.6 %collective-permute-done.22 = bf16[2,2,64,256]{3,2,0,1:T(8,128)(2,1)S(1)} collective-permute-done((bf16[2,2,64,256]{3,2,0,1:T(8,128)(2,1)S(1)}, bf16[2,2,64,256]{3,2,0,1:T(8,128)(2,1)S(1)}, u32[]{:S(2)}, u32[]{:S(2)}) %collective-permute-start.22) | collective-permute-done | bytes 131104 | tf_op jit(solution)/shard_map/ppermute | solution.py:25
  65.3 3.7 %collective-permute-start.23 = (bf16[2,64,256]{2,1,0:T(8,128)(2,1)S(1)}, bf16[2,64,256]{2,1,0:T(8,128)(2,1)S(1)}, u32[]{:S(2)}, u32[]{:S(2)}) collective-permute-start(bf16[2,64,256]{2,1,0:T(8,128)(2,1)S(1)} %fusion.5), channel_id=1, source_target_pairs={{0,64},{1,65},{2,66},{3,67},{4,68},{5,69},{6,70},{7,71},{8,72},{9,... | collective-permute-start | bytes 196616 | tf_op jit(solution)/shard_map/ppermute | solution.py:25
  69.4 2.8 %collective-permute-done.23 = bf16[2,64,256]{2,1,0:T(8,128)(2,1)S(1)} collective-permute-done((bf16[2,64,256]{2,1,0:T(8,128)(2,1)S(1)}, bf16[2,64,256]{2,1,0:T(8,128)(2,1)S(1)}, u32[]{:S(2)}, u32[]{:S(2)}) %collective-permute-start.23) | collective-permute-done | bytes 65568 | tf_op jit(solution)/shard_map/ppermute | solution.py:25
  72.2 3.0 %collective-permute-start.28 = (bf16[192,256]{1,0:T(8,128)(2,1)S(1)}, bf16[192,256]{1,0:T(8,128)(2,1)S(1)}, u32[]{:S(2)}, u32[]{:S(2)}) collective-permute-start(bf16[192,256]{1,0:T(8,128)(2,1)S(1)} %pad_maximum_fusion.7), channel_id=1, source_target_pairs={{0,128},{1,129},{2,130},{3,131},{4,132},{5,133},{6,134},{7,135},{8... | collective-permute-start | bytes 294920 | tf_op jit(solution)/shard_map/ppermute | solution.py:25
  76.1 2.9 %collective-permute-start.24 = (bf16[4,16,2048]{2,1,0:T(8,128)(2,1)S(1)}, bf16[4,16,2048]{2,1,0:T(8,128)(2,1)S(1)}, u32[]{:S(2)}, u32[]{:S(2)}) collective-permute-start(bf16[4,16,2048]{2,1,0:T(8,128)(2,1)S(1)} %slice.399), channel_id=1, source_target_pairs={{0,8},{1,9},{2,10},{3,11},{4,12},{5,13},{6,14},{7,15},{8,16},{9,17... | collective-permute-start | bytes 786440 | tf_op jit(solution)/shard_map/ppermute | solution.py:34
  82.9 3.8 %collective-permute-done.25 = bf16[4,16,2048]{2,1,0:T(8,128)(2,1)S(1)} collective-permute-done((bf16[4,16,2048]{2,1,0:T(8,128)(2,1)S(1)}, bf16[4,16,2048]{2,1,0:T(8,128)(2,1)S(1)}, u32[]{:S(2)}, u32[]{:S(2)}) %collective-permute-start.25) | collective-permute-done | bytes 262176 | tf_op jit(solution)/shard_map/ppermute | solution.py:34
  87.2 6.1 %shard_map.103 = f32[8,256]{1,0:T(8,128)S(1)} custom-call(s32[2]{0:T(128)S(1)} %get-tuple-element.113.first_ref, bf16[256,4096]{1,0:T(8,128)(2,1)S(1)} %bitcast.169, bf16[256,4224]{1,0:T(8,128)(2,1)S(1)} %bitcast.168, bf16[501,8192]{1,0:T(8,128)(2,1)S(1)} %bitcast.173, bf16[501,8192]{1,0:T(8,128)(2,1)} %collective-permute-done.10.two_ref), custom_call_target="tpu_custom_call" | custom-call | flops 4202692608 | bytes 20611072 | tf_op jit(solution)/shard_map/pallas_call | solution.py:147
  93.4 4.2 %collective-permute-start.29 = (bf16[144,256]{1,0:T(8,128)(2,1)S(1)}, bf16[144,256]{1,0:T(8,128)(2,1)S(1)}, u32[]{:S(2)}, u32[]{:S(2)}) collective-permute-start(bf16[144,256]{1,0:T(8,128)(2,1)S(1)} %pad_maximum_fusion.8), channel_id=1, source_target_pairs={{0,32},{1,33},{2,34},{3,35},{4,36},{5,37},{6,38},{7,39},{8,40},{9,... | collective-permute-start | bytes 221192 | tf_op jit(solution)/shard_map/ppermute | solution.py:25
  97.6 2.5 %collective-permute-start.31 = (bf16[144,256]{1,0:T(8,128)(2,1)S(1)}, bf16[144,256]{1,0:T(8,128)(2,1)S(1)}, u32[]{:S(2)}, u32[]{:S(2)}) collective-permute-start(bf16[144,256]{1,0:T(8,128)(2,1)S(1)} %pad_maximum_fusion.8), channel_id=1, source_target_pairs={{0,64},{1,65},{2,66},{3,67},{4,68},{5,69},{6,70},{7,71},{8,72},{9,... | collective-permute-start | bytes 221192 | tf_op jit(solution)/shard_map/ppermute | solution.py:25
  100.1 3.2 %collective-permute-done.31 = bf16[144,256]{1,0:T(8,128)(2,1)S(1)} collective-permute-done((bf16[144,256]{1,0:T(8,128)(2,1)S(1)}, bf16[144,256]{1,0:T(8,128)(2,1)S(1)}, u32[]{:S(2)}, u32[]{:S(2)}) %collective-permute-start.31) | collective-permute-done | bytes 73760 | tf_op jit(solution)/shard_map/ppermute | solution.py:25
  109.2 2.8 %collective-permute-start.35 = (bf16[288,256]{1,0:T(8,128)(2,1)S(1)}, bf16[288,256]{1,0:T(8,128)(2,1)S(1)}, u32[]{:S(2)}, u32[]{:S(2)}) collective-permute-start(bf16[288,256]{1,0:T(8,128)(2,1)S(1)} %get-tuple-element.97), channel_id=1, source_target_pairs={{0,4},{1,5},{2,6},{3,7},{4,0},{5,1},{6,2},{7,3},{8,12},{9,13},{10,... | collective-permute-start | bytes 442376 | tf_op jit(solution)/shard_map/ppermute | solution.py:25
  112.0 2.6 %collective-permute-done.33 = bf16[288,256]{1,0:T(8,128)(2,1)S(1)} collective-permute-done((bf16[288,256]{1,0:T(8,128)(2,1)S(1)}, bf16[288,256]{1,0:T(8,128)(2,1)S(1)}, u32[]{:S(2)}, u32[]{:S(2)}) %collective-permute-start.33) | collective-permute-done | bytes 147488 | tf_op jit(solution)/shard_map/ppermute | solution.py:25
  120.1 2.7 %collective-permute-start.36 = (bf16[96,256]{1,0:T(8,128)(2,1)S(1)}, bf16[96,256]{1,0:T(8,128)(2,1)S(1)}, u32[]{:S(2)}, u32[]{:S(2)}) collective-permute-start(bf16[96,256]{1,0:T(8,128)(2,1)S(1)} %get-tuple-element.92), channel_id=1, source_target_pairs={{0,8},{1,9},{2,10},{3,11},{4,12},{5,13},{6,14},{7,15},{8,0},{9,1},... | collective-permute-start | bytes 147464 | tf_op jit(solution)/shard_map/ppermute | solution.py:25
  124.5 3.6 %collective-permute-done.37 = bf16[96,256]{1,0:T(8,128)(2,1)S(1)} collective-permute-done((bf16[96,256]{1,0:T(8,128)(2,1)S(1)}, bf16[96,256]{1,0:T(8,128)(2,1)S(1)}, u32[]{:S(2)}, u32[]{:S(2)}) %collective-permute-start.37) | collective-permute-done | bytes 49184 | tf_op jit(solution)/shard_map/ppermute | solution.py:25
  128.2 3.1 %collective-permute-start.39 = (f32[10,256]{1,0:T(8,128)S(1)}, f32[10,256]{1,0:T(8,128)S(1)}, u32[]{:S(2)}, u32[]{:S(2)}) collective-permute-start(f32[10,256]{1,0:T(8,128)S(1)} %pad_maximum_fusion.13.mine_ref), channel_id=1, source_target_pairs={{0,128},{1,129},{2,130},{3,131},{4,132},{5,133},{6,134},{7,135},{8... | collective-permute-start | bytes 30728 | tf_op jit(solution)/shard_map/ppermute | solution.py:25
  131.3 4.5 %collective-permute-start.40 = (bf16[64,256]{1,0:T(8,128)(2,1)S(1)}, bf16[64,256]{1,0:T(8,128)(2,1)S(1)}, u32[]{:S(2)}, u32[]{:S(2)}) collective-permute-start(bf16[64,256]{1,0:T(8,128)(2,1)S(1)} %fusion.8), channel_id=1, source_target_pairs={{0,0},{1,1},{2,2},{3,3},{4,32},{5,33},{6,34},{7,35},{8,64},{9,65},... | collective-permute-start | bytes 98312 | tf_op jit(solution)/shard_map/ppermute | solution.py:361
  138.4 6.2 %collective-permute-done.40 = bf16[64,256]{1,0:T(8,128)(2,1)S(1)} collective-permute-done((bf16[64,256]{1,0:T(8,128)(2,1)S(1)}, bf16[64,256]{1,0:T(8,128)(2,1)S(1)}, u32[]{:S(2)}, u32[]{:S(2)}) %collective-permute-start.40) | collective-permute-done | bytes 32800 | tf_op jit(solution)/shard_map/ppermute | solution.py:361
  (215 shorter events, 56.9 us)
Async XLA Ops:
  0.6 16.8 %collective-permute-start.2 = (bf16[64,256]{1,0:T(8,128)(2,1)}, bf16[64,256]{1,0:T(8,128)(2,1)S(1)}, u32[]{:S(2)}, u32[]{:S(2)}) collective-permute-start(bf16[64,256]{1,0:T(8,128)(2,1)} %param.13), channel_id=1, source_target_pairs={{0,0},{1,1},{2,2},{3,3},{32,4},{33,5},{34,6},{35,7},{64,8},{65,9},... | collective-permute-start | bytes 98312 | tf_op jit(solution)/shard_map/ppermute | solution.py:287
  11.1 26.2 %collective-permute-start.10 = (bf16[501,8192]{1,0:T(8,128)(2,1)}, bf16[501,8192]{1,0:T(8,128)(2,1)}, u32[]{:S(2)}, u32[]{:S(2)}) collective-permute-start(bf16[501,8192]{1,0:T(8,128)(2,1)} %bitcast.170), channel_id=1, source_target_pairs={{0,1},{1,0},{2,3},{3,2},{4,5},{5,4},{6,7},{7,6},{8,9},{9,8},{10,11... | collective-permute-start | bytes 24625160 | tf_op jit(solution)/shard_map/ppermute | solution.py:25
  12.8 8.9 %collective-permute-start = (bf16[1,2,8320]{2,1,0:T(2,128)(2,1)S(1)}, bf16[1,2,8320]{2,1,0:T(2,128)(2,1)S(1)}, u32[]{:S(2)}, u32[]{:S(2)}) collective-permute-start(bf16[1,2,8320]{2,1,0:T(2,128)(2,1)S(1)} %get-tuple-element.85), channel_id=1, source_target_pairs={{0,128},{1,129},{2,130},{3,131},{4,132},{5,133},{6,134},{7,135},{8... | collective-permute-start | bytes 99848 | tf_op jit(solution)/shard_map/ppermute | solution.py:25
  28.2 7.8 %collective-permute-start.8 = (bf16[4,64,256]{2,1,0:T(8,128)(2,1)S(1)}, bf16[4,64,256]{2,1,0:T(8,128)(2,1)S(1)}, u32[]{:S(2)}, u32[]{:S(2)}) collective-permute-start(bf16[4,64,256]{2,1,0:T(8,128)(2,1)S(1)} %bitcast_dynamic-update-slice_fusion.22), channel_id=1, source_target_pairs={{0,6},{1,7},{2,4},{3,5},{4,2},{5,3},{6,0},{7,1},{8,14},{9,15},{10,... | collective-permute-start | bytes 393224 | tf_op jit(solution)/shard_map/ppermute | solution.py:25
  29.2 6.8 %collective-permute-start.9 = (bf16[4,64,256]{2,1,0:T(8,128)(2,1)S(1)}, bf16[4,64,256]{2,1,0:T(8,128)(2,1)S(1)}, u32[]{:S(2)}, u32[]{:S(2)}) collective-permute-start(bf16[4,64,256]{2,1,0:T(8,128)(2,1)S(1)} %bitcast_dynamic-update-slice_fusion.22), channel_id=1, source_target_pairs={{0,4},{1,5},{2,6},{3,7},{4,0},{5,1},{6,2},{7,3},{8,12},{9,13},{10,... | collective-permute-start | bytes 393224 | tf_op jit(solution)/shard_map/ppermute | solution.py:25
  39.6 6.5 %collective-permute-start.13 = (bf16[16,4096]{1,0:T(8,128)(2,1)S(1)}, bf16[16,4096]{1,0:T(8,128)(2,1)S(1)}, u32[]{:S(2)}, u32[]{:S(2)}) collective-permute-start(bf16[16,4096]{1,0:T(8,128)(2,1)S(1)} %slice.389), channel_id=1, source_target_pairs={{0,4},{1,5},{2,6},{3,7},{4,0},{5,1},{6,2},{7,3},{8,12},{9,13},{10,... | collective-permute-start | bytes 393224 | tf_op jit(solution)/shard_map/ppermute | solution.py:25
  47.9 6.6 %collective-permute-start.17 = (bf16[16,4224]{1,0:T(8,128)(2,1)S(1)}, bf16[16,4224]{1,0:T(8,128)(2,1)S(1)}, u32[]{:S(2)}, u32[]{:S(2)}) collective-permute-start(bf16[16,4224]{1,0:T(8,128)(2,1)S(1)} %slice.390), channel_id=1, source_target_pairs={{0,16},{1,17},{2,18},{3,19},{4,20},{5,21},{6,22},{7,23},{8,24},{9,... | collective-permute-start | bytes 405512 | tf_op jit(solution)/shard_map/ppermute | solution.py:25
  54.5 17.7 %collective-permute-start.20 = (bf16[4,16,4224]{2,1,0:T(8,128)(2,1)S(1)}, bf16[4,16,4224]{2,1,0:T(8,128)(2,1)S(1)}, u32[]{:S(2)}, u32[]{:S(2)}) collective-permute-start(bf16[4,16,4224]{2,1,0:T(8,128)(2,1)S(1)} %bitcast_dynamic-update-slice_fusion.10), channel_id=1, source_target_pairs={{0,2},{1,3},{2,4},{3,5},{4,6},{5,7},{6,0},{7,1},{8,10},{9,11},{10,... | collective-permute-start | bytes 1622024 | tf_op jit(solution)/shard_map/ppermute | solution.py:34
  55.4 16.8 %collective-permute-start.21 = (bf16[4,16,4224]{2,1,0:T(8,128)(2,1)S(1)}, bf16[4,16,4224]{2,1,0:T(8,128)(2,1)S(1)}, u32[]{:S(2)}, u32[]{:S(2)}) collective-permute-start(bf16[4,16,4224]{2,1,0:T(8,128)(2,1)S(1)} %bitcast_dynamic-update-slice_fusion.10), channel_id=1, source_target_pairs={{0,6},{1,7},{2,0},{3,1},{4,2},{5,3},{6,4},{7,5},{8,14},{9,15},{10,... | collective-permute-start | bytes 1622024 | tf_op jit(solution)/shard_map/ppermute | solution.py:34
  57.8 14.3 %collective-permute-start.18 = (bf16[4,16,4096]{2,1,0:T(8,128)(2,1)S(1)}, bf16[4,16,4096]{2,1,0:T(8,128)(2,1)S(1)}, u32[]{:S(2)}, u32[]{:S(2)}) collective-permute-start(bf16[4,16,4096]{2,1,0:T(8,128)(2,1)S(1)} %bitcast_dynamic-update-slice_fusion.14), channel_id=1, source_target_pairs={{0,8},{1,9},{2,10},{3,11},{4,12},{5,13},{6,14},{7,15},{8,16},{9,17... | collective-permute-start | bytes 1572872 | tf_op jit(solution)/shard_map/ppermute | solution.py:34
  59.9 12.3 %collective-permute-start.19 = (bf16[4,16,4096]{2,1,0:T(8,128)(2,1)S(1)}, bf16[4,16,4096]{2,1,0:T(8,128)(2,1)S(1)}, u32[]{:S(2)}, u32[]{:S(2)}) collective-permute-start(bf16[4,16,4096]{2,1,0:T(8,128)(2,1)S(1)} %bitcast_dynamic-update-slice_fusion.14), channel_id=1, source_target_pairs={{0,24},{1,25},{2,26},{3,27},{4,28},{5,29},{6,30},{7,31},{8,0},{9,1... | collective-permute-start | bytes 1572872 | tf_op jit(solution)/shard_map/ppermute | solution.py:34
  65.3 6.8 %collective-permute-start.23 = (bf16[2,64,256]{2,1,0:T(8,128)(2,1)S(1)}, bf16[2,64,256]{2,1,0:T(8,128)(2,1)S(1)}, u32[]{:S(2)}, u32[]{:S(2)}) collective-permute-start(bf16[2,64,256]{2,1,0:T(8,128)(2,1)S(1)} %fusion.5), channel_id=1, source_target_pairs={{0,64},{1,65},{2,66},{3,67},{4,68},{5,69},{6,70},{7,71},{8,72},{9,... | collective-permute-start | bytes 196616 | tf_op jit(solution)/shard_map/ppermute | solution.py:25
  72.2 9.5 %collective-permute-start.28 = (bf16[192,256]{1,0:T(8,128)(2,1)S(1)}, bf16[192,256]{1,0:T(8,128)(2,1)S(1)}, u32[]{:S(2)}, u32[]{:S(2)}) collective-permute-start(bf16[192,256]{1,0:T(8,128)(2,1)S(1)} %pad_maximum_fusion.7), channel_id=1, source_target_pairs={{0,128},{1,129},{2,130},{3,131},{4,132},{5,133},{6,134},{7,135},{8... | collective-permute-start | bytes 294920 | tf_op jit(solution)/shard_map/ppermute | solution.py:25
  75.3 11.7 %collective-permute-start.27 = (bf16[4,16,2176]{2,1,0:T(8,128)(2,1)S(1)}, bf16[4,16,2176]{2,1,0:T(8,128)(2,1)S(1)}, u32[]{:S(2)}, u32[]{:S(2)}) collective-permute-start(bf16[4,16,2176]{2,1,0:T(8,128)(2,1)S(1)} %slice.402), channel_id=1, source_target_pairs={{0,6},{1,7},{2,0},{3,1},{4,2},{5,3},{6,4},{7,5},{8,14},{9,15},{10,... | collective-permute-start | bytes 835592 | tf_op jit(solution)/shard_map/ppermute | solution.py:34
  76.1 6.8 %collective-permute-start.24 = (bf16[4,16,2048]{2,1,0:T(8,128)(2,1)S(1)}, bf16[4,16,2048]{2,1,0:T(8,128)(2,1)S(1)}, u32[]{:S(2)}, u32[]{:S(2)}) collective-permute-start(bf16[4,16,2048]{2,1,0:T(8,128)(2,1)S(1)} %slice.399), channel_id=1, source_target_pairs={{0,8},{1,9},{2,10},{3,11},{4,12},{5,13},{6,14},{7,15},{8,16},{9,17... | collective-permute-start | bytes 786440 | tf_op jit(solution)/shard_map/ppermute | solution.py:34
  79.0 7.7 %collective-permute-start.25 = (bf16[4,16,2048]{2,1,0:T(8,128)(2,1)S(1)}, bf16[4,16,2048]{2,1,0:T(8,128)(2,1)S(1)}, u32[]{:S(2)}, u32[]{:S(2)}) collective-permute-start(bf16[4,16,2048]{2,1,0:T(8,128)(2,1)S(1)} %slice.400), channel_id=1, source_target_pairs={{0,24},{1,25},{2,26},{3,27},{4,28},{5,29},{6,30},{7,31},{8,0},{9,1... | collective-permute-start | bytes 786440 | tf_op jit(solution)/shard_map/ppermute | solution.py:34
  79.2 7.9 %collective-permute-start.26 = (bf16[4,16,2048]{2,1,0:T(8,128)(2,1)S(1)}, bf16[4,16,2048]{2,1,0:T(8,128)(2,1)S(1)}, u32[]{:S(2)}, u32[]{:S(2)}) collective-permute-start(bf16[4,16,2048]{2,1,0:T(8,128)(2,1)S(1)} %slice.401), channel_id=1, source_target_pairs={{0,2},{1,3},{2,4},{3,5},{4,6},{5,7},{6,0},{7,1},{8,10},{9,11},{10,... | collective-permute-start | bytes 786440 | tf_op jit(solution)/shard_map/ppermute | solution.py:34
  93.4 10.1 %collective-permute-start.29 = (bf16[144,256]{1,0:T(8,128)(2,1)S(1)}, bf16[144,256]{1,0:T(8,128)(2,1)S(1)}, u32[]{:S(2)}, u32[]{:S(2)}) collective-permute-start(bf16[144,256]{1,0:T(8,128)(2,1)S(1)} %pad_maximum_fusion.8), channel_id=1, source_target_pairs={{0,32},{1,33},{2,34},{3,35},{4,36},{5,37},{6,38},{7,39},{8,40},{9,... | collective-permute-start | bytes 221192 | tf_op jit(solution)/shard_map/ppermute | solution.py:25
  107.8 6.8 %collective-permute-start.33 = (bf16[288,256]{1,0:T(8,128)(2,1)S(1)}, bf16[288,256]{1,0:T(8,128)(2,1)S(1)}, u32[]{:S(2)}, u32[]{:S(2)}) collective-permute-start(bf16[288,256]{1,0:T(8,128)(2,1)S(1)} %get-tuple-element.95), channel_id=1, source_target_pairs={{0,2},{1,3},{2,0},{3,1},{4,6},{5,7},{6,4},{7,5},{8,10},{9,11},{10,... | collective-permute-start | bytes 442376 | tf_op jit(solution)/shard_map/ppermute | solution.py:25
  107.9 10.3 %collective-permute-start.34 = (bf16[288,256]{1,0:T(8,128)(2,1)S(1)}, bf16[288,256]{1,0:T(8,128)(2,1)S(1)}, u32[]{:S(2)}, u32[]{:S(2)}) collective-permute-start(bf16[288,256]{1,0:T(8,128)(2,1)S(1)} %get-tuple-element.96), channel_id=1, source_target_pairs={{0,6},{1,7},{2,4},{3,5},{4,2},{5,3},{6,0},{7,1},{8,14},{9,15},{10,... | collective-permute-start | bytes 442376 | tf_op jit(solution)/shard_map/ppermute | solution.py:25
  109.2 7.5 %collective-permute-start.35 = (bf16[288,256]{1,0:T(8,128)(2,1)S(1)}, bf16[288,256]{1,0:T(8,128)(2,1)S(1)}, u32[]{:S(2)}, u32[]{:S(2)}) collective-permute-start(bf16[288,256]{1,0:T(8,128)(2,1)S(1)} %get-tuple-element.97), channel_id=1, source_target_pairs={{0,4},{1,5},{2,6},{3,7},{4,0},{5,1},{6,2},{7,3},{8,12},{9,13},{10,... | collective-permute-start | bytes 442376 | tf_op jit(solution)/shard_map/ppermute | solution.py:25
  120.1 8.0 %collective-permute-start.36 = (bf16[96,256]{1,0:T(8,128)(2,1)S(1)}, bf16[96,256]{1,0:T(8,128)(2,1)S(1)}, u32[]{:S(2)}, u32[]{:S(2)}) collective-permute-start(bf16[96,256]{1,0:T(8,128)(2,1)S(1)} %get-tuple-element.92), channel_id=1, source_target_pairs={{0,8},{1,9},{2,10},{3,11},{4,12},{5,13},{6,14},{7,15},{8,0},{9,1},... | collective-permute-start | bytes 147464 | tf_op jit(solution)/shard_map/ppermute | solution.py:25
  128.2 7.7 %collective-permute-start.39 = (f32[10,256]{1,0:T(8,128)S(1)}, f32[10,256]{1,0:T(8,128)S(1)}, u32[]{:S(2)}, u32[]{:S(2)}) collective-permute-start(f32[10,256]{1,0:T(8,128)S(1)} %pad_maximum_fusion.13.mine_ref), channel_id=1, source_target_pairs={{0,128},{1,129},{2,130},{3,131},{4,132},{5,133},{6,134},{7,135},{8... | collective-permute-start | bytes 30728 | tf_op jit(solution)/shard_map/ppermute | solution.py:25
  131.3 13.3 %collective-permute-start.40 = (bf16[64,256]{1,0:T(8,128)(2,1)S(1)}, bf16[64,256]{1,0:T(8,128)(2,1)S(1)}, u32[]{:S(2)}, u32[]{:S(2)}) collective-permute-start(bf16[64,256]{1,0:T(8,128)(2,1)S(1)} %fusion.8), channel_id=1, source_target_pairs={{0,0},{1,1},{2,2},{3,3},{4,32},{5,33},{6,34},{7,35},{8,64},{9,65},... | collective-permute-start | bytes 98312 | tf_op jit(solution)/shard_map/ppermute | solution.py:361
  (21 other events, 188.8 us)

commit v4 on v3

--- a/solution.py
+++ b/solution.py
@@ -221,7 +221,20 @@
     loss, kept = rest[2:4], rest[4:6]
     excess = loss - (top + jnp.log(total) - rest[0:2])
     credit = jnp.where(kept > 0.0, jax.nn.softplus(excess), 0.0)
-    weight = credit / (jnp.sum(credit) / jnp.sum(kept))
+    weight = credit / (jnp.sum(credit) / jnp.sum(jnp.where(kept > 0.0, 1.0, 0.0)))
+
+    def by_slot(values):
+        n = u_ref.shape[0]
+        slots = n // 8
+        r = lax.broadcasted_iota(jnp.int32, (n, 256), 0)
+        j = lax.broadcasted_iota(jnp.int32, (n, 256), 1)
+        code = r + 1
+        for g in range(1, 8):
+            code = code + jnp.where(r >= g * slots, 64 - slots, 0)
+        at = ((j // 2) % 8) * 64
+        number = kept.astype(jnp.int32)
+        hits = [jnp.where(at + number[c : c + 1] == code, values[c : c + 1], 0.0) for c in (0, 1)]
+        return jnp.sum(hits[0] + hits[1], axis=1, keepdims=True)
 
     def column(values, n, first):
         r = lax.broadcasted_iota(jnp.int32, (n, 256), 0) + first
@@ -230,7 +243,7 @@
         picked = jnp.where((r // 2) % 2 == 1, values[1:2], values[0:1])
         return jnp.sum(jnp.where(at == j, picked, 0.0), axis=1, keepdims=True)
 
-    slope = (column(weight, 512, 0) * u_ref[...].astype(F32)).astype(BF)
+    slope = (by_slot(weight) * u_ref[...].astype(F32)).astype(BF)
     grad_ref[...] = lax.dot_general(
         x_ref[...], slope, (((0,), (0,)), ((), ())), preferred_element_type=F32
     )
@@ -269,6 +282,7 @@
     half = head.shape[0] // 2
     dv = layer_weight.shape[1]
     rows = train_loss.shape[0]
+    slots = keep_index.shape[1]
     vocab = lax.axis_index("vocab")
     shard = lax.axis_index("dp") * 32 + vocab
 
@@ -284,15 +298,19 @@
     meta = jnp.where(lane < 3, meta, 0).astype(BF)
     h = jnp.concatenate([hidden_ref, meta], axis=1)[None]
     h = pair_up(h, ex(h, "z", 4), bits("z", 2), 0)[:, None]
-    xs = lax.ppermute(layer_input, AXES, plane_pairs(False))
+    hot = (keep_index[0][:, None] == jnp.arange(rows, dtype=jnp.int32)[None, :]).astype(BF)
+    inputs, cotangent_kept = [
+        jnp.dot(hot, full, preferred_element_type=F32).astype(BF) for full in (layer_input, cotangent)
+    ]
+    xs = lax.ppermute(inputs, AXES, plane_pairs(False))
 
     h = pair_up(h, ex(h, "z", 2), bits("z", 1), 1)[:, :, None]
     xs = gather_direct(xs, co, "x", 0)
     h, xs = sync(h, xs)
 
     h = pair_up(h, ex(h, "z", 1), bits("z", 0), 2).reshape(16, 2 * half + 128)
-    xs = gather_direct(xs, co, "y", 0).reshape(2, 2, 4, rows, dv)
-    xs = jnp.concatenate([xs[:, j].swapaxes(0, 1).reshape(8 * rows, dv) for j in (0, 1)], 1)
+    xs = gather_direct(xs, co, "y", 0).reshape(2, 2, 4, slots, dv)
+    xs = jnp.concatenate([xs[:, j].swapaxes(0, 1).reshape(8 * slots, dv) for j in (0, 1)], 1)
     h, xs, other_head = sync(h, xs, other_head)
 
     p, q = h[:, :half], h[:, half:]
@@ -310,14 +328,14 @@
     p, q, pre = sync(p, q, pre)
 
     p_near, q_near = ring_first(p, "x"), ring_first(q, "y")
-    pre = halve(pre.reshape(2, 2, 2, rows, dv), co, "z", 0, 2, BF)
-    pre = halve(pre, co, "z", 1, 1, BF).astype(BF).reshape(2 * rows, dv)
+    pre = halve(pre.reshape(2, 2, 2, slots, dv), co, "z", 0, 2, BF)
+    pre = halve(pre, co, "z", 1, 1, BF).astype(BF).reshape(2 * slots, dv)
     p_near, q_near, pre = sync(p_near, q_near, pre)
 
     p_far, q_far = ring_second(*p_near, "x", half // 2), ring_second(*q_near, "y", half // 2)
-    got = ex(jnp.concatenate([pre, cotangent]), "z", 4)
-    pre = pre.astype(F32) + got[: 2 * rows].astype(F32)
-    cot = pair_up(cotangent, got[2 * rows :], bits("z", 2), 0)
+    got = ex(jnp.concatenate([pre, cotangent_kept]), "z", 4)
+    pre = pre.astype(F32) + got[: 2 * slots].astype(F32)
+    cot = pair_up(cotangent_kept, got[2 * slots :], bits("z", 2), 0)
     u = (cot.astype(F32) * derivative(pre)).astype(BF)
     p_far, q_far, u = sync(p_far, q_far, u)
 
@@ -327,20 +345,22 @@
     stats, u = sync(local_stats(p, q, head, other_head, first)[:3], u)
 
     here = jnp.arange(8, dtype=jnp.int32) == co["z"]
-    marks = jnp.any(keep_index[0][None, :] == jnp.arange(rows, dtype=jnp.int32)[:, None], axis=1)
+    number = jnp.arange(1, slots + 1, dtype=jnp.int32)
+    here_kept = keep_index[0][None, :] == jnp.arange(rows, dtype=jnp.int32)[:, None]
+    marks = jnp.sum(jnp.where(here_kept, number[None, :], 0), axis=1)
     own = jnp.stack([train_loss, marks.astype(F32)]).reshape(2, 16, 1, 2, 2)
     own = jnp.where(bits("c", 0), own[:, :, :, 1], own[:, :, :, 0])
     own = jnp.where(here[None, None, :, None], own, 0.0).reshape(2, 256)
 
-    u_all = jnp.zeros((2, 4, rows, dv), BF)
-    u_all = lax.dynamic_update_slice_in_dim(u_all, u.reshape(2, 1, rows, dv), co["z"] % 4, 1)
+    u_all = jnp.zeros((2, 4, slots, dv), BF)
+    u_all = lax.dynamic_update_slice_in_dim(u_all, u.reshape(2, 1, slots, dv), co["z"] % 4, 1)
     mine = jnp.concatenate([stats, own])
     for mask in (1, 3, 2):
         got_s, got = without_terms(ex(with_terms(mine, u), "z", mask), 5)
         stats, own = combine(stats, got_s[:3]), own + got_s[3:]
-        got = got.reshape(2, 1, rows, dv)
+        got = got.reshape(2, 1, slots, dv)
         u_all = lax.dynamic_update_slice_in_dim(u_all, got, (co["z"] % 4) ^ mask, 1)
-    u_all = u_all.reshape(8 * rows, dv)
+    u_all = u_all.reshape(8 * slots, dv)
     stats, own, u_all = sync(stats, own, u_all)
 
     terms = lax.dot_general(
@@ -355,13 +375,14 @@
         for a, b in ((stats, got_s[:3]), (own, got_s[3:]))
     ]
     back = (keep.astype(F32) + got.astype(F32)).astype(BF)
-    back = back.reshape(2, 4, 2, rows, dv).transpose(2, 0, 1, 3, 4).reshape(4, 4 * rows, dv)
+    back = back.reshape(2, 4, 2, slots, dv).transpose(2, 0, 1, 3, 4).reshape(4, 4 * slots, dv)
     stats, back = four_way(stats, back, co, "y")
-    stats, back = four_way(stats, back.astype(BF).reshape(4, rows, dv), co, "x")
+    stats, back = four_way(stats, back.astype(BF).reshape(4, slots, dv), co, "x")
     back = lax.ppermute(back.astype(BF), AXES, plane_pairs(True))
     mine = jnp.concatenate([stats, own])
     got_s = ex(mine, "z", 4)
-    mine_grad = cotangent.astype(F32) + back.astype(F32)
+    spread = lax.dot_general(hot, back, (((0,), (0,)), ((), ())), preferred_element_type=F32)
+    mine_grad = cotangent.astype(F32) + spread
     grad_weight, own = tail(co["z"].astype(jnp.int32)[None], mine, got_s, u_all, x_all)
     grad_input = (own[:, :1] * mine_grad).astype(BF)
     return (own[:, 1], grad_weight, grad_input)

time: 146 us -> 142 us (0.973)
  waiting for transfers between devices: 50.5 us -> 46.8 us
  matrix products: 0.91 us -> 3.65 us
  other arithmetic: 6.06 us -> 4.36 us
    ppermute x31, waiting for transfers between devices: 39.1 us -> 35.6 us  [ex(): return lax.ppermute(a, AXES, [(i, i ^ m) for i in range(256)])]
    dot_general x0 -> x3, matrix products: none -> 2.88 us  [the longest x2 1.99 us: on_device(): jnp.dot(hot, full, preferred_element_type=F32).astype(BF)]
    ppermute x1, starting transfers between devices: 4.48 us -> 5.98 us  [on_device(): back = lax.ppermute(back.astype(BF), AXES, plane_pairs(True))]
where the time goes in v4:
time: 142 us
  starting transfers between devices  73.2 us (52%)
  waiting for transfers between devices  46.8 us (33%)
  Pallas kernels  7.85 us (6%)
  other arithmetic  4.36 us (3%)
  local copies, waits for them, and re-layouts  4.12 us (3%)
  matrix products  3.65 us (3%)
  between operations  2.07 us (1%)
    ppermute x31, starting transfers between devices, ex(): return lax.ppermute(a, AXES, [(i, i ^ m) for i in range(256)])  46.4 us
    ppermute x31, waiting for transfers between devices, ex(): return lax.ppermute(a, AXES, [(i, i ^ m) for i in range(256)])  35.6 us
    ppermute x8, starting transfers between devices, shift(): return lax.ppermute(a, AXES, pairs)  10.5 us
    ppermute x1, starting transfers between devices, on_device(): xs = lax.ppermute(inputs, AXES, plane_pairs(False))  10.3 us
    ppermute x8, waiting for transfers between devices, shift(): return lax.ppermute(a, AXES, pairs)  6.4 us
    pallas_call x1, Pallas kernels, local_stats(): pl.pallas_call(logits_kernel, out_shape=jax.ShapeDtypeStruct((8, rows), F...  6.09 us
    ppermute x1, starting transfers between devices, on_device(): back = lax.ppermute(back.astype(BF), AXES, plane_pairs(True))  5.98 us
    ppermute x1, waiting for transfers between devices, on_device(): back = lax.ppermute(back.astype(BF), AXES, plane_pairs(True))  4.78 us
  transfers between devices with their start and end apart: 41, of which 26 were waited for; matrix products, arithmetic and copies ran while one was open for 6% of the time, Pallas kernels for 1%

profile of v4, /device:TPU:38, one launch (start us, length us, event | category | flops | bytes accessed | tf_op | source)
XLA Modules:
  0.0 142.0 jit_solution(1041329208853689826)
XLA Ops:
  1.7 10.3 %collective-permute-start.2 = (bf16[48,256]{1,0:T(8,128)(2,1)S(1)}, bf16[48,256]{1,0:T(8,128)(2,1)S(1)}, u32[]{:S(2)}, u32[]{:S(2)}) collective-permute-start(bf16[48,256]{1,0:T(8,128)(2,1)S(1)} %convolution_convert_fusion.2), channel_id=1, source_target_pairs={{0,0},{1,1},{2,2},{3,3},{32,4},{33,5},{34,6},{35,7},{64,8},{65,9},... | collective-permute-start | bytes 73736 | tf_op jit(solution)/shard_map/ppermute | solution.py:305
  21.1 2.4 %collective-permute-start.5 = (bf16[48,256]{1,0:T(8,128)(2,1)S(1)}, bf16[48,256]{1,0:T(8,128)(2,1)S(1)}, u32[]{:S(2)}, u32[]{:S(2)}) collective-permute-start(bf16[48,256]{1,0:T(8,128)(2,1)S(1)} %collective-permute-done.2), channel_id=1, source_target_pairs={{0,16},{1,17},{2,18},{3,19},{4,20},{5,21},{6,22},{7,23},{8,24},{9,... | collective-permute-start | bytes 73736 | tf_op jit(solution)/shard_map/ppermute | solution.py:25
  26.5 2.6 %collective-permute-done.1 = bf16[2,1,2,8320]{3,2,0,1:T(2,128)(2,1)S(1)} collective-permute-done((bf16[2,1,2,8320]{3,2,0,1:T(2,128)(2,1)S(1)}, bf16[2,1,2,8320]{3,2,0,1:T(2,128)(2,1)S(1)}, u32[]{:S(2)}, u32[]{:S(2)}) %collective-permute-start.1) | collective-permute-done | bytes 66592 | tf_op jit(solution)/shard_map/ppermute | solution.py:25
  31.0 2.4 %collective-permute-start.9 = (bf16[4,48,256]{2,1,0:T(8,128)(2,1)S(1)}, bf16[4,48,256]{2,1,0:T(8,128)(2,1)S(1)}, u32[]{:S(2)}, u32[]{:S(2)}) collective-permute-start(bf16[4,48,256]{2,1,0:T(8,128)(2,1)S(1)} %bitcast_dynamic-update-slice_fusion.22), channel_id=1, source_target_pairs={{0,4},{1,5},{2,6},{3,7},{4,0},{5,1},{6,2},{7,3},{8,12},{9,13},{10,... | collective-permute-start | bytes 294920 | tf_op jit(solution)/shard_map/ppermute | solution.py:25
  41.1 2.3 %collective-permute-start.13 = (bf16[16,4096]{1,0:T(8,128)(2,1)S(1)}, bf16[16,4096]{1,0:T(8,128)(2,1)S(1)}, u32[]{:S(2)}, u32[]{:S(2)}) collective-permute-start(bf16[16,4096]{1,0:T(8,128)(2,1)S(1)} %slice.389), channel_id=1, source_target_pairs={{0,4},{1,5},{2,6},{3,7},{4,0},{5,1},{6,2},{7,3},{8,12},{9,13},{10,... | collective-permute-start | bytes 393224 | tf_op jit(solution)/shard_map/ppermute | solution.py:25
  49.4 2.4 %collective-permute-start.17 = (bf16[16,4224]{1,0:T(8,128)(2,1)S(1)}, bf16[16,4224]{1,0:T(8,128)(2,1)S(1)}, u32[]{:S(2)}, u32[]{:S(2)}) collective-permute-start(bf16[16,4224]{1,0:T(8,128)(2,1)S(1)} %slice.390), channel_id=1, source_target_pairs={{0,16},{1,17},{2,18},{3,19},{4,20},{5,21},{6,22},{7,23},{8,24},{9,... | collective-permute-start | bytes 405512 | tf_op jit(solution)/shard_map/ppermute | solution.py:25
  56.7 2.6 %collective-permute-start.21 = (bf16[4,16,4224]{2,1,0:T(8,128)(2,1)S(1)}, bf16[4,16,4224]{2,1,0:T(8,128)(2,1)S(1)}, u32[]{:S(2)}, u32[]{:S(2)}) collective-permute-start(bf16[4,16,4224]{2,1,0:T(8,128)(2,1)S(1)} %bitcast_dynamic-update-slice_fusion.10), channel_id=1, source_target_pairs={{0,6},{1,7},{2,0},{3,1},{4,2},{5,3},{6,4},{7,5},{8,14},{9,15},{10,... | collective-permute-start | bytes 1622024 | tf_op jit(solution)/shard_map/ppermute | solution.py:34
  63.0 3.6 %collective-permute-done.22 = bf16[2,2,48,256]{3,2,0,1:T(8,128)(2,1)S(1)} collective-permute-done((bf16[2,2,48,256]{3,2,0,1:T(8,128)(2,1)S(1)}, bf16[2,2,48,256]{3,2,0,1:T(8,128)(2,1)S(1)}, u32[]{:S(2)}, u32[]{:S(2)}) %collective-permute-start.22) | collective-permute-done | bytes 98336 | tf_op jit(solution)/shard_map/ppermute | solution.py:25
  66.7 3.3 %collective-permute-start.23 = (bf16[2,48,256]{2,1,0:T(8,128)(2,1)S(1)}, bf16[2,48,256]{2,1,0:T(8,128)(2,1)S(1)}, u32[]{:S(2)}, u32[]{:S(2)}) collective-permute-start(bf16[2,48,256]{2,1,0:T(8,128)(2,1)S(1)} %fusion.5), channel_id=1, source_target_pairs={{0,64},{1,65},{2,66},{3,67},{4,68},{5,69},{6,70},{7,71},{8,72},{9,... | collective-permute-start | bytes 147464 | tf_op jit(solution)/shard_map/ppermute | solution.py:25
  70.2 2.1 %collective-permute-done.23 = bf16[2,48,256]{2,1,0:T(8,128)(2,1)S(1)} collective-permute-done((bf16[2,48,256]{2,1,0:T(8,128)(2,1)S(1)}, bf16[2,48,256]{2,1,0:T(8,128)(2,1)S(1)}, u32[]{:S(2)}, u32[]{:S(2)}) %collective-permute-start.23) | collective-permute-done | bytes 49184 | tf_op jit(solution)/shard_map/ppermute | solution.py:25
  72.4 4.1 %collective-permute-start.28 = (bf16[144,256]{1,0:T(8,128)(2,1)S(1)}, bf16[144,256]{1,0:T(8,128)(2,1)S(1)}, u32[]{:S(2)}, u32[]{:S(2)}) collective-permute-start(bf16[144,256]{1,0:T(8,128)(2,1)S(1)} %pad_maximum_fusion.7), channel_id=1, source_target_pairs={{0,128},{1,129},{2,130},{3,131},{4,132},{5,133},{6,134},{7,135},{8... | collective-permute-start | bytes 221192 | tf_op jit(solution)/shard_map/ppermute | solution.py:25
  77.2 3.3 %collective-permute-start.24 = (bf16[4,16,2048]{2,1,0:T(8,128)(2,1)S(1)}, bf16[4,16,2048]{2,1,0:T(8,128)(2,1)S(1)}, u32[]{:S(2)}, u32[]{:S(2)}) collective-permute-start(bf16[4,16,2048]{2,1,0:T(8,128)(2,1)S(1)} %slice.399), channel_id=1, source_target_pairs={{0,8},{1,9},{2,10},{3,11},{4,12},{5,13},{6,14},{7,15},{8,16},{9,17... | collective-permute-start | bytes 786440 | tf_op jit(solution)/shard_map/ppermute | solution.py:34
  82.1 2.3 %collective-permute-done.24 = bf16[4,16,2048]{2,1,0:T(8,128)(2,1)S(1)} collective-permute-done((bf16[4,16,2048]{2,1,0:T(8,128)(2,1)S(1)}, bf16[4,16,2048]{2,1,0:T(8,128)(2,1)S(1)}, u32[]{:S(2)}, u32[]{:S(2)}) %collective-permute-start.24) | collective-permute-done | bytes 262176 | tf_op jit(solution)/shard_map/ppermute | solution.py:34
  84.4 3.8 %collective-permute-done.25 = bf16[4,16,2048]{2,1,0:T(8,128)(2,1)S(1)} collective-permute-done((bf16[4,16,2048]{2,1,0:T(8,128)(2,1)S(1)}, bf16[4,16,2048]{2,1,0:T(8,128)(2,1)S(1)}, u32[]{:S(2)}, u32[]{:S(2)}) %collective-permute-start.25) | collective-permute-done | bytes 262176 | tf_op jit(solution)/shard_map/ppermute | solution.py:34
  88.7 6.1 %shard_map.103 = f32[8,256]{1,0:T(8,128)S(1)} custom-call(s32[2]{0:T(128)S(1)} %get-tuple-element.113.first_ref, bf16[256,4096]{1,0:T(8,128)(2,1)S(1)} %bitcast.172, bf16[256,4224]{1,0:T(8,128)(2,1)S(1)} %bitcast.171, bf16[501,8192]{1,0:T(8,128)(2,1)S(1)} %bitcast.176, bf16[501,8192]{1,0:T(8,128)(2,1)} %collective-permute-done.10.two_ref), custom_call_target="tpu_custom_call" | custom-call | flops 4202692608 | bytes 20611072 | tf_op jit(solution)/shard_map/pallas_call | solution.py:147
  94.8 3.0 %collective-permute-start.29 = (bf16[112,256]{1,0:T(8,128)(2,1)S(1)}, bf16[112,256]{1,0:T(8,128)(2,1)S(1)}, u32[]{:S(2)}, u32[]{:S(2)}) collective-permute-start(bf16[112,256]{1,0:T(8,128)(2,1)S(1)} %pad_maximum_fusion.8), channel_id=1, source_target_pairs={{0,32},{1,33},{2,34},{3,35},{4,36},{5,37},{6,38},{7,39},{8,40},{9,... | collective-permute-start | bytes 172040 | tf_op jit(solution)/shard_map/ppermute | solution.py:25
  97.9 2.5 %collective-permute-start.31 = (bf16[112,256]{1,0:T(8,128)(2,1)S(1)}, bf16[112,256]{1,0:T(8,128)(2,1)S(1)}, u32[]{:S(2)}, u32[]{:S(2)}) collective-permute-start(bf16[112,256]{1,0:T(8,128)(2,1)S(1)} %pad_maximum_fusion.8), channel_id=1, source_target_pairs={{0,64},{1,65},{2,66},{3,67},{4,68},{5,69},{6,70},{7,71},{8,72},{9,... | collective-permute-start | bytes 172040 | tf_op jit(solution)/shard_map/ppermute | solution.py:25
  100.4 2.8 %collective-permute-done.31 = bf16[112,256]{1,0:T(8,128)(2,1)S(1)} collective-permute-done((bf16[112,256]{1,0:T(8,128)(2,1)S(1)}, bf16[112,256]{1,0:T(8,128)(2,1)S(1)}, u32[]{:S(2)}, u32[]{:S(2)}) %collective-permute-start.31) | collective-permute-done | bytes 57376 | tf_op jit(solution)/shard_map/ppermute | solution.py:25
  107.5 3.0 %collective-permute-start.35 = (bf16[224,256]{1,0:T(8,128)(2,1)S(1)}, bf16[224,256]{1,0:T(8,128)(2,1)S(1)}, u32[]{:S(2)}, u32[]{:S(2)}) collective-permute-start(bf16[224,256]{1,0:T(8,128)(2,1)S(1)} %get-tuple-element.97), channel_id=1, source_target_pairs={{0,4},{1,5},{2,6},{3,7},{4,0},{5,1},{6,2},{7,3},{8,12},{9,13},{10,... | collective-permute-start | bytes 344072 | tf_op jit(solution)/shard_map/ppermute | solution.py:25
  117.2 2.7 %collective-permute-start.36 = (bf16[80,256]{1,0:T(8,128)(2,1)S(1)}, bf16[80,256]{1,0:T(8,128)(2,1)S(1)}, u32[]{:S(2)}, u32[]{:S(2)}) collective-permute-start(bf16[80,256]{1,0:T(8,128)(2,1)S(1)} %get-tuple-element.92), channel_id=1, source_target_pairs={{0,8},{1,9},{2,10},{3,11},{4,12},{5,13},{6,14},{7,15},{8,0},{9,1},... | collective-permute-start | bytes 122888 | tf_op jit(solution)/shard_map/ppermute | solution.py:25
  121.6 3.5 %collective-permute-done.37 = bf16[80,256]{1,0:T(8,128)(2,1)S(1)} collective-permute-done((bf16[80,256]{1,0:T(8,128)(2,1)S(1)}, bf16[80,256]{1,0:T(8,128)(2,1)S(1)}, u32[]{:S(2)}, u32[]{:S(2)}) %collective-permute-start.37) | collective-permute-done | bytes 40992 | tf_op jit(solution)/shard_map/ppermute | solution.py:25
  125.2 2.7 %collective-permute-start.39 = (f32[10,256]{1,0:T(8,128)S(1)}, f32[10,256]{1,0:T(8,128)S(1)}, u32[]{:S(2)}, u32[]{:S(2)}) collective-permute-start(f32[10,256]{1,0:T(8,128)S(1)} %pad_maximum_fusion.13.mine_ref), channel_id=1, source_target_pairs={{0,128},{1,129},{2,130},{3,131},{4,132},{5,133},{6,134},{7,135},{8... | collective-permute-start | bytes 30728 | tf_op jit(solution)/shard_map/ppermute | solution.py:25
  127.9 6.0 %collective-permute-start.40 = (bf16[48,256]{1,0:T(8,128)(2,1)S(1)}, bf16[48,256]{1,0:T(8,128)(2,1)S(1)}, u32[]{:S(2)}, u32[]{:S(2)}) collective-permute-start(bf16[48,256]{1,0:T(8,128)(2,1)S(1)} %fusion.8), channel_id=1, source_target_pairs={{0,0},{1,1},{2,2},{3,3},{4,32},{5,33},{6,34},{7,35},{8,64},{9,65},... | collective-permute-start | bytes 73736 | tf_op jit(solution)/shard_map/ppermute | solution.py:381
  136.3 4.8 %collective-permute-done.40 = bf16[48,256]{1,0:T(8,128)(2,1)S(1)} collective-permute-done((bf16[48,256]{1,0:T(8,128)(2,1)S(1)}, bf16[48,256]{1,0:T(8,128)(2,1)S(1)}, u32[]{:S(2)}, u32[]{:S(2)}) %collective-permute-start.40) | collective-permute-done | bytes 24608 | tf_op jit(solution)/shard_map/ppermute | solution.py:381
  (220 shorter events, 55.5 us)
Async XLA Ops:
  1.7 17.7 %collective-permute-start.2 = (bf16[48,256]{1,0:T(8,128)(2,1)S(1)}, bf16[48,256]{1,0:T(8,128)(2,1)S(1)}, u32[]{:S(2)}, u32[]{:S(2)}) collective-permute-start(bf16[48,256]{1,0:T(8,128)(2,1)S(1)} %convolution_convert_fusion.2), channel_id=1, source_target_pairs={{0,0},{1,1},{2,2},{3,3},{32,4},{33,5},{34,6},{35,7},{64,8},{65,9},... | collective-permute-start | bytes 73736 | tf_op jit(solution)/shard_map/ppermute | solution.py:305
  12.0 27.2 %collective-permute-start.10 = (bf16[501,8192]{1,0:T(8,128)(2,1)}, bf16[501,8192]{1,0:T(8,128)(2,1)}, u32[]{:S(2)}, u32[]{:S(2)}) collective-permute-start(bf16[501,8192]{1,0:T(8,128)(2,1)} %bitcast.173), channel_id=1, source_target_pairs={{0,1},{1,0},{2,3},{3,2},{4,5},{5,4},{6,7},{7,6},{8,9},{9,8},{10,11... | collective-permute-start | bytes 24625160 | tf_op jit(solution)/shard_map/ppermute | solution.py:25
  13.7 9.8 %collective-permute-start = (bf16[1,2,8320]{2,1,0:T(2,128)(2,1)S(1)}, bf16[1,2,8320]{2,1,0:T(2,128)(2,1)S(1)}, u32[]{:S(2)}, u32[]{:S(2)}) collective-permute-start(bf16[1,2,8320]{2,1,0:T(2,128)(2,1)S(1)} %get-tuple-element.85), channel_id=1, source_target_pairs={{0,128},{1,129},{2,130},{3,131},{4,132},{5,133},{6,134},{7,135},{8... | collective-permute-start | bytes 99848 | tf_op jit(solution)/shard_map/ppermute | solution.py:25
  19.3 6.2 %collective-permute-start.3 = (bf16[48,256]{1,0:T(8,128)(2,1)S(1)}, bf16[48,256]{1,0:T(8,128)(2,1)S(1)}, u32[]{:S(2)}, u32[]{:S(2)}) collective-permute-start(bf16[48,256]{1,0:T(8,128)(2,1)S(1)} %collective-permute-done.2), channel_id=1, source_target_pairs={{0,8},{1,9},{2,10},{3,11},{4,12},{5,13},{6,14},{7,15},{8,0},{9,1},... | collective-permute-start | bytes 73736 | tf_op jit(solution)/shard_map/ppermute | solution.py:25
  31.0 6.1 %collective-permute-start.9 = (bf16[4,48,256]{2,1,0:T(8,128)(2,1)S(1)}, bf16[4,48,256]{2,1,0:T(8,128)(2,1)S(1)}, u32[]{:S(2)}, u32[]{:S(2)}) collective-permute-start(bf16[4,48,256]{2,1,0:T(8,128)(2,1)S(1)} %bitcast_dynamic-update-slice_fusion.22), channel_id=1, source_target_pairs={{0,4},{1,5},{2,6},{3,7},{4,0},{5,1},{6,2},{7,3},{8,12},{9,13},{10,... | collective-permute-start | bytes 294920 | tf_op jit(solution)/shard_map/ppermute | solution.py:25
  39.9 6.2 %collective-permute-start.12 = (bf16[16,4096]{1,0:T(8,128)(2,1)S(1)}, bf16[16,4096]{1,0:T(8,128)(2,1)S(1)}, u32[]{:S(2)}, u32[]{:S(2)}) collective-permute-start(bf16[16,4096]{1,0:T(8,128)(2,1)S(1)} %slice.389), channel_id=1, source_target_pairs={{0,6},{1,7},{2,4},{3,5},{4,2},{5,3},{6,0},{7,1},{8,14},{9,15},{10,... | collective-permute-start | bytes 393224 | tf_op jit(solution)/shard_map/ppermute | solution.py:25
  41.1 6.5 %collective-permute-start.13 = (bf16[16,4096]{1,0:T(8,128)(2,1)S(1)}, bf16[16,4096]{1,0:T(8,128)(2,1)S(1)}, u32[]{:S(2)}, u32[]{:S(2)}) collective-permute-start(bf16[16,4096]{1,0:T(8,128)(2,1)S(1)} %slice.389), channel_id=1, source_target_pairs={{0,4},{1,5},{2,6},{3,7},{4,0},{5,1},{6,2},{7,3},{8,12},{9,13},{10,... | collective-permute-start | bytes 393224 | tf_op jit(solution)/shard_map/ppermute | solution.py:25
  48.3 6.2 %collective-permute-start.16 = (bf16[16,4224]{1,0:T(8,128)(2,1)S(1)}, bf16[16,4224]{1,0:T(8,128)(2,1)S(1)}, u32[]{:S(2)}, u32[]{:S(2)}) collective-permute-start(bf16[16,4224]{1,0:T(8,128)(2,1)S(1)} %slice.390), channel_id=1, source_target_pairs={{0,24},{1,25},{2,26},{3,27},{4,28},{5,29},{6,30},{7,31},{8,16},{9,... | collective-permute-start | bytes 405512 | tf_op jit(solution)/shard_map/ppermute | solution.py:25
  49.4 6.6 %collective-permute-start.17 = (bf16[16,4224]{1,0:T(8,128)(2,1)S(1)}, bf16[16,4224]{1,0:T(8,128)(2,1)S(1)}, u32[]{:S(2)}, u32[]{:S(2)}) collective-permute-start(bf16[16,4224]{1,0:T(8,128)(2,1)S(1)} %slice.390), channel_id=1, source_target_pairs={{0,16},{1,17},{2,18},{3,19},{4,20},{5,21},{6,22},{7,23},{8,24},{9,... | collective-permute-start | bytes 405512 | tf_op jit(solution)/shard_map/ppermute | solution.py:25
  56.0 16.4 %collective-permute-start.20 = (bf16[4,16,4224]{2,1,0:T(8,128)(2,1)S(1)}, bf16[4,16,4224]{2,1,0:T(8,128)(2,1)S(1)}, u32[]{:S(2)}, u32[]{:S(2)}) collective-permute-start(bf16[4,16,4224]{2,1,0:T(8,128)(2,1)S(1)} %bitcast_dynamic-update-slice_fusion.10), channel_id=1, source_target_pairs={{0,2},{1,3},{2,4},{3,5},{4,6},{5,7},{6,0},{7,1},{8,10},{9,11},{10,... | collective-permute-start | bytes 1622024 | tf_op jit(solution)/shard_map/ppermute | solution.py:34
  56.7 15.7 %collective-permute-start.21 = (bf16[4,16,4224]{2,1,0:T(8,128)(2,1)S(1)}, bf16[4,16,4224]{2,1,0:T(8,128)(2,1)S(1)}, u32[]{:S(2)}, u32[]{:S(2)}) collective-permute-start(bf16[4,16,4224]{2,1,0:T(8,128)(2,1)S(1)} %bitcast_dynamic-update-slice_fusion.10), channel_id=1, source_target_pairs={{0,6},{1,7},{2,0},{3,1},{4,2},{5,3},{6,4},{7,5},{8,14},{9,15},{10,... | collective-permute-start | bytes 1622024 | tf_op jit(solution)/shard_map/ppermute | solution.py:34
  59.3 13.1 %collective-permute-start.18 = (bf16[4,16,4096]{2,1,0:T(8,128)(2,1)S(1)}, bf16[4,16,4096]{2,1,0:T(8,128)(2,1)S(1)}, u32[]{:S(2)}, u32[]{:S(2)}) collective-permute-start(bf16[4,16,4096]{2,1,0:T(8,128)(2,1)S(1)} %bitcast_dynamic-update-slice_fusion.14), channel_id=1, source_target_pairs={{0,8},{1,9},{2,10},{3,11},{4,12},{5,13},{6,14},{7,15},{8,16},{9,17... | collective-permute-start | bytes 1572872 | tf_op jit(solution)/shard_map/ppermute | solution.py:34
  61.4 11.0 %collective-permute-start.19 = (bf16[4,16,4096]{2,1,0:T(8,128)(2,1)S(1)}, bf16[4,16,4096]{2,1,0:T(8,128)(2,1)S(1)}, u32[]{:S(2)}, u32[]{:S(2)}) collective-permute-start(bf16[4,16,4096]{2,1,0:T(8,128)(2,1)S(1)} %bitcast_dynamic-update-slice_fusion.14), channel_id=1, source_target_pairs={{0,24},{1,25},{2,26},{3,27},{4,28},{5,29},{6,30},{7,31},{8,0},{9,1... | collective-permute-start | bytes 1572872 | tf_op jit(solution)/shard_map/ppermute | solution.py:34
  72.4 9.6 %collective-permute-start.28 = (bf16[144,256]{1,0:T(8,128)(2,1)S(1)}, bf16[144,256]{1,0:T(8,128)(2,1)S(1)}, u32[]{:S(2)}, u32[]{:S(2)}) collective-permute-start(bf16[144,256]{1,0:T(8,128)(2,1)S(1)} %pad_maximum_fusion.7), channel_id=1, source_target_pairs={{0,128},{1,129},{2,130},{3,131},{4,132},{5,133},{6,134},{7,135},{8... | collective-permute-start | bytes 221192 | tf_op jit(solution)/shard_map/ppermute | solution.py:25
  76.6 11.9 %collective-permute-start.27 = (bf16[4,16,2176]{2,1,0:T(8,128)(2,1)S(1)}, bf16[4,16,2176]{2,1,0:T(8,128)(2,1)S(1)}, u32[]{:S(2)}, u32[]{:S(2)}) collective-permute-start(bf16[4,16,2176]{2,1,0:T(8,128)(2,1)S(1)} %slice.402), channel_id=1, source_target_pairs={{0,6},{1,7},{2,0},{3,1},{4,2},{5,3},{6,4},{7,5},{8,14},{9,15},{10,... | collective-permute-start | bytes 835592 | tf_op jit(solution)/shard_map/ppermute | solution.py:34
  77.2 7.2 %collective-permute-start.24 = (bf16[4,16,2048]{2,1,0:T(8,128)(2,1)S(1)}, bf16[4,16,2048]{2,1,0:T(8,128)(2,1)S(1)}, u32[]{:S(2)}, u32[]{:S(2)}) collective-permute-start(bf16[4,16,2048]{2,1,0:T(8,128)(2,1)S(1)} %slice.399), channel_id=1, source_target_pairs={{0,8},{1,9},{2,10},{3,11},{4,12},{5,13},{6,14},{7,15},{8,16},{9,17... | collective-permute-start | bytes 786440 | tf_op jit(solution)/shard_map/ppermute | solution.py:34
  80.5 7.7 %collective-permute-start.25 = (bf16[4,16,2048]{2,1,0:T(8,128)(2,1)S(1)}, bf16[4,16,2048]{2,1,0:T(8,128)(2,1)S(1)}, u32[]{:S(2)}, u32[]{:S(2)}) collective-permute-start(bf16[4,16,2048]{2,1,0:T(8,128)(2,1)S(1)} %slice.400), channel_id=1, source_target_pairs={{0,24},{1,25},{2,26},{3,27},{4,28},{5,29},{6,30},{7,31},{8,0},{9,1... | collective-permute-start | bytes 786440 | tf_op jit(solution)/shard_map/ppermute | solution.py:34
  80.6 7.9 %collective-permute-start.26 = (bf16[4,16,2048]{2,1,0:T(8,128)(2,1)S(1)}, bf16[4,16,2048]{2,1,0:T(8,128)(2,1)S(1)}, u32[]{:S(2)}, u32[]{:S(2)}) collective-permute-start(bf16[4,16,2048]{2,1,0:T(8,128)(2,1)S(1)} %slice.401), channel_id=1, source_target_pairs={{0,2},{1,3},{2,4},{3,5},{4,6},{5,7},{6,0},{7,1},{8,10},{9,11},{10,... | collective-permute-start | bytes 786440 | tf_op jit(solution)/shard_map/ppermute | solution.py:34
  94.8 8.5 %collective-permute-start.29 = (bf16[112,256]{1,0:T(8,128)(2,1)S(1)}, bf16[112,256]{1,0:T(8,128)(2,1)S(1)}, u32[]{:S(2)}, u32[]{:S(2)}) collective-permute-start(bf16[112,256]{1,0:T(8,128)(2,1)S(1)} %pad_maximum_fusion.8), channel_id=1, source_target_pairs={{0,32},{1,33},{2,34},{3,35},{4,36},{5,37},{6,38},{7,39},{8,40},{9,... | collective-permute-start | bytes 172040 | tf_op jit(solution)/shard_map/ppermute | solution.py:25
  107.2 8.6 %collective-permute-start.34 = (bf16[224,256]{1,0:T(8,128)(2,1)S(1)}, bf16[224,256]{1,0:T(8,128)(2,1)S(1)}, u32[]{:S(2)}, u32[]{:S(2)}) collective-permute-start(bf16[224,256]{1,0:T(8,128)(2,1)S(1)} %get-tuple-element.96), channel_id=1, source_target_pairs={{0,6},{1,7},{2,4},{3,5},{4,2},{5,3},{6,0},{7,1},{8,14},{9,15},{10,... | collective-permute-start | bytes 344072 | tf_op jit(solution)/shard_map/ppermute | solution.py:25
  107.5 6.4 %collective-permute-start.35 = (bf16[224,256]{1,0:T(8,128)(2,1)S(1)}, bf16[224,256]{1,0:T(8,128)(2,1)S(1)}, u32[]{:S(2)}, u32[]{:S(2)}) collective-permute-start(bf16[224,256]{1,0:T(8,128)(2,1)S(1)} %get-tuple-element.97), channel_id=1, source_target_pairs={{0,4},{1,5},{2,6},{3,7},{4,0},{5,1},{6,2},{7,3},{8,12},{9,13},{10,... | collective-permute-start | bytes 344072 | tf_op jit(solution)/shard_map/ppermute | solution.py:25
  117.2 7.9 %collective-permute-start.36 = (bf16[80,256]{1,0:T(8,128)(2,1)S(1)}, bf16[80,256]{1,0:T(8,128)(2,1)S(1)}, u32[]{:S(2)}, u32[]{:S(2)}) collective-permute-start(bf16[80,256]{1,0:T(8,128)(2,1)S(1)} %get-tuple-element.92), channel_id=1, source_target_pairs={{0,8},{1,9},{2,10},{3,11},{4,12},{5,13},{6,14},{7,15},{8,0},{9,1},... | collective-permute-start | bytes 122888 | tf_op jit(solution)/shard_map/ppermute | solution.py:25
  125.2 8.7 %collective-permute-start.39 = (f32[10,256]{1,0:T(8,128)S(1)}, f32[10,256]{1,0:T(8,128)S(1)}, u32[]{:S(2)}, u32[]{:S(2)}) collective-permute-start(f32[10,256]{1,0:T(8,128)S(1)} %pad_maximum_fusion.13.mine_ref), channel_id=1, source_target_pairs={{0,128},{1,129},{2,130},{3,131},{4,132},{5,133},{6,134},{7,135},{8... | collective-permute-start | bytes 30728 | tf_op jit(solution)/shard_map/ppermute | solution.py:25
  127.9 13.2 %collective-permute-start.40 = (bf16[48,256]{1,0:T(8,128)(2,1)S(1)}, bf16[48,256]{1,0:T(8,128)(2,1)S(1)}, u32[]{:S(2)}, u32[]{:S(2)}) collective-permute-start(bf16[48,256]{1,0:T(8,128)(2,1)S(1)} %fusion.8), channel_id=1, source_target_pairs={{0,0},{1,1},{2,2},{3,3},{4,32},{5,33},{6,34},{7,35},{8,64},{9,65},... | collective-permute-start | bytes 73736 | tf_op jit(solution)/shard_map/ppermute | solution.py:381
  (22 other events, 250.0 us)

commit v5 on v4

--- a/solution.py
+++ b/solution.py
@@ -95,32 +95,20 @@
     return [(j, i) for i, j in pairs] if back else pairs
 
 
-def logits_kernel(first_ref, p_ref, q_ref, one_ref, two_ref, out_ref, buf, sems):
+def logits_kernel(first_ref, p_ref, q_ref, one_ref, two_ref, out_ref):
     half = p_ref.shape[1]
-    kb = buf.shape[2]
-    steps = buf.shape[0]
     dims = (((1,), (1,)), ((), ()))
-    copies = [
-        pltpu.make_async_copy(two_ref.at[:, pl.ds(j * kb, kb)], buf.at[j], sems.at[j])
-        for j in range(steps)
-    ]
-    for copy in copies:
-        copy.start()
-
-    one = lax.dot_general(
-        p_ref[...], one_ref[:, :half], dims, preferred_element_type=F32
-    ) + lax.dot_general(q_ref[:, :half], one_ref[:, half:], dims, preferred_element_type=F32)
-    n = steps // 2
-    two = jnp.zeros(one.shape, F32)
-    for j, copy in enumerate(copies):
-        copy.wait()
-        a_ref = p_ref if j < n else q_ref
-        two += lax.dot_general(
-            a_ref[:, (j % n) * kb : (j % n + 1) * kb], buf[j], dims, preferred_element_type=F32
+
+    def logits(w_ref):
+        return lax.dot_general(
+            p_ref[...], w_ref[:, :half], dims, preferred_element_type=F32
+        ) + lax.dot_general(
+            q_ref[:, :half], w_ref[:, half:], dims, preferred_element_type=F32
         )
 
     meta = q_ref[:, half:].astype(F32)
     label = (meta[:, 0:1] * 65536.0 + meta[:, 1:2] * 256.0 + meta[:, 2:3]).astype(jnp.int32)
+    two, one = logits(two_ref), logits(one_ref)
     top = jnp.maximum(jnp.max(one, axis=1, keepdims=True), jnp.max(two, axis=1, keepdims=True))
     total = jnp.sum(jnp.exp(one - top), axis=1, keepdims=True) + jnp.sum(
         jnp.exp(two - top), axis=1, keepdims=True
@@ -142,23 +130,12 @@
 def local_stats(p, q, head, other_head, first):
     voc, d = head.shape
     rows = p.shape[0]
-    steps = 4
-    vmem = pl.BlockSpec(memory_space=pltpu.VMEM)
     return pl.pallas_call(
         logits_kernel,
         out_shape=jax.ShapeDtypeStruct((8, rows), F32),
-        in_specs=[
-            pl.BlockSpec(memory_space=pltpu.SMEM),
-            vmem,
-            vmem,
-            vmem,
-            pl.BlockSpec(memory_space=pl.ANY),
-        ],
-        out_specs=vmem,
-        scratch_shapes=[
-            pltpu.VMEM((steps, voc, d // steps), BF),
-            pltpu.SemaphoreType.DMA((steps,)),
-        ],
+        in_specs=[pl.BlockSpec(memory_space=pltpu.SMEM)]
+        + [pl.BlockSpec(memory_space=pltpu.VMEM)] * 4,
+        out_specs=pl.BlockSpec(memory_space=pltpu.VMEM),
         compiler_params=pltpu.CompilerParams(vmem_limit_bytes=20 * 1024 * 1024),
         cost_estimate=pl.CostEstimate(
             flops=4 * rows * d * voc,

time: 142 us -> 145 us (1.021)
  Pallas kernels: 7.85 us -> 10.1 us
    pallas_call x1, Pallas kernels: 6.09 us -> 8.33 us  [local_stats(): pl.pallas_call(logits_kernel, out_shape=jax.ShapeDtypeStruct((8, rows), F...]
where the time goes in v5:
time: 145 us; the launch traced here: 144 us
  starting transfers between devices  73.2 us (50%)
  waiting for transfers between devices  46.8 us (32%)
  Pallas kernels  10.1 us (7%)
  other arithmetic  4.36 us (3%)
  local copies, waits for them, and re-layouts  4.12 us (3%)
  matrix products  3.65 us (3%)
  between operations  2.06 us (1%)
    ppermute x31, starting transfers between devices, ex(): return lax.ppermute(a, AXES, [(i, i ^ m) for i in range(256)])  46.4 us
    ppermute x31, waiting for transfers between devices, ex(): return lax.ppermute(a, AXES, [(i, i ^ m) for i in range(256)])  35.6 us
    ppermute x8, starting transfers between devices, shift(): return lax.ppermute(a, AXES, pairs)  10.5 us
    ppermute x1, starting transfers between devices, on_device(): xs = lax.ppermute(inputs, AXES, plane_pairs(False))  10.3 us
    pallas_call x1, Pallas kernels, local_stats(): pl.pallas_call(logits_kernel, out_shape=jax.ShapeDtypeStruct((8, rows), F...  8.33 us
    ppermute x8, waiting for transfers between devices, shift(): return lax.ppermute(a, AXES, pairs)  6.4 us
    ppermute x1, starting transfers between devices, on_device(): back = lax.ppermute(back.astype(BF), AXES, plane_pairs(True))  5.98 us
    ppermute x1, waiting for transfers between devices, on_device(): back = lax.ppermute(back.astype(BF), AXES, plane_pairs(True))  4.78 us
  transfers between devices with their start and end apart: 41, of which 26 were waited for; matrix products, arithmetic and copies ran while one was open for 6% of the time, Pallas kernels for 1%

profile of v5, /device:TPU:38, one launch (start us, length us, event | category | flops | bytes accessed | tf_op | source)
XLA Modules:
  0.0 144.3 jit_solution(15241720117710857357)
XLA Ops:
  1.7 10.3 %collective-permute-start.2 = (bf16[48,256]{1,0:T(8,128)(2,1)S(1)}, bf16[48,256]{1,0:T(8,128)(2,1)S(1)}, u32[]{:S(2)}, u32[]{:S(2)}) collective-permute-start(bf16[48,256]{1,0:T(8,128)(2,1)S(1)} %convolution_convert_fusion.2), channel_id=1, source_target_pairs={{0,0},{1,1},{2,2},{3,3},{32,4},{33,5},{34,6},{35,7},{64,8},{65,9},... | collective-permute-start | bytes 73736 | tf_op jit(solution)/shard_map/ppermute | solution.py:282
  21.1 2.4 %collective-permute-start.5 = (bf16[48,256]{1,0:T(8,128)(2,1)S(1)}, bf16[48,256]{1,0:T(8,128)(2,1)S(1)}, u32[]{:S(2)}, u32[]{:S(2)}) collective-permute-start(bf16[48,256]{1,0:T(8,128)(2,1)S(1)} %collective-permute-done.2), channel_id=1, source_target_pairs={{0,16},{1,17},{2,18},{3,19},{4,20},{5,21},{6,22},{7,23},{8,24},{9,... | collective-permute-start | bytes 73736 | tf_op jit(solution)/shard_map/ppermute | solution.py:25
  26.5 2.6 %collective-permute-done.1 = bf16[2,1,2,8320]{3,2,0,1:T(2,128)(2,1)S(1)} collective-permute-done((bf16[2,1,2,8320]{3,2,0,1:T(2,128)(2,1)S(1)}, bf16[2,1,2,8320]{3,2,0,1:T(2,128)(2,1)S(1)}, u32[]{:S(2)}, u32[]{:S(2)}) %collective-permute-start.1) | collective-permute-done | bytes 66592 | tf_op jit(solution)/shard_map/ppermute | solution.py:25
  31.0 2.4 %collective-permute-start.9 = (bf16[4,48,256]{2,1,0:T(8,128)(2,1)S(1)}, bf16[4,48,256]{2,1,0:T(8,128)(2,1)S(1)}, u32[]{:S(2)}, u32[]{:S(2)}) collective-permute-start(bf16[4,48,256]{2,1,0:T(8,128)(2,1)S(1)} %bitcast_dynamic-update-slice_fusion.22), channel_id=1, source_target_pairs={{0,4},{1,5},{2,6},{3,7},{4,0},{5,1},{6,2},{7,3},{8,12},{9,13},{10,... | collective-permute-start | bytes 294920 | tf_op jit(solution)/shard_map/ppermute | solution.py:25
  41.1 2.3 %collective-permute-start.13 = (bf16[16,4096]{1,0:T(8,128)(2,1)S(1)}, bf16[16,4096]{1,0:T(8,128)(2,1)S(1)}, u32[]{:S(2)}, u32[]{:S(2)}) collective-permute-start(bf16[16,4096]{1,0:T(8,128)(2,1)S(1)} %slice.389), channel_id=1, source_target_pairs={{0,4},{1,5},{2,6},{3,7},{4,0},{5,1},{6,2},{7,3},{8,12},{9,13},{10,... | collective-permute-start | bytes 393224 | tf_op jit(solution)/shard_map/ppermute | solution.py:25
  49.4 2.4 %collective-permute-start.17 = (bf16[16,4224]{1,0:T(8,128)(2,1)S(1)}, bf16[16,4224]{1,0:T(8,128)(2,1)S(1)}, u32[]{:S(2)}, u32[]{:S(2)}) collective-permute-start(bf16[16,4224]{1,0:T(8,128)(2,1)S(1)} %slice.390), channel_id=1, source_target_pairs={{0,16},{1,17},{2,18},{3,19},{4,20},{5,21},{6,22},{7,23},{8,24},{9,... | collective-permute-start | bytes 405512 | tf_op jit(solution)/shard_map/ppermute | solution.py:25
  56.7 2.6 %collective-permute-start.21 = (bf16[4,16,4224]{2,1,0:T(8,128)(2,1)S(1)}, bf16[4,16,4224]{2,1,0:T(8,128)(2,1)S(1)}, u32[]{:S(2)}, u32[]{:S(2)}) collective-permute-start(bf16[4,16,4224]{2,1,0:T(8,128)(2,1)S(1)} %bitcast_dynamic-update-slice_fusion.10), channel_id=1, source_target_pairs={{0,6},{1,7},{2,0},{3,1},{4,2},{5,3},{6,4},{7,5},{8,14},{9,15},{10,... | collective-permute-start | bytes 1622024 | tf_op jit(solution)/shard_map/ppermute | solution.py:34
  63.0 3.6 %collective-permute-done.22 = bf16[2,2,48,256]{3,2,0,1:T(8,128)(2,1)S(1)} collective-permute-done((bf16[2,2,48,256]{3,2,0,1:T(8,128)(2,1)S(1)}, bf16[2,2,48,256]{3,2,0,1:T(8,128)(2,1)S(1)}, u32[]{:S(2)}, u32[]{:S(2)}) %collective-permute-start.22) | collective-permute-done | bytes 98336 | tf_op jit(solution)/shard_map/ppermute | solution.py:25
  66.7 3.3 %collective-permute-start.23 = (bf16[2,48,256]{2,1,0:T(8,128)(2,1)S(1)}, bf16[2,48,256]{2,1,0:T(8,128)(2,1)S(1)}, u32[]{:S(2)}, u32[]{:S(2)}) collective-permute-start(bf16[2,48,256]{2,1,0:T(8,128)(2,1)S(1)} %fusion.5), channel_id=1, source_target_pairs={{0,64},{1,65},{2,66},{3,67},{4,68},{5,69},{6,70},{7,71},{8,72},{9,... | collective-permute-start | bytes 147464 | tf_op jit(solution)/shard_map/ppermute | solution.py:25
  70.2 2.1 %collective-permute-done.23 = bf16[2,48,256]{2,1,0:T(8,128)(2,1)S(1)} collective-permute-done((bf16[2,48,256]{2,1,0:T(8,128)(2,1)S(1)}, bf16[2,48,256]{2,1,0:T(8,128)(2,1)S(1)}, u32[]{:S(2)}, u32[]{:S(2)}) %collective-permute-start.23) | collective-permute-done | bytes 49184 | tf_op jit(solution)/shard_map/ppermute | solution.py:25
  72.4 4.1 %collective-permute-start.28 = (bf16[144,256]{1,0:T(8,128)(2,1)S(1)}, bf16[144,256]{1,0:T(8,128)(2,1)S(1)}, u32[]{:S(2)}, u32[]{:S(2)}) collective-permute-start(bf16[144,256]{1,0:T(8,128)(2,1)S(1)} %pad_maximum_fusion.7), channel_id=1, source_target_pairs={{0,128},{1,129},{2,130},{3,131},{4,132},{5,133},{6,134},{7,135},{8... | collective-permute-start | bytes 221192 | tf_op jit(solution)/shard_map/ppermute | solution.py:25
  77.2 3.3 %collective-permute-start.24 = (bf16[4,16,2048]{2,1,0:T(8,128)(2,1)S(1)}, bf16[4,16,2048]{2,1,0:T(8,128)(2,1)S(1)}, u32[]{:S(2)}, u32[]{:S(2)}) collective-permute-start(bf16[4,16,2048]{2,1,0:T(8,128)(2,1)S(1)} %slice.399), channel_id=1, source_target_pairs={{0,8},{1,9},{2,10},{3,11},{4,12},{5,13},{6,14},{7,15},{8,16},{9,17... | collective-permute-start | bytes 786440 | tf_op jit(solution)/shard_map/ppermute | solution.py:34
  82.1 2.3 %collective-permute-done.24 = bf16[4,16,2048]{2,1,0:T(8,128)(2,1)S(1)} collective-permute-done((bf16[4,16,2048]{2,1,0:T(8,128)(2,1)S(1)}, bf16[4,16,2048]{2,1,0:T(8,128)(2,1)S(1)}, u32[]{:S(2)}, u32[]{:S(2)}) %collective-permute-start.24) | collective-permute-done | bytes 262176 | tf_op jit(solution)/shard_map/ppermute | solution.py:34
  84.4 3.8 %collective-permute-done.25 = bf16[4,16,2048]{2,1,0:T(8,128)(2,1)S(1)} collective-permute-done((bf16[4,16,2048]{2,1,0:T(8,128)(2,1)S(1)}, bf16[4,16,2048]{2,1,0:T(8,128)(2,1)S(1)}, u32[]{:S(2)}, u32[]{:S(2)}) %collective-permute-start.25) | collective-permute-done | bytes 262176 | tf_op jit(solution)/shard_map/ppermute | solution.py:34
  88.7 8.3 %shard_map.103 = f32[8,256]{1,0:T(8,128)S(1)} custom-call(s32[2]{0:T(128)S(1)} %get-tuple-element.113.first_ref, bf16[256,4096]{1,0:T(8,128)(2,1)S(1)} %bitcast.172, bf16[256,4224]{1,0:T(8,128)(2,1)S(1)} %bitcast.171, bf16[501,8192]{1,0:T(8,128)(2,1)S(1)} %bitcast.176, bf16[501,8192]{1,0:T(8,128)(2,1)} %collective-permute-done.10.two_ref), custom_call_target="tpu_custom_call" | custom-call | flops 4202692608 | bytes 20611072 | tf_op jit(solution)/shard_map/pallas_call | solution.py:133
  97.1 3.0 %collective-permute-start.29 = (bf16[112,256]{1,0:T(8,128)(2,1)S(1)}, bf16[112,256]{1,0:T(8,128)(2,1)S(1)}, u32[]{:S(2)}, u32[]{:S(2)}) collective-permute-start(bf16[112,256]{1,0:T(8,128)(2,1)S(1)} %pad_maximum_fusion.8), channel_id=1, source_target_pairs={{0,32},{1,33},{2,34},{3,35},{4,36},{5,37},{6,38},{7,39},{8,40},{9,... | collective-permute-start | bytes 172040 | tf_op jit(solution)/shard_map/ppermute | solution.py:25
  100.1 2.5 %collective-permute-start.31 = (bf16[112,256]{1,0:T(8,128)(2,1)S(1)}, bf16[112,256]{1,0:T(8,128)(2,1)S(1)}, u32[]{:S(2)}, u32[]{:S(2)}) collective-permute-start(bf16[112,256]{1,0:T(8,128)(2,1)S(1)} %pad_maximum_fusion.8), channel_id=1, source_target_pairs={{0,64},{1,65},{2,66},{3,67},{4,68},{5,69},{6,70},{7,71},{8,72},{9,... | collective-permute-start | bytes 172040 | tf_op jit(solution)/shard_map/ppermute | solution.py:25
  102.6 2.8 %collective-permute-done.31 = bf16[112,256]{1,0:T(8,128)(2,1)S(1)} collective-permute-done((bf16[112,256]{1,0:T(8,128)(2,1)S(1)}, bf16[112,256]{1,0:T(8,128)(2,1)S(1)}, u32[]{:S(2)}, u32[]{:S(2)}) %collective-permute-start.31) | collective-permute-done | bytes 57376 | tf_op jit(solution)/shard_map/ppermute | solution.py:25
  109.7 3.0 %collective-permute-start.35 = (bf16[224,256]{1,0:T(8,128)(2,1)S(1)}, bf16[224,256]{1,0:T(8,128)(2,1)S(1)}, u32[]{:S(2)}, u32[]{:S(2)}) collective-permute-start(bf16[224,256]{1,0:T(8,128)(2,1)S(1)} %get-tuple-element.97), channel_id=1, source_target_pairs={{0,4},{1,5},{2,6},{3,7},{4,0},{5,1},{6,2},{7,3},{8,12},{9,13},{10,... | collective-permute-start | bytes 344072 | tf_op jit(solution)/shard_map/ppermute | solution.py:25
  119.4 2.7 %collective-permute-start.36 = (bf16[80,256]{1,0:T(8,128)(2,1)S(1)}, bf16[80,256]{1,0:T(8,128)(2,1)S(1)}, u32[]{:S(2)}, u32[]{:S(2)}) collective-permute-start(bf16[80,256]{1,0:T(8,128)(2,1)S(1)} %get-tuple-element.92), channel_id=1, source_target_pairs={{0,8},{1,9},{2,10},{3,11},{4,12},{5,13},{6,14},{7,15},{8,0},{9,1},... | collective-permute-start | bytes 122888 | tf_op jit(solution)/shard_map/ppermute | solution.py:25
  123.8 3.5 %collective-permute-done.37 = bf16[80,256]{1,0:T(8,128)(2,1)S(1)} collective-permute-done((bf16[80,256]{1,0:T(8,128)(2,1)S(1)}, bf16[80,256]{1,0:T(8,128)(2,1)S(1)}, u32[]{:S(2)}, u32[]{:S(2)}) %collective-permute-start.37) | collective-permute-done | bytes 40992 | tf_op jit(solution)/shard_map/ppermute | solution.py:25
  127.4 2.7 %collective-permute-start.39 = (f32[10,256]{1,0:T(8,128)S(1)}, f32[10,256]{1,0:T(8,128)S(1)}, u32[]{:S(2)}, u32[]{:S(2)}) collective-permute-start(f32[10,256]{1,0:T(8,128)S(1)} %pad_maximum_fusion.13.mine_ref), channel_id=1, source_target_pairs={{0,128},{1,129},{2,130},{3,131},{4,132},{5,133},{6,134},{7,135},{8... | collective-permute-start | bytes 30728 | tf_op jit(solution)/shard_map/ppermute | solution.py:25
  130.1 6.0 %collective-permute-start.40 = (bf16[48,256]{1,0:T(8,128)(2,1)S(1)}, bf16[48,256]{1,0:T(8,128)(2,1)S(1)}, u32[]{:S(2)}, u32[]{:S(2)}) collective-permute-start(bf16[48,256]{1,0:T(8,128)(2,1)S(1)} %fusion.8), channel_id=1, source_target_pairs={{0,0},{1,1},{2,2},{3,3},{4,32},{5,33},{6,34},{7,35},{8,64},{9,65},... | collective-permute-start | bytes 73736 | tf_op jit(solution)/shard_map/ppermute | solution.py:358
  138.6 4.8 %collective-permute-done.40 = bf16[48,256]{1,0:T(8,128)(2,1)S(1)} collective-permute-done((bf16[48,256]{1,0:T(8,128)(2,1)S(1)}, bf16[48,256]{1,0:T(8,128)(2,1)S(1)}, u32[]{:S(2)}, u32[]{:S(2)}) %collective-permute-start.40) | collective-permute-done | bytes 24608 | tf_op jit(solution)/shard_map/ppermute | solution.py:358
  (220 shorter events, 55.5 us)
Async XLA Ops:
  1.7 17.7 %collective-permute-start.2 = (bf16[48,256]{1,0:T(8,128)(2,1)S(1)}, bf16[48,256]{1,0:T(8,128)(2,1)S(1)}, u32[]{:S(2)}, u32[]{:S(2)}) collective-permute-start(bf16[48,256]{1,0:T(8,128)(2,1)S(1)} %convolution_convert_fusion.2), channel_id=1, source_target_pairs={{0,0},{1,1},{2,2},{3,3},{32,4},{33,5},{34,6},{35,7},{64,8},{65,9},... | collective-permute-start | bytes 73736 | tf_op jit(solution)/shard_map/ppermute | solution.py:282
  12.0 27.2 %collective-permute-start.10 = (bf16[501,8192]{1,0:T(8,128)(2,1)}, bf16[501,8192]{1,0:T(8,128)(2,1)}, u32[]{:S(2)}, u32[]{:S(2)}) collective-permute-start(bf16[501,8192]{1,0:T(8,128)(2,1)} %bitcast.173), channel_id=1, source_target_pairs={{0,1},{1,0},{2,3},{3,2},{4,5},{5,4},{6,7},{7,6},{8,9},{9,8},{10,11... | collective-permute-start | bytes 24625160 | tf_op jit(solution)/shard_map/ppermute | solution.py:25
  13.7 9.8 %collective-permute-start = (bf16[1,2,8320]{2,1,0:T(2,128)(2,1)S(1)}, bf16[1,2,8320]{2,1,0:T(2,128)(2,1)S(1)}, u32[]{:S(2)}, u32[]{:S(2)}) collective-permute-start(bf16[1,2,8320]{2,1,0:T(2,128)(2,1)S(1)} %get-tuple-element.85), channel_id=1, source_target_pairs={{0,128},{1,129},{2,130},{3,131},{4,132},{5,133},{6,134},{7,135},{8... | collective-permute-start | bytes 99848 | tf_op jit(solution)/shard_map/ppermute | solution.py:25
  19.3 6.2 %collective-permute-start.3 = (bf16[48,256]{1,0:T(8,128)(2,1)S(1)}, bf16[48,256]{1,0:T(8,128)(2,1)S(1)}, u32[]{:S(2)}, u32[]{:S(2)}) collective-permute-start(bf16[48,256]{1,0:T(8,128)(2,1)S(1)} %collective-permute-done.2), channel_id=1, source_target_pairs={{0,8},{1,9},{2,10},{3,11},{4,12},{5,13},{6,14},{7,15},{8,0},{9,1},... | collective-permute-start | bytes 73736 | tf_op jit(solution)/shard_map/ppermute | solution.py:25
  31.0 6.1 %collective-permute-start.9 = (bf16[4,48,256]{2,1,0:T(8,128)(2,1)S(1)}, bf16[4,48,256]{2,1,0:T(8,128)(2,1)S(1)}, u32[]{:S(2)}, u32[]{:S(2)}) collective-permute-start(bf16[4,48,256]{2,1,0:T(8,128)(2,1)S(1)} %bitcast_dynamic-update-slice_fusion.22), channel_id=1, source_target_pairs={{0,4},{1,5},{2,6},{3,7},{4,0},{5,1},{6,2},{7,3},{8,12},{9,13},{10,... | collective-permute-start | bytes 294920 | tf_op jit(solution)/shard_map/ppermute | solution.py:25
  39.9 6.2 %collective-permute-start.12 = (bf16[16,4096]{1,0:T(8,128)(2,1)S(1)}, bf16[16,4096]{1,0:T(8,128)(2,1)S(1)}, u32[]{:S(2)}, u32[]{:S(2)}) collective-permute-start(bf16[16,4096]{1,0:T(8,128)(2,1)S(1)} %slice.389), channel_id=1, source_target_pairs={{0,6},{1,7},{2,4},{3,5},{4,2},{5,3},{6,0},{7,1},{8,14},{9,15},{10,... | collective-permute-start | bytes 393224 | tf_op jit(solution)/shard_map/ppermute | solution.py:25
  41.1 6.5 %collective-permute-start.13 = (bf16[16,4096]{1,0:T(8,128)(2,1)S(1)}, bf16[16,4096]{1,0:T(8,128)(2,1)S(1)}, u32[]{:S(2)}, u32[]{:S(2)}) collective-permute-start(bf16[16,4096]{1,0:T(8,128)(2,1)S(1)} %slice.389), channel_id=1, source_target_pairs={{0,4},{1,5},{2,6},{3,7},{4,0},{5,1},{6,2},{7,3},{8,12},{9,13},{10,... | collective-permute-start | bytes 393224 | tf_op jit(solution)/shard_map/ppermute | solution.py:25
  48.3 6.2 %collective-permute-start.16 = (bf16[16,4224]{1,0:T(8,128)(2,1)S(1)}, bf16[16,4224]{1,0:T(8,128)(2,1)S(1)}, u32[]{:S(2)}, u32[]{:S(2)}) collective-permute-start(bf16[16,4224]{1,0:T(8,128)(2,1)S(1)} %slice.390), channel_id=1, source_target_pairs={{0,24},{1,25},{2,26},{3,27},{4,28},{5,29},{6,30},{7,31},{8,16},{9,... | collective-permute-start | bytes 405512 | tf_op jit(solution)/shard_map/ppermute | solution.py:25
  49.4 6.6 %collective-permute-start.17 = (bf16[16,4224]{1,0:T(8,128)(2,1)S(1)}, bf16[16,4224]{1,0:T(8,128)(2,1)S(1)}, u32[]{:S(2)}, u32[]{:S(2)}) collective-permute-start(bf16[16,4224]{1,0:T(8,128)(2,1)S(1)} %slice.390), channel_id=1, source_target_pairs={{0,16},{1,17},{2,18},{3,19},{4,20},{5,21},{6,22},{7,23},{8,24},{9,... | collective-permute-start | bytes 405512 | tf_op jit(solution)/shard_map/ppermute | solution.py:25
  56.0 16.4 %collective-permute-start.20 = (bf16[4,16,4224]{2,1,0:T(8,128)(2,1)S(1)}, bf16[4,16,4224]{2,1,0:T(8,128)(2,1)S(1)}, u32[]{:S(2)}, u32[]{:S(2)}) collective-permute-start(bf16[4,16,4224]{2,1,0:T(8,128)(2,1)S(1)} %bitcast_dynamic-update-slice_fusion.10), channel_id=1, source_target_pairs={{0,2},{1,3},{2,4},{3,5},{4,6},{5,7},{6,0},{7,1},{8,10},{9,11},{10,... | collective-permute-start | bytes 1622024 | tf_op jit(solution)/shard_map/ppermute | solution.py:34
  56.7 15.7 %collective-permute-start.21 = (bf16[4,16,4224]{2,1,0:T(8,128)(2,1)S(1)}, bf16[4,16,4224]{2,1,0:T(8,128)(2,1)S(1)}, u32[]{:S(2)}, u32[]{:S(2)}) collective-permute-start(bf16[4,16,4224]{2,1,0:T(8,128)(2,1)S(1)} %bitcast_dynamic-update-slice_fusion.10), channel_id=1, source_target_pairs={{0,6},{1,7},{2,0},{3,1},{4,2},{5,3},{6,4},{7,5},{8,14},{9,15},{10,... | collective-permute-start | bytes 1622024 | tf_op jit(solution)/shard_map/ppermute | solution.py:34
  59.3 13.1 %collective-permute-start.18 = (bf16[4,16,4096]{2,1,0:T(8,128)(2,1)S(1)}, bf16[4,16,4096]{2,1,0:T(8,128)(2,1)S(1)}, u32[]{:S(2)}, u32[]{:S(2)}) collective-permute-start(bf16[4,16,4096]{2,1,0:T(8,128)(2,1)S(1)} %bitcast_dynamic-update-slice_fusion.14), channel_id=1, source_target_pairs={{0,8},{1,9},{2,10},{3,11},{4,12},{5,13},{6,14},{7,15},{8,16},{9,17... | collective-permute-start | bytes 1572872 | tf_op jit(solution)/shard_map/ppermute | solution.py:34
  61.4 11.0 %collective-permute-start.19 = (bf16[4,16,4096]{2,1,0:T(8,128)(2,1)S(1)}, bf16[4,16,4096]{2,1,0:T(8,128)(2,1)S(1)}, u32[]{:S(2)}, u32[]{:S(2)}) collective-permute-start(bf16[4,16,4096]{2,1,0:T(8,128)(2,1)S(1)} %bitcast_dynamic-update-slice_fusion.14), channel_id=1, source_target_pairs={{0,24},{1,25},{2,26},{3,27},{4,28},{5,29},{6,30},{7,31},{8,0},{9,1... | collective-permute-start | bytes 1572872 | tf_op jit(solution)/shard_map/ppermute | solution.py:34
  72.4 9.6 %collective-permute-start.28 = (bf16[144,256]{1,0:T(8,128)(2,1)S(1)}, bf16[144,256]{1,0:T(8,128)(2,1)S(1)}, u32[]{:S(2)}, u32[]{:S(2)}) collective-permute-start(bf16[144,256]{1,0:T(8,128)(2,1)S(1)} %pad_maximum_fusion.7), channel_id=1, source_target_pairs={{0,128},{1,129},{2,130},{3,131},{4,132},{5,133},{6,134},{7,135},{8... | collective-permute-start | bytes 221192 | tf_op jit(solution)/shard_map/ppermute | solution.py:25
  76.6 11.9 %collective-permute-start.27 = (bf16[4,16,2176]{2,1,0:T(8,128)(2,1)S(1)}, bf16[4,16,2176]{2,1,0:T(8,128)(2,1)S(1)}, u32[]{:S(2)}, u32[]{:S(2)}) collective-permute-start(bf16[4,16,2176]{2,1,0:T(8,128)(2,1)S(1)} %slice.402), channel_id=1, source_target_pairs={{0,6},{1,7},{2,0},{3,1},{4,2},{5,3},{6,4},{7,5},{8,14},{9,15},{10,... | collective-permute-start | bytes 835592 | tf_op jit(solution)/shard_map/ppermute | solution.py:34
  77.2 7.2 %collective-permute-start.24 = (bf16[4,16,2048]{2,1,0:T(8,128)(2,1)S(1)}, bf16[4,16,2048]{2,1,0:T(8,128)(2,1)S(1)}, u32[]{:S(2)}, u32[]{:S(2)}) collective-permute-start(bf16[4,16,2048]{2,1,0:T(8,128)(2,1)S(1)} %slice.399), channel_id=1, source_target_pairs={{0,8},{1,9},{2,10},{3,11},{4,12},{5,13},{6,14},{7,15},{8,16},{9,17... | collective-permute-start | bytes 786440 | tf_op jit(solution)/shard_map/ppermute | solution.py:34
  80.5 7.7 %collective-permute-start.25 = (bf16[4,16,2048]{2,1,0:T(8,128)(2,1)S(1)}, bf16[4,16,2048]{2,1,0:T(8,128)(2,1)S(1)}, u32[]{:S(2)}, u32[]{:S(2)}) collective-permute-start(bf16[4,16,2048]{2,1,0:T(8,128)(2,1)S(1)} %slice.400), channel_id=1, source_target_pairs={{0,24},{1,25},{2,26},{3,27},{4,28},{5,29},{6,30},{7,31},{8,0},{9,1... | collective-permute-start | bytes 786440 | tf_op jit(solution)/shard_map/ppermute | solution.py:34
  80.6 7.9 %collective-permute-start.26 = (bf16[4,16,2048]{2,1,0:T(8,128)(2,1)S(1)}, bf16[4,16,2048]{2,1,0:T(8,128)(2,1)S(1)}, u32[]{:S(2)}, u32[]{:S(2)}) collective-permute-start(bf16[4,16,2048]{2,1,0:T(8,128)(2,1)S(1)} %slice.401), channel_id=1, source_target_pairs={{0,2},{1,3},{2,4},{3,5},{4,6},{5,7},{6,0},{7,1},{8,10},{9,11},{10,... | collective-permute-start | bytes 786440 | tf_op jit(solution)/shard_map/ppermute | solution.py:34
  97.1 8.5 %collective-permute-start.29 = (bf16[112,256]{1,0:T(8,128)(2,1)S(1)}, bf16[112,256]{1,0:T(8,128)(2,1)S(1)}, u32[]{:S(2)}, u32[]{:S(2)}) collective-permute-start(bf16[112,256]{1,0:T(8,128)(2,1)S(1)} %pad_maximum_fusion.8), channel_id=1, source_target_pairs={{0,32},{1,33},{2,34},{3,35},{4,36},{5,37},{6,38},{7,39},{8,40},{9,... | collective-permute-start | bytes 172040 | tf_op jit(solution)/shard_map/ppermute | solution.py:25
  109.4 8.6 %collective-permute-start.34 = (bf16[224,256]{1,0:T(8,128)(2,1)S(1)}, bf16[224,256]{1,0:T(8,128)(2,1)S(1)}, u32[]{:S(2)}, u32[]{:S(2)}) collective-permute-start(bf16[224,256]{1,0:T(8,128)(2,1)S(1)} %get-tuple-element.96), channel_id=1, source_target_pairs={{0,6},{1,7},{2,4},{3,5},{4,2},{5,3},{6,0},{7,1},{8,14},{9,15},{10,... | collective-permute-start | bytes 344072 | tf_op jit(solution)/shard_map/ppermute | solution.py:25
  109.7 6.4 %collective-permute-start.35 = (bf16[224,256]{1,0:T(8,128)(2,1)S(1)}, bf16[224,256]{1,0:T(8,128)(2,1)S(1)}, u32[]{:S(2)}, u32[]{:S(2)}) collective-permute-start(bf16[224,256]{1,0:T(8,128)(2,1)S(1)} %get-tuple-element.97), channel_id=1, source_target_pairs={{0,4},{1,5},{2,6},{3,7},{4,0},{5,1},{6,2},{7,3},{8,12},{9,13},{10,... | collective-permute-start | bytes 344072 | tf_op jit(solution)/shard_map/ppermute | solution.py:25
  119.4 7.9 %collective-permute-start.36 = (bf16[80,256]{1,0:T(8,128)(2,1)S(1)}, bf16[80,256]{1,0:T(8,128)(2,1)S(1)}, u32[]{:S(2)}, u32[]{:S(2)}) collective-permute-start(bf16[80,256]{1,0:T(8,128)(2,1)S(1)} %get-tuple-element.92), channel_id=1, source_target_pairs={{0,8},{1,9},{2,10},{3,11},{4,12},{5,13},{6,14},{7,15},{8,0},{9,1},... | collective-permute-start | bytes 122888 | tf_op jit(solution)/shard_map/ppermute | solution.py:25
  127.4 8.7 %collective-permute-start.39 = (f32[10,256]{1,0:T(8,128)S(1)}, f32[10,256]{1,0:T(8,128)S(1)}, u32[]{:S(2)}, u32[]{:S(2)}) collective-permute-start(f32[10,256]{1,0:T(8,128)S(1)} %pad_maximum_fusion.13.mine_ref), channel_id=1, source_target_pairs={{0,128},{1,129},{2,130},{3,131},{4,132},{5,133},{6,134},{7,135},{8... | collective-permute-start | bytes 30728 | tf_op jit(solution)/shard_map/ppermute | solution.py:25
  130.1 13.2 %collective-permute-start.40 = (bf16[48,256]{1,0:T(8,128)(2,1)S(1)}, bf16[48,256]{1,0:T(8,128)(2,1)S(1)}, u32[]{:S(2)}, u32[]{:S(2)}) collective-permute-start(bf16[48,256]{1,0:T(8,128)(2,1)S(1)} %fusion.8), channel_id=1, source_target_pairs={{0,0},{1,1},{2,2},{3,3},{4,32},{5,33},{6,34},{7,35},{8,64},{9,65},... | collective-permute-start | bytes 73736 | tf_op jit(solution)/shard_map/ppermute | solution.py:358
  (22 other events, 250.0 us)
